TPU v7x, 32 devices: a whole 2x2x4 slice. The times are simulated.
32 devices in a mesh: heads: 4 (over z), shard: 8 (over y, x, core).
Axes of the slice: x: 2, y: 2, z: 4, core: 2. Of those that a mesh axis runs over, the one named last changes fastest.
Arguments:
- tokens: bfloat16 [16, 1024, 1024], P('shard', 'heads'), may hold values from -6 to 6
- cotangent: bfloat16 [16, 1024, 1024], P('shard', 'heads'), may hold values from -6 to 6
- lengths: int32 [16], P('shard'), may hold values from 256 to 1024, as said below
- routes: int32 [16, 1024, 8], P('shard', 'heads'), may hold values from 0 to 31, all different within a row
- attention_input_weight: bfloat16 [1024, 2048], P(('heads', 'shard')), may hold values from -0.1875 to 0.1875
- attn_out: bfloat16 [1024, 1024], P(('heads', 'shard')), may hold values from -1.5 to 1.5
- router: bfloat16 [1024, 32], P(('heads', 'shard')), may hold values from -0.09375 to 0.09375
- gain_attn: bfloat16 [1024], P(('heads', 'shard')), may hold values from 0.5 to 1.5
- gain_ffn: bfloat16 [1024], P(('heads', 'shard')), may hold values from 0.5 to 1.5
- expert_in: bfloat16 [32768, 1024], P(('heads', 'shard')), may hold values from -0.1875 to 0.1875
- expert_out: bfloat16 [32768, 512], P(('heads', 'shard')), may hold values from -1 to 1
Outputs:
- mixed: bfloat16 [16, 1024, 1024], P('shard', 'heads')
- grad_tokens: bfloat16 [16, 1024, 1024], P('shard', 'heads')
- grad_attn_in: float32 [1024, 2048], P(('heads', 'shard'))
- grad_attn_out: float32 [1024, 1024], P(('heads', 'shard'))
- grad_router: float32 [1024, 32], P(('heads', 'shard'))
- grad_gain_attn: float32 [1024], P(('heads', 'shard'))
- grad_gain_ffn: float32 [1024], P(('heads', 'shard'))
- grad_expert_in: float32 [32768, 1024], P(('heads', 'shard'))
- grad_expert_out: float32 [32768, 512], P(('heads', 'shard'))
Inputs may be any that keep to these rules, and one draw needn't show every extreme that they name: `lengths`: of each 2 consecutive slots, one has length 1024. `routes`: A token's 8 experts differ; every expert is named by some token.
All inputs are finite; a program needn't handle non-finite values.
Results may differ from a plain program's by a relative error of at most 0.017.
Values may be sent and summed in bfloat16 or wider, within the bound.
No kernel may reach another device: no remote copies, remote signals or barrier semaphores. Data moves between devices by JAX's collectives and lax.ppermute only.
A program may use at most 512 MiB of HBM per device.

v0:
```python
import math

import jax
import jax.numpy as jnp
from jax import lax
from jax.sharding import PartitionSpec as P

D = 1024
QUERY_HEADS = 16
KEY_VALUE_HEADS = 8
HEAD_SIZE = 64
E = 32
FFE = 512
TOPK = 8
QUERIES_PER_KV = 2
CAP = 160


EPSILON = 1e-06
THETA_BASE = 10000.0
NEGATIVE = -1e30
TOP_PRECISION = lax.Precision.HIGHEST


def norm_rows(value, gain):
    factor = lax.rsqrt(jnp.mean(value * value, -1, keepdims=True) + EPSILON)
    return (value * factor * gain, factor)


def norm_back(grad_in, value, factor, gain):
    normalized_rows = value * factor
    scaled = grad_in * gain
    gain_term = jnp.sum(grad_in * normalized_rows, 0)
    grad_value = factor * (
        scaled - normalized_rows * jnp.mean(scaled * normalized_rows, -1, keepdims=True)
    )
    return (grad_value, gain_term)


def rotary_tables(positions):
    half_size = HEAD_SIZE // 2
    freqs = THETA_BASE ** (-2.0 * jnp.arange(half_size, dtype=jnp.float32) / HEAD_SIZE)
    angles = positions.astype(jnp.float32)[:, None] * freqs[None, :]
    return (jnp.cos(angles), jnp.sin(angles))


def turn(values, cosine, sine, sign):
    half_size = values.shape[-1] // 2
    first_half = values[..., :half_size]
    second_half = values[..., half_size:]
    return jnp.concatenate(
        [
            first_half * cosine - sign * second_half * sine,
            second_half * cosine + sign * first_half * sine,
        ],
        -1,
    )


def split_heads(packed_tokens):
    items, length, local_groups = packed_tokens.shape[:3]
    pieces = packed_tokens.reshape(items, length, local_groups, QUERIES_PER_KV + 2, HEAD_SIZE)
    return (
        pieces[:, :, :, :QUERIES_PER_KV],
        pieces[:, :, :, QUERIES_PER_KV],
        pieces[:, :, :, QUERIES_PER_KV + 1],
    )


def block_scores(query_block, keys, first_row, block_rows, length):
    scale = 1.0 / math.sqrt(HEAD_SIZE)
    scores = (
        jnp.einsum("nqhgd,nkhd->nhgqk", query_block, keys, preferred_element_type=jnp.float32)
        * scale
    )
    allowed = jnp.arange(length)[None, :] <= (first_row + jnp.arange(block_rows))[:, None]
    return jnp.where(allowed, scores, NEGATIVE)


def attend_forward(packed_tokens):
    queries, keys, values = split_heads(packed_tokens)
    items, length, local_groups = packed_tokens.shape[:3]
    block_rows = math.gcd(512, length)

    def one_block(first_row):
        query_block = lax.dynamic_slice_in_dim(queries, first_row, block_rows, 1)
        scores = block_scores(query_block, keys, first_row, block_rows, length)
        highest_score = jnp.max(scores, -1, keepdims=True)
        weights_exp = jnp.exp(scores - highest_score)
        total_exp = jnp.sum(weights_exp, -1, keepdims=True)
        probs = (weights_exp / total_exp).astype(jnp.bfloat16)
        result = jnp.einsum("nhgqk,nkhd->nqhgd", probs, values, preferred_element_type=jnp.float32)
        return (result.astype(jnp.bfloat16), (highest_score + jnp.log(total_exp))[..., 0])

    firsts = jnp.arange(length // block_rows) * block_rows
    results, log_totals = lax.map(one_block, firsts)
    context = jnp.moveaxis(results, 0, 1).reshape(
        items, length, local_groups, QUERIES_PER_KV * HEAD_SIZE
    )
    log_total = jnp.moveaxis(log_totals, 0, 3).reshape(items, local_groups, QUERIES_PER_KV, length)
    return (context, log_total, packed_tokens)


def attend_backward(packed_tokens, log_total, context_gradient):
    queries, keys, values = split_heads(packed_tokens)
    items, length, local_groups = packed_tokens.shape[:3]
    block_rows = math.gcd(512, length)
    scale = 1.0 / math.sqrt(HEAD_SIZE)
    grad_heads = context_gradient.reshape(items, length, local_groups, QUERIES_PER_KV, HEAD_SIZE)

    def one_block(totals, first_row):
        grad_keys, grad_values = totals
        query_block = lax.dynamic_slice_in_dim(queries, first_row, block_rows, 1)
        grad_block = lax.dynamic_slice_in_dim(grad_heads, first_row, block_rows, 1)
        total_block = lax.dynamic_slice_in_dim(log_total, first_row, block_rows, 3)
        scores = block_scores(query_block, keys, first_row, block_rows, length)
        probs = jnp.exp(scores - total_block[..., None])
        probs_low = probs.astype(jnp.bfloat16)
        grad_values = grad_values + jnp.einsum(
            "nhgqk,nqhgd->nkhd", probs_low, grad_block, preferred_element_type=jnp.float32
        )
        grad_probs = jnp.einsum(
            "nqhgd,nkhd->nhgqk", grad_block, values, preferred_element_type=jnp.float32
        )
        grad_scores = (
            probs * (grad_probs - jnp.sum(probs * grad_probs, -1, keepdims=True))
        ).astype(jnp.bfloat16)
        grad_query = (
            jnp.einsum("nhgqk,nkhd->nqhgd", grad_scores, keys, preferred_element_type=jnp.float32)
            * scale
        )
        grad_keys = (
            grad_keys
            + jnp.einsum(
                "nhgqk,nqhgd->nkhd", grad_scores, query_block, preferred_element_type=jnp.float32
            )
            * scale
        )
        return ((grad_keys, grad_values), grad_query.astype(jnp.bfloat16))

    firsts = jnp.arange(length // block_rows) * block_rows
    zeros_kv = jnp.zeros((items, length, local_groups, HEAD_SIZE), jnp.float32)
    (grad_keys, grad_values), grad_queries = lax.scan(one_block, (zeros_kv, zeros_kv), firsts)
    grad_queries = jnp.moveaxis(grad_queries, 0, 1).reshape(
        items, length, local_groups, QUERIES_PER_KV, HEAD_SIZE
    )
    joined = jnp.concatenate(
        [
            grad_queries,
            grad_keys.astype(jnp.bfloat16)[:, :, :, None],
            grad_values.astype(jnp.bfloat16)[:, :, :, None],
        ],
        3,
    )
    return joined.reshape(items, length, local_groups, (QUERIES_PER_KV + 2) * HEAD_SIZE)


def fold_rows(source, shard_rows, totals, weights_piece):
    piece_rows = weights_piece.shape[0]
    step_rows = math.gcd(piece_rows, shard_rows)
    out_width = totals.shape[2]

    def fold_one_step(step_index, accum):
        row_start = step_index * step_rows
        expert_index = row_start // D
        offset = row_start % D
        left_rows = lax.dynamic_slice(source, (0, expert_index, offset), (CAP, 1, step_rows))[:, 0]
        weights_rows = lax.dynamic_slice_in_dim(weights_piece, step_index * step_rows, step_rows, 0)
        term = jnp.dot(left_rows, weights_rows, preferred_element_type=jnp.float32)
        current = lax.dynamic_slice(accum, (0, expert_index, 0), (CAP, 1, out_width))
        return lax.dynamic_update_slice(accum, current + term[:, None], (0, expert_index, 0))

    return lax.fori_loop(0, piece_rows // step_rows, fold_one_step, totals)


def map_rows(source, shard_rows, weights_piece):
    piece_rows = weights_piece.shape[0]
    step_rows = math.gcd(piece_rows, shard_rows)

    def map_one_step(step_index):
        row_start = step_index * step_rows
        expert_index = row_start // D
        left_rows = lax.dynamic_slice_in_dim(source, expert_index, 1, 1)[:, 0]
        weights_rows = lax.dynamic_slice_in_dim(weights_piece, step_index * step_rows, step_rows, 0)
        return lax.dot_general(
            left_rows, weights_rows, (((1,), (1,)), ((), ())), preferred_element_type=jnp.float32
        )

    results = lax.map(map_one_step, jnp.arange(piece_rows // step_rows, dtype=jnp.int32))
    return jnp.moveaxis(results, 0, 1).reshape(CAP, piece_rows)


def grad_rows(left_source, right_source, shard_rows, piece_rows):
    row_count = left_source.shape[0]
    step_rows = math.gcd(piece_rows, shard_rows)

    def grad_one_step(step_index):
        row_start = step_index * step_rows
        expert_index = row_start // D
        offset = row_start % D
        left_rows = lax.dynamic_slice(
            left_source, (0, expert_index, offset), (row_count, 1, step_rows)
        )[:, 0]
        right_rows = lax.dynamic_slice_in_dim(right_source, expert_index, 1, 1)[:, 0]
        return lax.dot_general(
            left_rows, right_rows, (((0,), (0,)), ((), ())), preferred_element_type=jnp.float32
        )

    results = lax.map(grad_one_step, jnp.arange(piece_rows // step_rows, dtype=jnp.int32))
    return results.reshape(piece_rows, right_source.shape[2])


def swiglu(pre_ffn):
    gate_pre = pre_ffn[..., :FFE]
    up_pre = pre_ffn[..., FFE:]
    sigmoid_gate = jax.nn.sigmoid(gate_pre)
    silu_gate = gate_pre * sigmoid_gate
    return ((silu_gate * up_pre).astype(jnp.bfloat16), (gate_pre, up_pre, sigmoid_gate, silu_gate))


def swiglu_back(grad_hidden, pieces_kept):
    gate_pre, up_pre, sigmoid_gate, silu_gate = pieces_kept
    grad_gate = grad_hidden * up_pre * sigmoid_gate * (1.0 + gate_pre * (1.0 - sigmoid_gate))
    grad_up = grad_hidden * silu_gate
    return jnp.concatenate([grad_gate, grad_up], -1).astype(jnp.bfloat16)


def local(
    tokens,
    cotangent,
    lengths,
    routes,
    attention_input_weight,
    attn_out,
    router,
    gain_attn,
    gain_ffn,
    expert_in,
    expert_out,
):
    device_slots, device_span, model_width = tokens.shape
    token_rows = device_slots * device_span
    shard_rows = expert_in.shape[0]
    w_qkv, w_proj, w_router, gain_one, gain_two = (
        lax.all_gather(attention_input_weight, ("heads", "shard"), axis=0, tiled=True),
        lax.all_gather(attn_out, ("heads", "shard"), axis=0, tiled=True),
        lax.all_gather(router, ("heads", "shard"), axis=0, tiled=True),
        lax.all_gather(gain_attn, ("heads", "shard"), axis=0, tiled=True),
        lax.all_gather(gain_ffn, ("heads", "shard"), axis=0, tiled=True),
    )
    gain_one = gain_one.astype(jnp.float32)
    gain_two = gain_two.astype(jnp.float32)
    positions = lax.axis_index("heads") * device_span + jnp.arange(device_span, dtype=jnp.int32)
    valid = (positions[None, :] < lengths[:, None]).reshape(token_rows)
    valid_float = valid.astype(jnp.float32)[:, None]
    state = tokens.astype(jnp.float32).reshape(token_rows, model_width)
    normed_one, factor_one = norm_rows(state, gain_one)
    normed_attn = normed_one.astype(jnp.bfloat16)
    before_projection = jnp.dot(normed_attn, w_qkv, preferred_element_type=jnp.float32)
    before_projection = before_projection.reshape(
        device_slots, device_span, KEY_VALUE_HEADS, QUERIES_PER_KV + 2, HEAD_SIZE
    )
    cosine, sine = rotary_tables(positions)
    cosine = cosine[None, :, None, None, :]
    sine = sine[None, :, None, None, :]
    turned = turn(before_projection[:, :, :, : QUERIES_PER_KV + 1], cosine, sine, 1.0)
    packed_tokens = jnp.concatenate(
        [turned, before_projection[:, :, :, QUERIES_PER_KV + 1 :]], 3
    ).astype(jnp.bfloat16)
    packed_tokens = packed_tokens.reshape(
        device_slots, device_span, KEY_VALUE_HEADS, (QUERIES_PER_KV + 2) * HEAD_SIZE
    )
    context_heads, log_total, received = attend_forward(
        lax.all_to_all(packed_tokens, "heads", split_axis=2, concat_axis=1, tiled=True)
    )
    context = lax.all_to_all(
        context_heads, "heads", split_axis=1, concat_axis=2, tiled=True
    ).reshape(token_rows, QUERY_HEADS * HEAD_SIZE)
    mid_state = state + jnp.dot(context, w_proj, preferred_element_type=jnp.float32)
    normed_two, factor_two = norm_rows(mid_state, gain_two)
    normed_ffn = normed_two.astype(jnp.bfloat16)
    logits = jnp.dot(normed_ffn, w_router, preferred_element_type=jnp.float32)
    route_rows = routes.reshape(token_rows, TOPK)
    route_hits = route_rows[:, :, None] == jnp.arange(E, dtype=jnp.int32)[None, None, :]
    chosen = jnp.sum(jnp.where(route_hits, logits[:, None, :], 0.0), -1)
    highest_logit = jnp.max(chosen, -1, keepdims=True)
    weights_exp = jnp.exp(chosen - highest_logit)
    gates = weights_exp / jnp.sum(weights_exp, -1, keepdims=True)
    flat_routes = route_rows.reshape(token_rows * TOPK)
    live_pairs = jnp.repeat(valid, TOPK)
    one_hot = (
        (flat_routes[:, None] == jnp.arange(E, dtype=jnp.int32)[None, :]) & live_pairs[:, None]
    ).astype(jnp.int32)
    slot_index = jnp.sum((jnp.cumsum(one_hot, 0) - one_hot) * one_hot, 1)
    kept_pairs = live_pairs & (slot_index < CAP)
    target = jnp.where(kept_pairs, slot_index * E + flat_routes, CAP * E)
    spread = jnp.repeat(normed_ffn, TOPK, 0)
    buffer = jnp.zeros((CAP * E, model_width), jnp.bfloat16).at[target].set(spread, mode="drop")
    buffer = buffer.reshape(CAP, E, model_width)
    grad_out = cotangent.astype(jnp.float32).reshape(token_rows, model_width) * valid_float
    grad_pick = (gates[..., None] * grad_out[:, None, :]).reshape(token_rows * TOPK, model_width)
    grad_outputs = (
        jnp.zeros((CAP * E, model_width), jnp.float32).at[target].set(grad_pick, mode="drop")
    )
    grad_outputs = grad_outputs.astype(jnp.bfloat16).reshape(CAP, E, model_width)
    pre_ffn = fold_rows(
        buffer,
        shard_rows,
        jnp.zeros((CAP, E, 2 * FFE), jnp.float32),
        lax.all_gather(expert_in, ("heads", "shard"), axis=0, tiled=True),
    )
    hidden, pieces_kept = swiglu(pre_ffn)
    outputs = map_rows(
        hidden, shard_rows, lax.all_gather(expert_out, ("heads", "shard"), axis=0, tiled=True)
    ).reshape(CAP, E, D)
    grad_hidden = fold_rows(
        grad_outputs,
        shard_rows,
        jnp.zeros((CAP, E, FFE), jnp.float32),
        lax.all_gather(expert_out, ("heads", "shard"), axis=0, tiled=True),
    )
    grad_pre_ffn = swiglu_back(grad_hidden, pieces_kept)
    grad_buffer = map_rows(
        grad_pre_ffn, shard_rows, lax.all_gather(expert_in, ("heads", "shard"), axis=0, tiled=True)
    ).reshape(CAP, E, D)
    grad_expert_in = lax.psum_scatter(
        grad_rows(buffer, grad_pre_ffn, shard_rows, shard_rows * lax.axis_size(("heads", "shard"))),
        ("heads", "shard"),
        scatter_dimension=0,
        tiled=True,
    )
    grad_expert_out = lax.psum_scatter(
        grad_rows(grad_outputs, hidden, shard_rows, shard_rows * lax.axis_size(("heads", "shard"))),
        ("heads", "shard"),
        scatter_dimension=0,
        tiled=True,
    )
    table = jnp.concatenate([outputs.reshape(CAP * E, D), jnp.zeros((1, D), jnp.float32)], 0)
    picked = table[target].reshape(token_rows, TOPK, D)
    mixture = jnp.sum(picked * gates[..., None], 1)
    mixed = (valid_float * (mid_state + mixture)).astype(jnp.bfloat16).reshape(tokens.shape)
    grad_gates = jnp.sum(picked * grad_out[:, None, :], -1)
    grad_chosen = gates * (grad_gates - jnp.sum(gates * grad_gates, -1, keepdims=True))
    grad_logits = jnp.sum(jnp.where(route_hits, grad_chosen[..., None], 0.0), 1)
    grad_table = jnp.concatenate(
        [grad_buffer.reshape(CAP * E, D), jnp.zeros((1, D), jnp.float32)], 0
    )
    grad_normed_ffn = jnp.sum(grad_table[target].reshape(token_rows, TOPK, D), 1)
    grad_normed_ffn = grad_normed_ffn + jnp.dot(
        grad_logits, w_router.astype(jnp.float32).T, precision=TOP_PRECISION
    )
    router_term = jnp.dot(normed_ffn.astype(jnp.float32).T, grad_logits, precision=TOP_PRECISION)
    grad_mid_norm, gain_two_term = norm_back(grad_normed_ffn, mid_state, factor_two, gain_two)
    grad_mid = grad_out + grad_mid_norm
    grad_mid_low = grad_mid.astype(jnp.bfloat16)
    proj_term = lax.dot_general(
        context, grad_mid_low, (((0,), (0,)), ((), ())), preferred_element_type=jnp.float32
    )
    context_gradient = jnp.dot(grad_mid_low, w_proj.T, preferred_element_type=jnp.float32).astype(
        jnp.bfloat16
    )
    context_gradient = context_gradient.reshape(
        device_slots, device_span, KEY_VALUE_HEADS, QUERIES_PER_KV * HEAD_SIZE
    )
    grad_context_heads = lax.all_to_all(
        context_gradient, "heads", split_axis=2, concat_axis=1, tiled=True
    )
    grad_packed_heads = attend_backward(received, log_total, grad_context_heads)
    grad_packed = lax.all_to_all(
        grad_packed_heads, "heads", split_axis=1, concat_axis=2, tiled=True
    )
    grad_pieces = grad_packed.astype(jnp.float32).reshape(
        device_slots, device_span, KEY_VALUE_HEADS, QUERIES_PER_KV + 2, HEAD_SIZE
    )
    grad_turned = turn(grad_pieces[:, :, :, : QUERIES_PER_KV + 1], cosine, sine, -1.0)
    gradient_before_norm = jnp.concatenate(
        [grad_turned, grad_pieces[:, :, :, QUERIES_PER_KV + 1 :]], 3
    ).astype(jnp.bfloat16)
    gradient_before_norm = gradient_before_norm.reshape(
        token_rows, (QUERY_HEADS + 2 * KEY_VALUE_HEADS) * HEAD_SIZE
    )
    qkv_term = lax.dot_general(
        normed_attn,
        gradient_before_norm,
        (((0,), (0,)), ((), ())),
        preferred_element_type=jnp.float32,
    )
    grad_normed_attn = jnp.dot(gradient_before_norm, w_qkv.T, preferred_element_type=jnp.float32)
    grad_state_norm, gain_one_term = norm_back(grad_normed_attn, state, factor_one, gain_one)
    grad_tokens = (grad_mid + grad_state_norm).astype(jnp.bfloat16).reshape(tokens.shape)
    grad_attn_in, grad_attn_out, grad_router, grad_gain_attn, grad_gain_ffn = (
        lax.psum_scatter(qkv_term, ("heads", "shard"), scatter_dimension=0, tiled=True),
        lax.psum_scatter(proj_term, ("heads", "shard"), scatter_dimension=0, tiled=True),
        lax.psum_scatter(router_term, ("heads", "shard"), scatter_dimension=0, tiled=True),
        lax.psum_scatter(gain_one_term, ("heads", "shard"), scatter_dimension=0, tiled=True),
        lax.psum_scatter(gain_two_term, ("heads", "shard"), scatter_dimension=0, tiled=True),
    )
    return (
        mixed,
        grad_tokens,
        grad_attn_in,
        grad_attn_out,
        grad_router,
        grad_gain_attn,
        grad_gain_ffn,
        grad_expert_in,
        grad_expert_out,
    )


def solution(mesh):
    in_specs = (
        P("shard", "heads", None),
        P("shard", "heads", None),
        P("shard"),
        P("shard", "heads", None),
        P(("heads", "shard"), None),
        P(("heads", "shard"), None),
        P(("heads", "shard"), None),
        P(("heads", "shard")),
        P(("heads", "shard")),
        P(("heads", "shard"), None),
        P(("heads", "shard"), None),
    )
    out_specs = (
        P("shard", "heads", None),
        P("shard", "heads", None),
        P(("heads", "shard"), None),
        P(("heads", "shard"), None),
        P(("heads", "shard"), None),
        P(("heads", "shard")),
        P(("heads", "shard")),
        P(("heads", "shard"), None),
        P(("heads", "shard"), None),
    )
    return jax.shard_map(local, mesh=mesh, in_specs=in_specs, out_specs=out_specs, check_vma=False)
```

profile of v0, /device:TPU:0, one launch (start us, length us, event | category | flops | bytes accessed | tf_op | source)
XLA Modules:
  0.0 3852.2 jit_solution(13364599887594401866)
XLA Ops:
  11.7 42.2 %all-reduce.8 = (bf16[1024]{0:T(1024)(128)(2,1)S(1)}, bf16[1024]{0:T(1024)(128)(2,1)}) all-reduce(bf16[1024]{0:T(1024)(128)(2,1)S(1)} %dynamic-update-slice, bf16[1024]{0:T(1024)(128)(2,1)S(1)} %dynamic-update-slice.1), channel_id=1, replica_groups=mesh['heads'=4,'shard'=8] {'heads','shard'}, use_global_device_ids=true, to_apply=%add.2 | all-reduce | flops 2048 | bytes 8192
  58.4 17.4 all-gather.5.cloned.1.call-done
  109.7 38.3 all-to-all-done
  158.7 36.7 while.105
  212.1 70.6 %all_gather.29 = bf16[1024,32]{1,0:T(8,128)(2,1)S(1)} all-gather(bf16[32,32]{1,0:T(8,128)(2,1)S(1)} %copy-done.53), channel_id=1, replica_groups=mesh['heads'=4,'shard'=8] {'heads','shard'}, dimensions={0}, use_global_device_ids=true | all-gather | bytes 67584 | tf_op jit(solution)/shard_map/all_gather | solution.py:247
  298.1 24.9 scatter_custom_fusion
  337.1 29.2 scatter_custom_fusion.1
  397.9 79.6 %while.108 = (s32[]{:T(128)}, f32[160,32,512]{2,0,1:T(8,128)}, bf16[160,32,1024]{2,0,1:T(8,128)(2,1)}, bf16[32768,512]{1,0:T(8,128)(2,1)}, s32[]{:T(128)}, /*ind...) while((s32[]{:T(128)}, f32[160,32,512]{2,0,1:T(8,128)}, ...), condition=%wide.region_20.21_spmd, body=%wide.region_19.20_spmd.sunk | while | flops 167854096 | bytes 2033490 | solution.py:173
  477.5 254.8 %all-gather.9.cloned.1.call-done = bf16[32768,1024]{1,0:T(8,128)(2,1)} async-done(((bf16[1024,1024]{1,0:T(8,128)(2,1)}), bf16[32768,1024]{1,0:T(8,128)(2,1)}) %all-gather.9.cloned.1.call-update) | async-done | bytes 67108880 | tf_op jit(solution)/shard_map/all_gather | solution.py:310
  742.0 101.9 %while.106 = (s32[]{:T(128)}, f32[160,32,1024]{2,0,1:T(8,128)}, bf16[160,32,1024]{2,0,1:T(8,128)(2,1)}, bf16[32768,1024]{1,0:T(8,128)(2,1)}, s32[]{:T(128)}, /*i...) while((s32[]{:T(128)}, f32[160,32,1024]{2,0,1:T(8,128)}, ...), condition=%wide.region_11.12_spmd, body=%wide.region_10.11_spmd.sunk | while | flops 335708192 | bytes 3737426 | solution.py:173
  873.1 145.8 %while.109 = (s32[]{:T(128)}, f32[32,160,1024]{2,1,0:T(8,128)}, s32[32]{0:T(128)S(1)}, bf16[160,32,1024]{2,0,1:T(8,128)(2,1)}, bf16[32768,1024]{1,0:T(8,128)(2,1...) while((s32[]{:T(128)}, f32[32,160,1024]{2,1,0:T(8,128)}, ...), condition=%wide.region_22.23_spmd, body=%wide.region_21.22_spmd.sunk | while | flops 335544352 | bytes 3080570 | solution.py:189
  1018.9 18.5 copy.144
  1044.8 29.4 gather_fusion.1
  1093.3 126.1 %while.107 = (s32[]{:T(128)}, f32[32,160,1024]{2,1,0:T(8,128)}, s32[32]{0:T(128)S(1)}, bf16[160,32,512]{2,0,1:T(8,128)(2,1)}, bf16[32768,512]{1,0:T(8,128)(2,1)}...) while((s32[]{:T(128)}, f32[32,160,1024]{2,1,0:T(8,128)}, ...), condition=%wide.region_13.14_spmd, body=%wide.region_12.13_spmd.sunk | while | flops 167772176 | bytes 1868154 | solution.py:189
  1219.5 18.7 copy.140
  1245.5 29.5 gather_fusion
  1311.0 18.5 all-to-all-done.2
  1333.9 94.8 %while.112 = (s32[]{:T(128)}, f32[2,1024,2,64]{1,3,2,0:T(8,128)}, f32[2,1024,2,64]{1,3,2,0:T(8,128)}, bf16[2,2,512,2,2,64]{2,5,4,3,1,0:T(8,128)(2,1)}, s32[2]{0:...) while((s32[]{:T(128)}, f32[2,1024,2,64]{1,3,2,0:T(8,128)}, ...), condition=%wide.region_30.31_spmd.clone, body=%wide.region_28.30_spmd.clone.sunk | while | flops 2749624832 | bytes 195219888 | solution.py:143
  1437.0 58.8 %all_to_all.54 = bf16[2,1024,2,256]{3,2,0,1:T(2,128)(2,1)S(1)} all-to-all(bf16[2,1024,2,256]{3,2,0,1:T(2,128)(2,1)} %copy.151), channel_id=1, replica_groups=mesh['heads'=4,'shard'=8] {'heads'}, dimensions={1} | all-to-all | bytes 4194304 | tf_op jit(solution)/shard_map/all_to_all | solution.py:369
  1517.7 131.2 %while.111 = (s32[]{:T(128)}, f32[32,1024,512]{2,1,0:T(8,128)}, s32[32]{0:T(128)S(1)}, bf16[160,32,1024]{2,0,1:T(8,128)(2,1)}, bf16[160,32,512]{2,0,1:T(8,128)(2...) while((s32[]{:T(128)}, f32[32,1024,512]{2,1,0:T(8,128)}, ...), condition=%wide.region_43.44_spmd, body=%wide.region_42.43_spmd.sunk | while | flops 167772176 | bytes 2590541 | solution.py:209
  1649.0 162.7 %while.110 = (s32[]{:T(128)}, f32[32,1024,1024]{2,1,0:T(8,128)}, s32[32]{0:T(128)S(1)}, bf16[160,32,1024]{2,0,1:T(8,128)(2,1)}, bf16[160,32,1024]{2,0,1:T(8,128)...) while((s32[]{:T(128)}, f32[32,1024,1024]{2,1,0:T(8,128)}, ...), condition=%wide.region_40.41_spmd, body=%wide.region_39.40_spmd.sunk | while | flops 335544352 | bytes 4851533 | solution.py:209
  1820.0 42.4 %all-reduce.7 = (f32[1024]{0:T(1024)S(1)}, f32[1024]{0:T(1024)S(1)}) all-reduce(f32[1024]{0:T(1024)S(1)} %get-tuple-element.724, f32[1024]{0:T(1024)S(1)} %copy-done.52), channel_id=5, replica_groups=mesh['heads'=4,'shard'=8] {'heads','shard'}, use_global_device_ids=true, to_apply=%region_36.37.clone | all-reduce | flops 2048 | bytes 16384
  1866.7 568.8 %reduce-scatter.15.cloned.1.call-done = f32[1024,512]{1,0:T(8,128)} async-done(((f32[32768,512]{1,0:T(8,128)}), f32[1024,512]{1,0:T(8,128)}) %reduce-scatter.15.cloned.1.call-update) | async-done | bytes 2097168 | tf_op jit(solution)/shard_map/reduce_scatter | solution.py:332
  2435.5 1409.9 %reduce-scatter.17.cloned.1.call-done = f32[1024,1024]{1,0:T(8,128)} async-done(((f32[32768,1024]{1,0:T(8,128)}), f32[1024,1024]{1,0:T(8,128)}) %reduce-scatter.17.cloned.1.call-update) | async-done | bytes 4194320
  (643 shorter events, 1072.9 us)
Async XLA Ops:
  7.2 68.6 %all-gather.5.cloned.1.call-start = ((), (), s32[]{:S(2)}) async-start(), calls=%async_computation.9 | async-start | bytes 4325376 | tf_op jit(solution)/shard_map/all_gather | solution.py:245
  7.9 283.2 %all-gather.7.cloned.1.call-start = ((), (), s32[]{:S(2)}) async-start(), calls=%async_computation.10 | async-start | bytes 2162688 | tf_op jit(solution)/shard_map/all_gather | solution.py:246
  8.7 384.0 %all-gather.11.cloned.1.call-start = ((), (), s32[]{:S(2)}) async-start(), calls=%async_computation.12 | async-start | bytes 34603008 | tf_op jit(solution)/shard_map/all_gather | solution.py:314
  9.4 722.9 %all-gather.9.cloned.1.call-start = ((), (), s32[]{:S(2)}) async-start(), calls=%async_computation.11 | async-start | bytes 69206016 | tf_op jit(solution)/shard_map/all_gather | solution.py:310
  53.9 32.9 copy-start.43
  56.8 30.1 copy-start.30
  58.3 28.5 copy-start.26
  90.0 58.0 %all-to-all-start = ((bf16[2,256,8,256]{3,1,0,2:T(8,128)(2,1)}), bf16[2,256,8,256]{3,1,0,2:T(8,128)(2,1)S(1)}, u32[]{:S(2)}, u32[]{:S(2)}) async-start(bf16[2,256,8,256]{3,1,0,2:T(8,128)(2,1)} %copy.129), calls=%async_computation | async-start | bytes 4194304 | tf_op jit(solution)/shard_map/all_to_all | solution.py:274
  195.4 99.0 %copy-start.1 = (bf16[2,1024,2,64]{1,3,2,0:T(8,128)(2,1)}, bf16[2,1024,2,64]{1,3,2,0:T(8,128)(2,1)S(1)}, u32[]{:S(2)}) copy-start(bf16[2,1024,2,64]{1,3,2,0:T(8,128)(2,1)S(1)} %get-tuple-element.1434) | copy-start | bytes 1572868
  195.4 99.0 %copy-start.3 = (bf16[2,1024,2,2,64]{1,4,3,2,0:T(8,128)(2,1)}, bf16[2,1024,2,2,64]{1,4,3,2,0:T(8,128)(2,1)S(1)}, u32[]{:S(2)}) copy-start(bf16[2,1024,2,2,64]{1,4,3,2,0:T(8,128)(2,1)S(1)} %get-tuple-element.1435) | copy-start | bytes 3145732
  195.4 99.0 %copy-start.7 = (bf16[2,1024,2,64]{1,3,2,0:T(8,128)(2,1)}, bf16[2,1024,2,64]{1,3,2,0:T(8,128)(2,1)S(1)}, u32[]{:S(2)}) copy-start(bf16[2,1024,2,64]{1,3,2,0:T(8,128)(2,1)S(1)} %get-tuple-element.1438) | copy-start | bytes 1572868
  195.5 95.7 %copy-start.16 = (bf16[2,256,1024]{2,1,0:T(8,128)(2,1)S(1)}, bf16[2,256,1024]{2,1,0:T(8,128)(2,1)}, u32[]{:S(2)}) copy-start(bf16[2,256,1024]{2,1,0:T(8,128)(2,1)} %param.27) | copy-start | bytes 3145732
  207.7 77.9 %all-to-all-start.1 = ((bf16[2,1024,2,128]{3,2,0,1:T(2,128)(2,1)}), bf16[2,1024,2,128]{3,2,0,1:T(2,128)(2,1)}, u32[]{:S(2)}, u32[]{:S(2)}) async-start(bf16[2,1024,2,128]{3,2,0,1:T(2,128)(2,1)} %reshape.574), calls=%async_computation.1 | async-start | bytes 2097152 | tf_op jit(solution)/shard_map/all_to_all | solution.py:276
  212.1 70.7 %copy-start.49 = (f32[512]{0:T(512)}, f32[512]{0:T(512)S(1)}, u32[]{:S(2)}) copy-start(f32[512]{0:T(512)S(1)} %convert_element_type.121) | copy-start | bytes 6148
  212.1 83.9 %copy-start.36 = (f32[1024]{0:T(1024)}, f32[1024]{0:T(1024)S(1)}, u32[]{:S(2)}) copy-start(f32[1024]{0:T(1024)S(1)} %convert_element_type.129) | copy-start | bytes 12292
  1245.5 29.5 copy-start.23
  1298.6 31.0 all-to-all-start.2
  1302.8 563.8 %reduce-scatter.13.cloned.1.call-start = ((), (), s32[]{:S(2)}) async-start(), calls=%async_computation.15 | async-start | bytes 540672 | tf_op jit(solution)/shard_map/reduce_scatter | solution.py:394
  1306.3 27.6 copy-start.2
  1306.3 560.3 %reduce-scatter.11.cloned.1.call-start = ((), (), s32[]{:S(2)}) async-start(), calls=%async_computation.14 | async-start | bytes 4325376 | tf_op jit(solution)/shard_map/reduce_scatter | solution.py:393
  1311.0 555.7 %reduce-scatter.9.cloned.1.call-start = ((), (), s32[]{:S(2)}) async-start(), calls=%async_computation.13 | async-start | bytes 8650752 | tf_op jit(solution)/shard_map/reduce_scatter | solution.py:392
  1517.6 917.9 %reduce-scatter.15.cloned.1.call-start = ((), (), s32[]{:S(2)}) async-start(), calls=%async_computation.16 | async-start | bytes 69206016 | tf_op jit(solution)/shard_map/reduce_scatter | solution.py:332
  1648.9 2196.5 %reduce-scatter.17.cloned.1.call-start = ((), (), s32[]{:S(2)}) async-start(), calls=%async_computation.17 | async-start | bytes 138412032
  1811.8 51.8 %copy-start.9 = (f32[512,1024]{1,0:T(8,128)S(1)}, f32[512,1024]{1,0:T(8,128)}, u32[]{:S(2)}) copy-start(f32[512,1024]{1,0:T(8,128)} %copy-done.8) | copy-start | bytes 6291460
  (56 other events, 504.2 us)
Sparse Core Ops, SparseCore 0:
  10.9 64.8 all-gather.4
  78.6 77.5 all-gather.6
  159.0 216.0 all-gather.10
  377.8 354.4 all-gather.8
  1306.4 134.9 reduce-scatter.12
  1444.2 140.5 reduce-scatter.10
  1587.8 144.5 reduce-scatter.8
  1735.4 700.0 reduce-scatter.14
  2438.6 1406.8 reduce-scatter.16
where the time goes:
time: 3870 us; the launch traced here: 3850 us
  waiting for transfers between devices  2310 us (60%)
  matrix products  700 us (18%)
  local copies, waits for them, and re-layouts  359 us (9%)
  blocking collectives  214 us (6%)
  other arithmetic  148 us (4%)
  loops' own time  92.3 us (2%)
    unnamed x10, waiting for transfers between devices  1410 us
    reduce_scatter x1, waiting for transfers between devices, local(): lax.psum_scatter(grad_rows(grad_outputs, hidden, shard_rows, shard_rows *...  569 us
    all_gather x1, waiting for transfers between devices, local(): lax.all_gather(expert_in, ('heads', 'shard'), axis=0, tiled=True)  255 us
    dot_general x64, matrix products, grad_one_step(): lax.dot_general(left_rows, right_rows, (((0,), (0,)), ((), ())), preferre...  213 us
    dot_general x64, matrix products, map_one_step(): lax.dot_general(left_rows, weights_rows, (((1,), (1,)), ((), ())), prefer...  195 us
    dot_general x64, matrix products, fold_one_step(): term = jnp.dot(left_rows, weights_rows, preferred_element_type=jnp.float32)  181 us
    unnamed x2, blocking collectives  84.6 us
  transfers between devices with their start and end apart: 12, of which 6 were waited for; matrix products, arithmetic and copies ran while one was open for 17% of the time, Pallas kernels for 0%

commit v1 on v0

v1 whole, which is shorter than its diff:
```python
import math

import jax
import jax.numpy as jnp
from jax import lax
from jax.sharding import PartitionSpec as P

D = 1024
QUERY_HEADS = 16
KEY_VALUE_HEADS = 8
HEAD_SIZE = 64
E = 32
FFE = 512
TOPK = 8
QUERIES_PER_KV = 2
CAP = 160


EPSILON = 1e-06
THETA_BASE = 10000.0
NEGATIVE = -1e30
TOP_PRECISION = lax.Precision.HIGHEST


def norm_rows(value, gain):
    factor = lax.rsqrt(jnp.mean(value * value, -1, keepdims=True) + EPSILON)
    return (value * factor * gain, factor)


def norm_back(grad_in, value, factor, gain):
    normalized_rows = value * factor
    scaled = grad_in * gain
    gain_term = jnp.sum(grad_in * normalized_rows, 0)
    grad_value = factor * (
        scaled - normalized_rows * jnp.mean(scaled * normalized_rows, -1, keepdims=True)
    )
    return (grad_value, gain_term)


def rotary_tables(positions):
    half_size = HEAD_SIZE // 2
    freqs = THETA_BASE ** (-2.0 * jnp.arange(half_size, dtype=jnp.float32) / HEAD_SIZE)
    angles = positions.astype(jnp.float32)[:, None] * freqs[None, :]
    return (jnp.cos(angles), jnp.sin(angles))


def turn(values, cosine, sine, sign):
    half_size = values.shape[-1] // 2
    first_half = values[..., :half_size]
    second_half = values[..., half_size:]
    return jnp.concatenate(
        [
            first_half * cosine - sign * second_half * sine,
            second_half * cosine + sign * first_half * sine,
        ],
        -1,
    )


def split_heads(packed_tokens):
    items, length, local_groups = packed_tokens.shape[:3]
    pieces = packed_tokens.reshape(items, length, local_groups, QUERIES_PER_KV + 2, HEAD_SIZE)
    return (
        pieces[:, :, :, :QUERIES_PER_KV],
        pieces[:, :, :, QUERIES_PER_KV],
        pieces[:, :, :, QUERIES_PER_KV + 1],
    )


def block_scores(query_block, keys, first_row, block_rows, length):
    scale = 1.0 / math.sqrt(HEAD_SIZE)
    scores = (
        jnp.einsum("nqhgd,nkhd->nhgqk", query_block, keys, preferred_element_type=jnp.float32)
        * scale
    )
    allowed = jnp.arange(length)[None, :] <= (first_row + jnp.arange(block_rows))[:, None]
    return jnp.where(allowed, scores, NEGATIVE)


def attend_forward(packed_tokens):
    queries, keys, values = split_heads(packed_tokens)
    items, length, local_groups = packed_tokens.shape[:3]
    block_rows = math.gcd(512, length)

    def one_block(first_row):
        query_block = lax.dynamic_slice_in_dim(queries, first_row, block_rows, 1)
        scores = block_scores(query_block, keys, first_row, block_rows, length)
        highest_score = jnp.max(scores, -1, keepdims=True)
        weights_exp = jnp.exp(scores - highest_score)
        total_exp = jnp.sum(weights_exp, -1, keepdims=True)
        probs = (weights_exp / total_exp).astype(jnp.bfloat16)
        result = jnp.einsum("nhgqk,nkhd->nqhgd", probs, values, preferred_element_type=jnp.float32)
        return (result.astype(jnp.bfloat16), (highest_score + jnp.log(total_exp))[..., 0])

    firsts = jnp.arange(length // block_rows) * block_rows
    results, log_totals = lax.map(one_block, firsts)
    context = jnp.moveaxis(results, 0, 1).reshape(
        items, length, local_groups, QUERIES_PER_KV * HEAD_SIZE
    )
    log_total = jnp.moveaxis(log_totals, 0, 3).reshape(items, local_groups, QUERIES_PER_KV, length)
    return (context, log_total, packed_tokens)


def attend_backward(packed_tokens, log_total, context_gradient):
    queries, keys, values = split_heads(packed_tokens)
    items, length, local_groups = packed_tokens.shape[:3]
    block_rows = math.gcd(512, length)
    scale = 1.0 / math.sqrt(HEAD_SIZE)
    grad_heads = context_gradient.reshape(items, length, local_groups, QUERIES_PER_KV, HEAD_SIZE)

    def one_block(totals, first_row):
        grad_keys, grad_values = totals
        query_block = lax.dynamic_slice_in_dim(queries, first_row, block_rows, 1)
        grad_block = lax.dynamic_slice_in_dim(grad_heads, first_row, block_rows, 1)
        total_block = lax.dynamic_slice_in_dim(log_total, first_row, block_rows, 3)
        scores = block_scores(query_block, keys, first_row, block_rows, length)
        probs = jnp.exp(scores - total_block[..., None])
        probs_low = probs.astype(jnp.bfloat16)
        grad_values = grad_values + jnp.einsum(
            "nhgqk,nqhgd->nkhd", probs_low, grad_block, preferred_element_type=jnp.float32
        )
        grad_probs = jnp.einsum(
            "nqhgd,nkhd->nhgqk", grad_block, values, preferred_element_type=jnp.float32
        )
        grad_scores = (
            probs * (grad_probs - jnp.sum(probs * grad_probs, -1, keepdims=True))
        ).astype(jnp.bfloat16)
        grad_query = (
            jnp.einsum("nhgqk,nkhd->nqhgd", grad_scores, keys, preferred_element_type=jnp.float32)
            * scale
        )
        grad_keys = (
            grad_keys
            + jnp.einsum(
                "nhgqk,nqhgd->nkhd", grad_scores, query_block, preferred_element_type=jnp.float32
            )
            * scale
        )
        return ((grad_keys, grad_values), grad_query.astype(jnp.bfloat16))

    firsts = jnp.arange(length // block_rows) * block_rows
    zeros_kv = jnp.zeros((items, length, local_groups, HEAD_SIZE), jnp.float32)
    (grad_keys, grad_values), grad_queries = lax.scan(one_block, (zeros_kv, zeros_kv), firsts)
    grad_queries = jnp.moveaxis(grad_queries, 0, 1).reshape(
        items, length, local_groups, QUERIES_PER_KV, HEAD_SIZE
    )
    joined = jnp.concatenate(
        [
            grad_queries,
            grad_keys.astype(jnp.bfloat16)[:, :, :, None],
            grad_values.astype(jnp.bfloat16)[:, :, :, None],
        ],
        3,
    )
    return joined.reshape(items, length, local_groups, (QUERIES_PER_KV + 2) * HEAD_SIZE)


def swiglu(pre_ffn):
    gate_pre = pre_ffn[..., :FFE]
    up_pre = pre_ffn[..., FFE:]
    sigmoid_gate = jax.nn.sigmoid(gate_pre)
    silu_gate = gate_pre * sigmoid_gate
    return ((silu_gate * up_pre).astype(jnp.bfloat16), (gate_pre, up_pre, sigmoid_gate, silu_gate))


def swiglu_back(grad_hidden, pieces_kept):
    gate_pre, up_pre, sigmoid_gate, silu_gate = pieces_kept
    grad_gate = grad_hidden * up_pre * sigmoid_gate * (1.0 + gate_pre * (1.0 - sigmoid_gate))
    grad_up = grad_hidden * silu_gate
    return jnp.concatenate([grad_gate, grad_up], -1).astype(jnp.bfloat16)


def norm_factor(value):
    return lax.rsqrt(jnp.mean(value * value, -1, keepdims=True) + EPSILON)


def make_local(n_heads, chip, core):
    everyone = ("heads", "chip", "core")
    group = ("heads", "core")
    group_size = n_heads * core
    n_local = E // group_size
    groups_local = KEY_VALUE_HEADS // n_heads
    group_width = (QUERIES_PER_KV + 2) * HEAD_SIZE

    def own_experts(dense):
        split = dense.reshape(dense.shape[:-1] + (n_heads, n_local, core))
        axis = dense.ndim - 1
        mine = lax.dynamic_index_in_dim(split, lax.axis_index("heads"), axis, False)
        return lax.dynamic_index_in_dim(mine, lax.axis_index("core"), axis + 1, False)

    def local(
        tokens,
        cotangent,
        lengths,
        routes,
        attention_input_weight,
        attn_out,
        router,
        gain_attn,
        gain_ffn,
        expert_in,
        expert_out,
    ):
        slots, span, width = tokens.shape
        token_rows = slots * span
        length = span * n_heads
        rank = lax.axis_index("heads")
        qkv_width = attention_input_weight.shape[1]
        small = jnp.concatenate(
            [
                attention_input_weight,
                attn_out,
                router,
                gain_attn[:, None],
                gain_ffn[:, None],
                jnp.zeros((router.shape[0], 128 - E - 2), jnp.bfloat16),
            ],
            1,
        )
        small = lax.all_gather(small, everyone, axis=0, tiled=True)
        w_qkv = small[:, :qkv_width]
        w_proj = small[:, qkv_width : qkv_width + D]
        w_router = small[:, qkv_width + D : qkv_width + D + E]
        gain_one = small[:, qkv_width + D + E].astype(jnp.float32)
        gain_two = small[:, qkv_width + D + E + 1].astype(jnp.float32)
        whole_tokens = lax.all_gather(tokens, "heads", axis=1, tiled=True)

        positions = rank * span + jnp.arange(span, dtype=jnp.int32)
        valid = (positions[None, :] < lengths[:, None]).reshape(token_rows)
        valid_float = valid.astype(jnp.float32)[:, None]
        route_rows = routes.reshape(token_rows, TOPK)
        routed = jnp.any(
            route_rows[:, :, None] == jnp.arange(E, dtype=jnp.int32)[None, None, :], 1
        )
        live = (routed & valid[:, None]).astype(jnp.bfloat16)
        earlier = (
            jnp.arange(token_rows)[:, None] > jnp.arange(token_rows)[None, :]
        ).astype(jnp.bfloat16)
        count = jnp.dot(earlier, live, preferred_element_type=jnp.float32)
        kept = (live > 0) & (count < CAP)
        code = jnp.where(kept, count, jnp.where(routed, 200.0, -1.0)).astype(jnp.bfloat16)
        early = jnp.concatenate(
            [
                cotangent.reshape(token_rows, width),
                code,
                jnp.zeros((token_rows, 128 - E), jnp.bfloat16),
            ],
            1,
        )
        early = lax.all_gather(early, group, axis=0)
        grad_group = early[:, :, :width]
        code_group = early[:, :, width : width + E].astype(jnp.float32)
        own_in = lax.all_gather(expert_in, "chip", axis=0, tiled=True).reshape(
            n_local, D, 2 * FFE
        )
        own_out = lax.all_gather(expert_out, "chip", axis=0, tiled=True).reshape(n_local, D, FFE)

        whole_state = whole_tokens.astype(jnp.float32)
        normed_whole = (whole_state * norm_factor(whole_state) * gain_one).astype(jnp.bfloat16)
        w_mine = lax.dynamic_slice_in_dim(
            w_qkv, rank * (groups_local * group_width), groups_local * group_width, 1
        )
        before = jnp.dot(
            normed_whole.reshape(slots * length, width), w_mine, preferred_element_type=jnp.float32
        ).reshape(slots, length, groups_local, QUERIES_PER_KV + 2, HEAD_SIZE)
        cosine, sine = rotary_tables(jnp.arange(length, dtype=jnp.int32))
        cosine = cosine[None, :, None, None, :]
        sine = sine[None, :, None, None, :]
        turned = turn(before[:, :, :, : QUERIES_PER_KV + 1], cosine, sine, 1.0)
        packed = jnp.concatenate([turned, before[:, :, :, QUERIES_PER_KV + 1 :]], 3).astype(
            jnp.bfloat16
        )
        packed = packed.reshape(slots, length, groups_local, group_width)
        context_heads, log_total, received = attend_forward(packed)
        context = lax.all_to_all(
            context_heads, "heads", split_axis=1, concat_axis=2, tiled=True
        ).reshape(token_rows, QUERY_HEADS * HEAD_SIZE)

        state = tokens.astype(jnp.float32).reshape(token_rows, width)
        mid_state = state + jnp.dot(context, w_proj, preferred_element_type=jnp.float32)
        normed_two, factor_two = norm_rows(mid_state, gain_two)
        normed_ffn = normed_two.astype(jnp.bfloat16)
        normed_group = lax.all_gather(normed_ffn, group, axis=0)

        def gates_of(rows, codes):
            logits = jnp.dot(rows, w_router, preferred_element_type=jnp.float32)
            inside = codes >= 0
            highest = jnp.max(jnp.where(inside, logits, NEGATIVE), -1, keepdims=True)
            weights = jnp.where(inside, jnp.exp(jnp.where(inside, logits - highest, 0.0)), 0.0)
            return weights / jnp.sum(weights, -1, keepdims=True)

        gates = gates_of(normed_ffn, code.astype(jnp.float32))
        gates_own = own_experts(gates_of(normed_group, code_group))
        code_own = own_experts(code_group)

        place = jnp.arange(CAP, dtype=jnp.float32)[None, :, None]
        picks, out_rows, back_rows, gate_grads, grads_in, grads_out = [], [], [], [], [], []
        flat = group_size * CAP
        for i in range(n_local):
            hit = code_own[:, None, :, i] == place
            pick = hit.astype(jnp.bfloat16)
            gate_row = jnp.sum(
                jnp.where(hit, gates_own[:, None, :, i], 0.0), -1
            ).reshape(flat, 1)
            buffer = jnp.einsum(
                "sct,std->scd", pick, normed_group, preferred_element_type=jnp.bfloat16
            ).reshape(flat, width)
            grad_row = jnp.einsum(
                "sct,std->scd", pick, grad_group, preferred_element_type=jnp.bfloat16
            ).reshape(flat, width)
            pre = jnp.dot(buffer, own_in[i], preferred_element_type=jnp.float32)
            hidden, pieces_kept = swiglu(pre)
            outputs = jnp.dot(hidden, own_out[i].T, preferred_element_type=jnp.float32)
            grad_plain = jnp.dot(grad_row, own_out[i], preferred_element_type=jnp.float32)
            gate_grad = jnp.sum(grad_plain * hidden.astype(jnp.float32), -1)
            grad_pre = swiglu_back(gate_row * grad_plain, pieces_kept)
            back = jnp.dot(grad_pre, own_in[i].T, preferred_element_type=jnp.float32)
            grad_outputs = (gate_row * grad_row.astype(jnp.float32)).astype(jnp.bfloat16)
            grads_in.append(
                lax.dot_general(
                    buffer,
                    grad_pre,
                    (((0,), (0,)), ((), ())),
                    preferred_element_type=jnp.float32,
                )
            )
            grads_out.append(
                lax.dot_general(
                    grad_outputs,
                    hidden,
                    (((0,), (0,)), ((), ())),
                    preferred_element_type=jnp.float32,
                )
            )
            picks.append(pick)
            out_rows.append(
                (gate_row * outputs).astype(jnp.bfloat16).reshape(group_size, CAP, width)
            )
            back_rows.append(back.astype(jnp.bfloat16).reshape(group_size, CAP, width))
            gate_grads.append(
                jnp.sum(
                    jnp.where(hit, gate_grad.reshape(group_size, CAP, 1), 0.0), 1
                )
            )
        pick_all = jnp.concatenate(picks, 1)
        back_sum = jnp.einsum(
            "sct,scd->std",
            pick_all,
            jnp.concatenate(back_rows, 1),
            preferred_element_type=jnp.float32,
        ).astype(jnp.bfloat16)
        back_sum = lax.psum_scatter(
            back_sum.reshape(group_size * token_rows, width),
            group,
            scatter_dimension=0,
            tiled=True,
        )
        gate_back = lax.all_to_all(
            jnp.stack(gate_grads, 1), group, split_axis=0, concat_axis=0, tiled=True
        )
        mix_sum = jnp.einsum(
            "sct,scd->std",
            pick_all,
            jnp.concatenate(out_rows, 1),
            preferred_element_type=jnp.float32,
        ).astype(jnp.bfloat16)
        mixture = lax.psum_scatter(
            mix_sum.reshape(group_size * token_rows, width),
            group,
            scatter_dimension=0,
            tiled=True,
        )
        grad_expert_in = lax.psum_scatter(
            jnp.concatenate(grads_in, 0), "chip", scatter_dimension=0, tiled=True
        )
        grad_expert_out = lax.psum_scatter(
            jnp.concatenate(grads_out, 0), "chip", scatter_dimension=0, tiled=True
        )
        mixed = (valid_float * (mid_state + mixture.astype(jnp.float32))).astype(jnp.bfloat16)

        grad_gates = jnp.transpose(
            gate_back.reshape(n_heads, core, n_local, token_rows), (3, 0, 2, 1)
        ).reshape(token_rows, E)
        grad_logits = gates * (grad_gates - jnp.sum(gates * grad_gates, -1, keepdims=True))
        grad_logits = grad_logits * valid_float
        grad_out = cotangent.astype(jnp.float32).reshape(token_rows, width) * valid_float
        grad_normed_ffn = back_sum.astype(jnp.float32) + jnp.dot(
            grad_logits, w_router.astype(jnp.float32).T, precision=TOP_PRECISION
        )
        router_term = jnp.dot(
            normed_ffn.astype(jnp.float32).T, grad_logits, precision=TOP_PRECISION
        )
        grad_mid_norm, gain_two_term = norm_back(grad_normed_ffn, mid_state, factor_two, gain_two)
        grad_mid = grad_out + grad_mid_norm
        grad_mid_low = grad_mid.astype(jnp.bfloat16)
        proj_term = lax.dot_general(
            context, grad_mid_low, (((0,), (0,)), ((), ())), preferred_element_type=jnp.float32
        )
        second = lax.psum_scatter(
            jnp.concatenate(
                [
                    proj_term,
                    router_term,
                    gain_two_term[:, None],
                    jnp.zeros((D, 128 - E - 1), jnp.float32),
                ],
                1,
            ),
            everyone,
            scatter_dimension=0,
            tiled=True,
        )
        grad_attn_out = second[:, :D]
        grad_router = second[:, D : D + E]
        grad_gain_ffn = second[:, D + E]
        context_gradient = jnp.dot(
            grad_mid_low, w_proj.T, preferred_element_type=jnp.float32
        ).astype(jnp.bfloat16)
        context_gradient = context_gradient.reshape(
            slots, span, KEY_VALUE_HEADS, QUERIES_PER_KV * HEAD_SIZE
        )
        grad_context_heads = lax.all_to_all(
            context_gradient, "heads", split_axis=2, concat_axis=1, tiled=True
        )
        grad_packed = attend_backward(received, log_total, grad_context_heads)
        grad_pieces = grad_packed.astype(jnp.float32).reshape(
            slots, length, groups_local, QUERIES_PER_KV + 2, HEAD_SIZE
        )
        grad_turned = turn(grad_pieces[:, :, :, : QUERIES_PER_KV + 1], cosine, sine, -1.0)
        grad_before = jnp.concatenate(
            [grad_turned, grad_pieces[:, :, :, QUERIES_PER_KV + 1 :]], 3
        ).astype(jnp.bfloat16)
        grad_before = grad_before.reshape(slots, length, groups_local * group_width)
        qkv_term = lax.dot_general(
            normed_whole.reshape(slots * length, width),
            grad_before.reshape(slots * length, groups_local * group_width),
            (((0,), (0,)), ((), ())),
            preferred_element_type=jnp.float32,
        )
        rows_each = D // (n_heads * chip * core)
        qkv_term = jnp.swapaxes(
            qkv_term.reshape(n_heads, chip * core, rows_each, groups_local * group_width), 0, 1
        ).reshape(D, groups_local * group_width)
        qkv_part = lax.psum_scatter(qkv_term, ("chip", "core"), scatter_dimension=0, tiled=True)
        grad_attn_in = lax.all_to_all(
            qkv_part, "heads", split_axis=0, concat_axis=1, tiled=True
        )
        grad_gain_attn = jnp.sum(
            grad_attn_in * attention_input_weight.astype(jnp.float32), -1
        ) / gain_attn.astype(jnp.float32)
        grad_mine = lax.all_to_all(
            grad_before, "heads", split_axis=1, concat_axis=2, tiled=True
        ).reshape(token_rows, qkv_width)
        grad_normed_attn = jnp.dot(grad_mine, w_qkv.T, preferred_element_type=jnp.float32)
        grad_state_norm, _ = norm_back(grad_normed_attn, state, norm_factor(state), gain_one)
        grad_tokens = (grad_mid + grad_state_norm).astype(jnp.bfloat16).reshape(tokens.shape)
        return (
            mixed.reshape(tokens.shape),
            grad_tokens,
            grad_attn_in,
            grad_attn_out,
            grad_router,
            grad_gain_attn,
            grad_gain_ffn,
            grad_expert_in,
            grad_expert_out,
        )

    return local


def solution(mesh):
    n_heads, n_shard = mesh.shape["heads"], mesh.shape["shard"]
    core = 2 if n_heads * n_shard == E else 1
    chip = n_shard // core
    split = jax.sharding.Mesh(
        mesh.devices.reshape(n_heads, chip, core), ("heads", "chip", "core")
    )
    shard = ("chip", "core")
    everyone = ("heads", "chip", "core")
    token_spec = P(shard, "heads", None)
    rows = P(everyone, None)
    in_specs = (
        token_spec,
        token_spec,
        P(shard),
        token_spec,
        rows,
        rows,
        rows,
        P(everyone),
        P(everyone),
        rows,
        rows,
    )
    out_specs = (token_spec, token_spec, rows, rows, rows, P(everyone), P(everyone), rows, rows)
    return jax.shard_map(
        make_local(n_heads, chip, core),
        mesh=split,
        in_specs=in_specs,
        out_specs=out_specs,
        check_vma=False,
    )
```

time: 3870 us -> 1370 us (0.35)
  waiting for transfers between devices: 2310 us -> 786 us
  matrix products: 700 us -> 282 us
  local copies, waits for them, and re-layouts: 359 us -> 104 us
  blocking collectives: 214 us -> 53.8 us
  loops' own time: 92.3 us -> 8.49 us
  other arithmetic: 148 us -> 94.2 us
    unnamed x10 -> x13, waiting for transfers between devices: 1410 us -> 17.5 us
    dot_general x196 -> x40, matrix products: 608 us -> 188 us  [the longest x4 25.9 us: local(): jnp.dot(grad_row, own_out[i], preferred_element_type=jnp.float32)]
    reduce_scatter x4 -> x5, waiting for transfers between devices: 569 us -> 370 us  [the longest x1 158 us: local(): lax.psum_scatter(jnp.concatenate(grads_in, 0), 'chip', scatter_dimension=...]
    unnamed x2 -> x0, blocking collectives: 84.6 us -> none
    another operation x6 -> x0, loops' own time: 83.9 us -> none  [the longest x2 43.4 us: grad_rows(): lax.map(grad_one_step, jnp.arange(piece_rows // step_rows, dtype=jnp.int32))]
    dynamic_slice x128 -> x0, local copies, waits for them, and re-layouts: 73.6 us -> none  [map_rows(): lax.map(map_one_step, jnp.arange(piece_rows // step_rows, dtype=jnp.int32))]
    all_gather x1 -> x0, blocking collectives: 70.6 us -> none  [local(): lax.all_gather(router, ('heads', 'shard'), axis=0, tiled=True)]
    gather x2 -> x0, local copies, waits for them, and re-layouts: 58.9 us -> none  [the longest x1 29.5 us: local(): picked = table[target].reshape(token_rows, TOPK, D)]
  transfers between devices with their start and end apart: 12 -> 16, of which waited for: 6 -> 14; matrix products, arithmetic and copies ran while one was open for 17% -> 19% of each run, Pallas kernels for 0% -> 0%
where the time goes in v1:
time: 1370 us; the launch traced here: 1360 us
  waiting for transfers between devices  786 us (57%)
  matrix products  282 us (21%)
  local copies, waits for them, and re-layouts  104 us (8%)
  other arithmetic  94.2 us (7%)
  blocking collectives  53.8 us (4%)
  starting transfers between devices  17.6 us (1%)
  between operations  16 us (1%)
    reduce_scatter x1, waiting for transfers between devices, local(): lax.psum_scatter(jnp.concatenate(grads_in, 0), 'chip', scatter_dimension=...  158 us
    reduce_scatter x1, waiting for transfers between devices, local(): lax.psum_scatter(mix_sum.reshape(group_size * token_rows, width), group,...  85.3 us
    reduce_scatter x1, waiting for transfers between devices, local(): lax.psum_scatter(jnp.concatenate(grads_out, 0), 'chip', scatter_dimension...  85 us
    all_gather x1, waiting for transfers between devices, local(): whole_tokens = lax.all_gather(tokens, 'heads', axis=1, tiled=True)  76.4 us
    all_gather x1, waiting for transfers between devices, local(): small = lax.all_gather(small, everyone, axis=0, tiled=True)  69.5 us
    all_gather x1, waiting for transfers between devices, local(): lax.all_gather(expert_in, 'chip', axis=0, tiled=True)  65.6 us
    all_to_all x1, waiting for transfers between devices, local(): lax.all_to_all(grad_before, 'heads', split_axis=1, concat_axis=2, tiled=T...  59.7 us
    all_to_all x1, blocking collectives, local(): lax.all_to_all(context_heads, 'heads', split_axis=1, concat_axis=2, tiled...  53.8 us
  transfers between devices with their start and end apart: 16, of which 14 were waited for; matrix products, arithmetic and copies ran while one was open for 19% of the time, Pallas kernels for 0%

profile of v1, /device:TPU:0, one launch (start us, length us, event | category | flops | bytes accessed | tf_op | source)
XLA Modules:
  0.0 1361.6 jit_solution(6161674826024370405)
XLA Ops:
  16.7 76.4 %all-gather.9.cloned.1.call-done = bf16[2,1024,1024]{2,1,0:T(8,128)(2,1)} async-done(((bf16[2,256,1024]{2,1,0:T(8,128)(2,1)}), bf16[2,1024,1024]{2,1,0:T(8,128)(2,1)}) %all-gather.9.cloned.1.call-update) | async-done | bytes 4194320 | tf_op jit(solution)/shard_map/all_gather | solution.py:226
  96.2 69.5 %all-gather.11.cloned.1.call-done = bf16[1024,3200]{1,0:T(8,128)(2,1)} async-done(((bf16[32,3200]{1,0:T(8,128)(2,1)}), bf16[1024,3200]{1,0:T(8,128)(2,1)}) %all-gather.11.cloned.1.call-update) | async-done | bytes 6553616 | tf_op jit(solution)/shard_map/all_gather | solution.py:220
  177.2 33.2 %while.27 = (s32[]{:T(128)}, bf16[2,2,512,2,2,64]{2,5,4,3,1,0:T(8,128)(2,1)S(1)}, f32[2,2,2,2,512]{4,3,2,1,0:T(2,128)S(1)}, s32[2]{0:T(128)S(1)}, bf16[2,1024,2,...) while((s32[]{:T(128)}, ...), condition=%wide.region_4.5_spmd, body=%wide.region_1.0_spmd.sunk | while | flops 1124856320 | bytes 54661288 | solution.py:96
  219.6 53.8 %all_to_all.69 = bf16[2,1024,2,128]{3,2,0,1:T(2,128)(2,1)S(1)} all-to-all(bf16[2,1024,2,128]{3,2,0,1:T(2,128)(2,1)S(1)} %reshape.439), channel_id=1, replica_groups=mesh['heads'=4,'chip'=4,'core'=2] {'heads'}, dimensions={1} | all-to-all | bytes 2097152 | tf_op jit(solution)/shard_map/all_to_all | solution.py:275
  286.7 7.9 fusion.80
  311.4 52.5 %all-gather.19.cloned.1.call-done = bf16[4096,1024]{1,0:T(8,128)(2,1)} async-done(((bf16[512,1024]{1,0:T(8,128)(2,1)}), bf16[4096,1024]{1,0:T(8,128)(2,1)}) %all-gather.19.cloned.1.call-update) | async-done | bytes 8388624 | tf_op jit(solution)/shard_map/all_gather | solution.py:283
  386.3 65.6 %all-gather.13.cloned.1.call-done = bf16[4096,1024]{1,0:T(8,128)(2,1)} async-done(((bf16[1024,1024]{1,0:T(8,128)(2,1)}), bf16[4096,1024]{1,0:T(8,128)(2,1)}) %all-gather.13.cloned.1.call-update) | async-done | bytes 8388624 | tf_op jit(solution)/shard_map/all_gather | solution.py:253
  451.8 7.6 fusion.123
  459.4 46.8 %all-gather.15.cloned.1.call-done = bf16[4096,512]{1,0:T(8,128)(2,1)} async-done(((bf16[1024,512]{1,0:T(8,128)(2,1)}), bf16[4096,512]{1,0:T(8,128)(2,1)}) %all-gather.15.cloned.1.call-update) | async-done | bytes 4194320 | tf_op jit(solution)/shard_map/all_gather | solution.py:256
  593.4 12.5 fusion.68
  621.3 12.5 fusion.71
  654.2 42.5 %reduce-scatter.11.cloned.1.call-done = bf16[512,1024]{1,0:T(8,128)(2,1)} async-done(((bf16[4096,1024]{1,0:T(8,128)(2,1)}), bf16[512,1024]{1,0:T(8,128)(2,1)}) %reduce-scatter.11.cloned.1.call-update) | async-done | bytes 1048592 | tf_op jit(solution)/shard_map/reduce_scatter | solution.py:352
  701.7 85.3 %reduce-scatter.9.cloned.1.call-done = bf16[512,1024]{1,0:T(8,128)(2,1)} async-done(((bf16[4096,1024]{1,0:T(8,128)(2,1)}), bf16[512,1024]{1,0:T(8,128)(2,1)}) %reduce-scatter.9.cloned.1.call-update) | async-done | bytes 1048592 | tf_op jit(solution)/shard_map/reduce_scatter | solution.py:367
  806.0 17.7 %all-to-all-done.2 = bf16[2,256,8,128]{3,1,0,2:T(8,128)(2,1)S(1)} async-done(((bf16[2,256,8,128]{3,1,0,2:T(8,128)(2,1)}), bf16[2,256,8,128]{3,1,0,2:T(8,128)(2,1)S(1)}, u32[]{:S(2)}, u32[]{:S(2)}) %all-to-all-start.2) | async-done | bytes 1048608 | tf_op jit(solution)/shard_map/all_to_all | solution.py:422
  827.0 91.9 %while.28 = (s32[]{:T(128)}, f32[2,1024,2,64]{1,3,2,0:T(8,128)}, f32[2,1024,2,64]{1,3,2,0:T(8,128)}, bf16[2,2,512,2,2,64]{2,5,4,3,1,0:T(8,128)(2,1)}, s32[2]{0:T...) while((s32[]{:T(128)}, f32[2,1024,2,64]{1,3,2,0:T(8,128)}, ...), condition=%wide.region_30.31_spmd.clone, body=%wide.region_28.30_spmd.clone.sunk | while | flops 2749624832 | bytes 195482096 | solution.py:143
  840.3 11.2 fusion.262
  851.5 8.4 fusion.263
  886.6 11.2 fusion.262
  897.8 8.4 fusion.263
  943.3 13.0 concatenate.72
  1012.2 59.7 %all-to-all-done.3 = bf16[2,1024,512]{2,0,1:T(2,128)(2,1)} async-done(((bf16[2,1024,512]{2,0,1:T(2,128)(2,1)}), bf16[2,1024,512]{2,0,1:T(2,128)(2,1)}, u32[]{:S(2)}, u32[]{:S(2)}) %all-to-all-start.3) | async-done | bytes 2097184 | tf_op jit(solution)/shard_map/all_to_all | solution.py:451
  1092.0 15.7 %reduce-scatter.19.cloned.1.call-done = f32[32,1152]{1,0:T(8,128)} async-done(((f32[1024,1152]{1,0:T(8,128)}), f32[32,1152]{1,0:T(8,128)}) %reduce-scatter.19.cloned.1.call-update) | async-done | bytes 147472
  1112.0 85.0 %reduce-scatter.17.cloned.1.call-done = f32[1024,512]{1,0:T(8,128)} async-done(((f32[4096,512]{1,0:T(8,128)}), f32[1024,512]{1,0:T(8,128)}) %reduce-scatter.17.cloned.1.call-update) | async-done | bytes 2097168 | tf_op jit(solution)/shard_map/reduce_scatter | solution.py:376
  1196.9 157.6 %reduce-scatter.15.cloned.1.call-done = f32[1024,1024]{1,0:T(8,128)} async-done(((f32[4096,1024]{1,0:T(8,128)}), f32[1024,1024]{1,0:T(8,128)}) %reduce-scatter.15.cloned.1.call-update) | async-done | bytes 4194320 | tf_op jit(solution)/shard_map/reduce_scatter | solution.py:373
  (476 shorter events, 416.5 us)
Async XLA Ops:
  7.2 85.9 %all-gather.9.cloned.1.call-start = ((), (), s32[]{:S(2)}) async-start(), calls=%async_computation.11 | async-start | bytes 5242880 | tf_op jit(solution)/shard_map/all_gather | solution.py:226
  7.9 157.8 %all-gather.11.cloned.1.call-start = ((), (), s32[]{:S(2)}) async-start(), calls=%async_computation.12 | async-start | bytes 6758400 | tf_op jit(solution)/shard_map/all_gather | solution.py:220
  11.2 273.6 %all-gather.17.cloned.1.call-start = ((), (), s32[]{:S(2)}) async-start(), calls=%async_computation.20 | async-start | bytes 10616832 | tf_op jit(solution)/shard_map/all_gather | solution.py:250
  15.4 348.5 %all-gather.19.cloned.1.call-start = ((), (), s32[]{:S(2)}) async-start(), calls=%async_computation.21 | async-start | bytes 9437184 | tf_op jit(solution)/shard_map/all_gather | solution.py:283
  16.7 159.6 %copy-start.58 = (f32[1024,32]{0,1:T(8,128)}, f32[1024,32]{0,1:T(8,128)S(1)}, u32[]{:S(2)}) copy-start(f32[1024,32]{0,1:T(8,128)S(1)} %get-tuple-element.275) | copy-start | bytes 393220
  283.6 168.2 %all-gather.13.cloned.1.call-start = ((), (), s32[]{:S(2)}) async-start(), calls=%async_computation.13 | async-start | bytes 10485760 | tf_op jit(solution)/shard_map/all_gather | solution.py:253
  284.2 222.1 %all-gather.15.cloned.1.call-start = ((), (), s32[]{:S(2)}) async-start(), calls=%async_computation.14 | async-start | bytes 5242880 | tf_op jit(solution)/shard_map/all_gather | solution.py:256
  284.8 412.0 %reduce-scatter.11.cloned.1.call-start = ((), (), s32[]{:S(2)}) async-start(), calls=%async_computation.16 | async-start | bytes 9437184 | tf_op jit(solution)/shard_map/reduce_scatter | solution.py:352
  374.6 170.3 %copy-start.20 = (bf16[8,160,1024]{2,1,0:T(8,128)(2,1)}, bf16[8,160,1024]{2,1,0:T(8,128)(2,1)S(1)}, u32[]{:S(2)}) copy-start(bf16[8,160,1024]{2,1,0:T(8,128)(2,1)S(1)} %fusion.84) | copy-start | bytes 7864324
  515.7 90.7 %copy-start.78 = (f32[1280]{0:T(1024)}, f32[1280]{0:T(1024)S(1)}, u32[]{:S(2)}) copy-start(f32[1280]{0:T(1024)S(1)} %mul.529) | copy-start | bytes 15364
  605.9 181.1 %reduce-scatter.9.cloned.1.call-start = ((), (), s32[]{:S(2)}) async-start(), calls=%async_computation.15 | async-start | bytes 9437184 | tf_op jit(solution)/shard_map/reduce_scatter | solution.py:367
  640.1 11.6 all-to-all-start.1
  654.2 132.8 %copy-start.28 = (bf16[2,256,1024]{2,1,0:T(8,128)(2,1)S(1)}, bf16[2,256,1024]{2,1,0:T(8,128)(2,1)}, u32[]{:S(2)}) copy-start(bf16[2,256,1024]{2,1,0:T(8,128)(2,1)} %param.16) | copy-start | bytes 3145732
  654.2 132.8 %copy-start.71 = (f32[1024]{0:T(1024)S(1)}, f32[1024]{0:T(1024)}, u32[]{:S(2)}) copy-start(f32[1024]{0:T(1024)} %get-tuple-element.193) | copy-start | bytes 12292
  654.2 132.8 %copy-start.77 = (f32[512]{0:T(512)S(1)}, f32[512]{0:T(512)}, u32[]{:S(2)}) copy-start(f32[512]{0:T(512)} %copy-done.76) | copy-start | bytes 6148
  654.2 132.8 %copy-start.89 = (f32[512]{0:T(512)S(1)}, f32[512]{0:T(512)}, u32[]{:S(2)}) copy-start(f32[512]{0:T(512)} %convert_element_type.239) | copy-start | bytes 6148
  795.9 27.8 %all-to-all-start.2 = ((bf16[2,256,8,128]{3,1,0,2:T(8,128)(2,1)}), bf16[2,256,8,128]{3,1,0,2:T(8,128)(2,1)S(1)}, u32[]{:S(2)}, u32[]{:S(2)}) async-start(bf16[2,256,8,128]{3,1,0,2:T(8,128)(2,1)} %copy.219), calls=%async_computation.4 | async-start | bytes 2097152 | tf_op jit(solution)/shard_map/all_to_all | solution.py:422
  799.4 278.2 %reduce-scatter.13.cloned.1.call-start = ((), (), s32[]{:S(2)}) async-start(), calls=%async_computation.17 | async-start | bytes 2359296 | tf_op jit(solution)/shard_map/reduce_scatter | solution.py:444
  936.7 171.0 %reduce-scatter.19.cloned.1.call-start = ((), (), s32[]{:S(2)}) async-start(), calls=%async_computation.22 | async-start | bytes 4866048
  962.8 234.2 %reduce-scatter.17.cloned.1.call-start = ((), (), s32[]{:S(2)}) async-start(), calls=%async_computation.19 | async-start | bytes 10485760 | tf_op jit(solution)/shard_map/reduce_scatter | solution.py:376
  978.2 376.3 %reduce-scatter.15.cloned.1.call-start = ((), (), s32[]{:S(2)}) async-start(), calls=%async_computation.18 | async-start | bytes 20971520 | tf_op jit(solution)/shard_map/reduce_scatter | solution.py:373
  1007.3 64.6 %all-to-all-start.3 = ((bf16[2,1024,512]{2,0,1:T(2,128)(2,1)}), bf16[2,1024,512]{2,0,1:T(2,128)(2,1)}, u32[]{:S(2)}, u32[]{:S(2)}) async-start(bf16[2,1024,512]{2,0,1:T(2,128)(2,1)} %copy.222), calls=%async_computation.5 | async-start | bytes 4194304 | tf_op jit(solution)/shard_map/all_to_all | solution.py:451
  1077.6 13.7 %all-to-all-start.4 = ((f32[4,32,512]{2,1,0:T(8,128)}), f32[4,32,512]{2,1,0:T(8,128)S(1)}, u32[]{:S(2)}, u32[]{:S(2)}) async-start(f32[4,32,512]{2,1,0:T(8,128)} %bitcast.368), calls=%async_computation.7 | async-start | bytes 524288 | tf_op jit(solution)/shard_map/all_to_all | solution.py:445
  1091.3 263.2 %copy-start.63 = (f32[4,4,8,512]{3,2,0,1:T(8,128)}, f32[4,4,8,512]{3,2,0,1:T(8,128)S(1)}, u32[]{:S(2)}) copy-start(f32[4,4,8,512]{3,2,0,1:T(8,128)S(1)} %copy.264) | copy-start | bytes 786436
  (121 other events, 1087.0 us)
Sparse Core Ops, SparseCore 0:
  9.6 83.4 all-gather.8
  96.5 69.1 all-gather.10
  167.4 111.5 all-gather.16
  283.7 80.1 all-gather.18
  365.6 86.1 all-gather.12
  453.5 52.6 all-gather.14
  606.0 90.6 reduce-scatter.10
  699.0 87.9 reduce-scatter.8
  936.9 40.2 reduce-scatter.12
  983.4 124.2 reduce-scatter.18
  1111.3 85.5 reduce-scatter.16
  1200.7 153.7 reduce-scatter.14

commit v2 on v1

v2 whole, which is shorter than its diff:
```python
import functools
import math

import jax
import jax.numpy as jnp
import numpy as np
from jax import lax
from jax.experimental import pallas as pl
from jax.experimental.pallas import tpu as pltpu
from jax.sharding import PartitionSpec as P

D = 1024
QUERY_HEADS = 16
KEY_VALUE_HEADS = 8
HEAD_SIZE = 64
E = 32
FFE = 512
TOPK = 8
QUERIES_PER_KV = 2
CAP = 160
GROUP = (QUERIES_PER_KV + 2) * HEAD_SIZE
PAIR = QUERIES_PER_KV * HEAD_SIZE
TAIL = 128
BLOCK = 256
VMEM_BYTES = 56 * 2**20


EPSILON = 1e-06
THETA_BASE = 10000.0
NEGATIVE = -1e30
TOP_PRECISION = lax.Precision.HIGHEST
SCALE = 1.0 / math.sqrt(HEAD_SIZE)
SHORT = pl.CostEstimate(flops=1024, bytes_accessed=1024, transcendentals=0)


def dot_nn(left, right):
    return jnp.dot(left, right, preferred_element_type=jnp.float32)


def dot_nt(left, right):
    return lax.dot_general(
        left, right, (((1,), (1,)), ((), ())), preferred_element_type=jnp.float32
    )


def dot_tn(left, right):
    return lax.dot_general(
        left, right, (((0,), (0,)), ((), ())), preferred_element_type=jnp.float32
    )


def norm_factor(value):
    return lax.rsqrt(jnp.mean(value * value, -1, keepdims=True) + EPSILON)


def norm_back(grad_in, value, factor, gain):
    normalized_rows = value * factor
    scaled = grad_in * gain
    gain_term = jnp.sum(grad_in * normalized_rows, 0)
    grad_value = factor * (
        scaled - normalized_rows * jnp.mean(scaled * normalized_rows, -1, keepdims=True)
    )
    return (grad_value, gain_term)


def rotary_tables(length):
    half_size = HEAD_SIZE // 2
    freqs = THETA_BASE ** (-2.0 * np.arange(half_size) / HEAD_SIZE)
    angles = np.arange(length)[:, None] * freqs[None, :]
    cosine, sine = np.cos(angles), np.sin(angles)
    one = np.ones((length, HEAD_SIZE))
    own = np.concatenate([cosine, cosine] * (QUERIES_PER_KV + 1) + [one], 1)
    other = np.concatenate([-sine, sine] * (QUERIES_PER_KV + 1) + [0.0 * one], 1)
    return (jnp.asarray(own, jnp.float32), jnp.asarray(other, jnp.float32))


def partner(values):
    width = values.shape[1]
    lane = lax.broadcasted_iota(jnp.int32, values.shape, 1)
    half_size = HEAD_SIZE // 2
    return jnp.where(
        lax.rem(lane, HEAD_SIZE) < half_size,
        pltpu.roll(values, width - half_size, 1),
        pltpu.roll(values, half_size, 1),
    )


def stack_queries(block):
    values = block.astype(jnp.float32) * SCALE
    low = lax.broadcasted_iota(jnp.int32, values.shape, 1) < HEAD_SIZE
    first = jnp.where(low, values, 0.0)
    second = jnp.where(low, pltpu.roll(values, HEAD_SIZE, 1), 0.0)
    return jnp.concatenate([first, second], 0).astype(jnp.bfloat16)


def stack_grads(block):
    values = block.astype(jnp.float32)
    low = lax.broadcasted_iota(jnp.int32, values.shape, 1) < HEAD_SIZE
    first = jnp.where(low, 0.0, pltpu.roll(values, HEAD_SIZE, 1))
    second = jnp.where(low, 0.0, values)
    return jnp.concatenate([first, second], 0).astype(jnp.bfloat16)


def attention_forward_kernel(pieces, place_ref, *refs):
    xs, refs = refs[:pieces], refs[pieces:]
    gain_ref, w_ref, own_ref, other_ref = refs[:4]
    packed_ref, context_ref, lse_ref, normed_ref = refs[4:]
    span = xs[0].shape[1]
    length = pieces * span

    @pl.when(pl.program_id(1) == 0)
    def _():
        for step in range(pieces):
            at = place_ref[step]
            for start in range(0, span, BLOCK):
                value = xs[step][0, start : start + BLOCK, :].astype(jnp.float32)
                normed_ref[at, 0, start : start + BLOCK, :] = (
                    value * norm_factor(value) * gain_ref[...]
                ).astype(jnp.bfloat16)

    for start in range(0, length, BLOCK):
        rows = slice(start, start + BLOCK)
        before = dot_nn(
            normed_ref[start // span, 0, start % span : start % span + BLOCK, :], w_ref[...]
        )
        packed_ref[0, rows, :] = (
            before * own_ref[rows, :] + partner(before) * other_ref[rows, :]
        ).astype(jnp.bfloat16)

    low = lax.broadcasted_iota(jnp.int32, (BLOCK, PAIR), 1) < HEAD_SIZE
    lane_zero = lax.broadcasted_iota(jnp.int32, (BLOCK, PAIR), 1) == 0
    query_row = lax.rem(lax.broadcasted_iota(jnp.int32, (2 * BLOCK, BLOCK), 0), BLOCK)
    allowed = lax.broadcasted_iota(jnp.int32, (2 * BLOCK, BLOCK), 1) <= query_row
    for start in range(0, length, BLOCK):
        rows = slice(start, start + BLOCK)
        queries = stack_queries(packed_ref[0, rows, :PAIR])
        inside = packed_ref[0, rows, PAIR:]
        scores_inside = jnp.where(allowed, dot_nt(queries, inside), NEGATIVE)
        highest = jnp.max(scores_inside, 1, keepdims=True)
        if start:
            before_keys = packed_ref[0, :start, PAIR:]
            scores_before = dot_nt(queries, before_keys)
            highest = jnp.maximum(highest, jnp.max(scores_before, 1, keepdims=True))
        weights = jnp.exp(scores_inside - highest)
        total = jnp.sum(weights, 1, keepdims=True)
        result = dot_nn(weights.astype(jnp.bfloat16), inside)
        if start:
            weights = jnp.exp(scores_before - highest)
            total = total + jnp.sum(weights, 1, keepdims=True)
            result = result + dot_nn(weights.astype(jnp.bfloat16), before_keys)
        result = result / total
        context_ref[start // span, 0, start % span : start % span + BLOCK, :] = jnp.where(
            low, pltpu.roll(result[:BLOCK], HEAD_SIZE, 1), result[BLOCK:]
        ).astype(jnp.bfloat16)
        log_total = highest + jnp.log(total)
        columns = jnp.where(lane_zero, log_total[:BLOCK], log_total[BLOCK:])
        lse_ref[0, 0, :, rows] = columns.T[:8, :]


def attention_forward(xs, places, gain, weights, tables, groups_local):
    pieces = len(xs)
    slots, span, width = xs[0].shape
    length = pieces * span
    bf16, f32 = jnp.bfloat16, jnp.float32
    return pl.pallas_call(
        functools.partial(attention_forward_kernel, pieces),
        grid_spec=pltpu.PrefetchScalarGridSpec(
            num_scalar_prefetch=1,
            grid=(slots, groups_local),
            in_specs=[pl.BlockSpec((1, span, width), lambda s, g, place: (s, 0, 0))] * pieces
            + [
                pl.BlockSpec((1, width), lambda s, g, place: (0, 0)),
                pl.BlockSpec((width, GROUP), lambda s, g, place: (0, g)),
                pl.BlockSpec((length, GROUP), lambda s, g, place: (0, 0)),
                pl.BlockSpec((length, GROUP), lambda s, g, place: (0, 0)),
            ],
            out_specs=[
                pl.BlockSpec((1, length, GROUP), lambda s, g, place: (s, 0, g)),
                pl.BlockSpec((pieces, 1, span, PAIR), lambda s, g, place: (0, s, 0, g)),
                pl.BlockSpec((1, 1, 8, length), lambda s, g, place: (s, g, 0, 0)),
                pl.BlockSpec((pieces, 1, span, width), lambda s, g, place: (0, s, 0, 0)),
            ],
        ),
        out_shape=[
            jax.ShapeDtypeStruct((slots, length, groups_local * GROUP), bf16),
            jax.ShapeDtypeStruct((pieces, slots, span, groups_local * PAIR), bf16),
            jax.ShapeDtypeStruct((slots, groups_local, 8, length), f32),
            jax.ShapeDtypeStruct((pieces, slots, span, width), bf16),
        ],
        compiler_params=pltpu.CompilerParams(vmem_limit_bytes=VMEM_BYTES),
        cost_estimate=SHORT,
        name="attention_forward",
    )(places, *xs, gain, weights, *tables)


def attention_backward_kernel(
    packed_ref, lse_ref, grad_ref, own_ref, other_ref, out_ref, total_ref
):
    length, span = packed_ref.shape[1], grad_ref.shape[2]
    low = lax.broadcasted_iota(jnp.int32, (BLOCK, PAIR), 1) < HEAD_SIZE
    query_lane = lax.rem(lax.broadcasted_iota(jnp.int32, (BLOCK, 2 * BLOCK), 1), BLOCK)
    allowed = lax.broadcasted_iota(jnp.int32, (BLOCK, 2 * BLOCK), 0) <= query_lane
    total_ref[...] = jnp.zeros_like(total_ref)

    def unturn(values, lanes, rows):
        values = values.astype(jnp.bfloat16).astype(jnp.float32)
        return (
            values * own_ref[rows, lanes] - partner(values) * other_ref[rows, lanes]
        ).astype(jnp.bfloat16)

    for start in range(0, length, BLOCK):
        rows = slice(start, start + BLOCK)
        queries = stack_queries(packed_ref[0, rows, :PAIR])
        inner = slice(start % span, start % span + BLOCK)
        grads = stack_grads(grad_ref[start // span, 0, inner, :])
        log_total = jnp.concatenate([lse_ref[0, 0, 0:1, rows], lse_ref[0, 0, 1:2, rows]], 1)

        def piece(keys):
            scores = dot_nt(keys, queries)
            probs = jnp.exp(scores - log_total)
            return (probs, dot_nt(keys, grads))

        inside = packed_ref[0, rows, PAIR:]
        probs_inside, grad_inside = piece(inside)
        probs_inside = jnp.where(allowed, probs_inside, 0.0)
        delta = jnp.sum(probs_inside * grad_inside, 0, keepdims=True)
        if start:
            before = packed_ref[0, :start, PAIR:]
            probs_before, grad_before = piece(before)
            delta = delta + jnp.sum(probs_before * grad_before, 0, keepdims=True)
        score_grads = (probs_inside * (grad_inside - delta)).astype(jnp.bfloat16)
        total_ref[rows, :] += dot_nn(probs_inside.astype(jnp.bfloat16), grads) + dot_nn(
            score_grads, queries
        )
        grad_query = dot_tn(score_grads, inside)
        if start:
            score_grads = (probs_before * (grad_before - delta)).astype(jnp.bfloat16)
            total_ref[:start, :] += dot_nn(probs_before.astype(jnp.bfloat16), grads) + dot_nn(
                score_grads, queries
            )
            grad_query = grad_query + dot_tn(score_grads, before)
        grad_query = (
            jnp.where(low, grad_query[:BLOCK], pltpu.roll(grad_query[BLOCK:], HEAD_SIZE, 1)) * SCALE
        )
        out_ref[start // span, 0, inner, :PAIR] = unturn(grad_query, slice(0, PAIR), rows)
    for start in range(0, length, BLOCK):
        rows = slice(start, start + BLOCK)
        inner = slice(start % span, start % span + BLOCK)
        out_ref[start // span, 0, inner, PAIR:] = unturn(
            total_ref[rows, :], slice(PAIR, GROUP), rows
        )


def attention_backward(packed, lse, grads, tables, groups_local):
    slots, length = packed.shape[:2]
    pieces, span = grads.shape[0], grads.shape[2]
    return pl.pallas_call(
        attention_backward_kernel,
        grid=(slots, groups_local),
        in_specs=[
            pl.BlockSpec((1, length, GROUP), lambda s, g: (s, 0, g)),
            pl.BlockSpec((1, 1, 8, length), lambda s, g: (s, g, 0, 0)),
            pl.BlockSpec((pieces, 1, span, PAIR), lambda s, g: (0, s, 0, g)),
            pl.BlockSpec((length, GROUP), lambda s, g: (0, 0)),
            pl.BlockSpec((length, GROUP), lambda s, g: (0, 0)),
        ],
        out_specs=pl.BlockSpec((pieces, 1, span, GROUP), lambda s, g: (0, s, 0, g)),
        out_shape=jax.ShapeDtypeStruct((pieces, slots, span, packed.shape[2]), jnp.bfloat16),
        scratch_shapes=[pltpu.VMEM((length, PAIR), jnp.float32)],
        compiler_params=pltpu.CompilerParams(vmem_limit_bytes=VMEM_BYTES),
        cost_estimate=SHORT,
        name="attention_backward",
    )(packed, lse, grads, *tables)


def expert_kernel(sources, n_local, kept, ids_ref, *refs):
    xs, refs = refs[:sources], refs[sources:]
    gs, refs = refs[:sources], refs[sources:]
    w_in_ref, w_out_ref = refs[:2]
    refs = refs[2 + kept :]
    buffer_ref, grad_out_ref, hidden_ref, grad_pre_ref = refs[:4]
    backs, mixes = refs[4 : 4 + sources], refs[4 + sources : 4 + 2 * sources]
    table, picks, mix_rows, back_rows, gate_back = refs[4 + 2 * sources :]
    step = pl.program_id(0)
    expert = ids_ref[step]
    tokens = xs[0].shape[0]
    here = pl.ds(pl.multiple_of(step * CAP, 16), CAP)

    @pl.when(step == 0)
    def _():
        for s in range(sources):
            table[s] = xs[s][:, D:].astype(jnp.float32).T
            gate_back[s] = jnp.zeros((TAIL, tokens), jnp.float32)

    place = lax.broadcasted_iota(jnp.int32, (CAP, tokens), 0).astype(jnp.float32)
    hits, gate_rows, grad_rows = [], [], []
    for s in range(sources):
        code = table[s, pl.ds(expert, 1), :]
        gate = table[s, pl.ds(expert + E, 1), :] + table[s, pl.ds(expert + 2 * E, 1), :]
        hit = code == place
        pick = jnp.where(hit, 1.0, 0.0).astype(jnp.bfloat16)
        picks[s, here, :] = pick
        hits.append(hit)
        gate_rows.append(jnp.sum(jnp.where(hit, gate, 0.0), 1, keepdims=True))
        buffer_ref[0, 0, s * CAP : (s + 1) * CAP, :] = dot_nn(pick, xs[s][:, :D]).astype(
            jnp.bfloat16
        )
        grad_rows.append(dot_nn(pick, gs[s][...]))
    gate_row = jnp.concatenate(gate_rows, 0)
    grad_row = jnp.concatenate(grad_rows, 0)
    grad_out_ref[0, 0] = (gate_row * grad_row).astype(jnp.bfloat16)
    pre = dot_nn(buffer_ref[0, 0], w_in_ref[0])
    grad_plain = dot_nn(grad_row.astype(jnp.bfloat16), w_out_ref[0])
    gate_pre, up_pre = pre[:, :FFE], pre[:, FFE:]
    sigmoid_gate = 1.0 / (1.0 + jnp.exp(-gate_pre))
    silu_gate = gate_pre * sigmoid_gate
    hidden = (silu_gate * up_pre).astype(jnp.bfloat16)
    hidden_ref[0, 0] = hidden
    gate_grad = jnp.sum(grad_plain * hidden.astype(jnp.float32), 1, keepdims=True)
    grad_hidden = gate_row * grad_plain
    grad_pre_ref[0, 0, :, :FFE] = (
        grad_hidden * up_pre * sigmoid_gate * (1.0 + gate_pre * (1.0 - sigmoid_gate))
    ).astype(jnp.bfloat16)
    grad_pre_ref[0, 0, :, FFE:] = (grad_hidden * silu_gate).astype(jnp.bfloat16)
    outputs = (gate_row * dot_nt(hidden, w_out_ref[0])).astype(jnp.bfloat16)
    back = dot_nt(grad_pre_ref[0, 0], w_in_ref[0]).astype(jnp.bfloat16)
    for s in range(sources):
        part = slice(s * CAP, (s + 1) * CAP)
        mix_rows[s, here, :] = outputs[part]
        back_rows[s, here, :] = back[part]
        row = jnp.sum(jnp.where(hits[s], gate_grad[part], 0.0), 0, keepdims=True)
        high = row.astype(jnp.bfloat16).astype(jnp.float32)
        gate_back[s, pl.ds(expert, 1), :] = high
        gate_back[s, pl.ds(expert + E, 1), :] = row - high

    @pl.when(step == n_local - 1)
    def _():
        for s in range(sources):
            backs[s][:, :D] = dot_tn(picks[s], back_rows[s]).astype(jnp.bfloat16)
            backs[s][:, D:] = gate_back[s].T.astype(jnp.bfloat16)
            mixes[s][...] = dot_tn(picks[s], mix_rows[s]).astype(jnp.bfloat16)


def experts(chunk, chunks, ids, xs, gs, own_in, own_out, kept):
    sources, n_local, tokens = len(xs), own_in.shape[0], xs[0].shape[0]
    rows = sources * CAP
    bf16, f32 = jnp.bfloat16, jnp.float32
    fixed = lambda i, ids: (0, 0)
    saved = lambda columns: pl.BlockSpec((1, 1, rows, columns), lambda i, ids: (i, chunk, 0, 0))
    widths = (D, D, FFE, 2 * FFE)
    in_specs = (
        [pl.BlockSpec((tokens, D + TAIL), fixed)] * sources
        + [pl.BlockSpec((tokens, D), fixed)] * sources
        + [
            pl.BlockSpec((1, D, 2 * FFE), lambda i, ids: (i, 0, 0)),
            pl.BlockSpec((1, D, FFE), lambda i, ids: (i, 0, 0)),
        ]
        + [pl.BlockSpec(memory_space=pl.ANY)] * len(kept)
    )
    results = pl.pallas_call(
        functools.partial(expert_kernel, sources, n_local, len(kept)),
        grid_spec=pltpu.PrefetchScalarGridSpec(
            num_scalar_prefetch=1,
            grid=(n_local,),
            in_specs=in_specs,
            out_specs=[saved(columns) for columns in widths]
            + [pl.BlockSpec((tokens, D + TAIL), fixed)] * sources
            + [pl.BlockSpec((tokens, D), fixed)] * sources,
            scratch_shapes=[
                pltpu.VMEM((sources, TAIL, tokens), f32),
                pltpu.VMEM((sources, n_local * CAP, tokens), bf16),
                pltpu.VMEM((sources, n_local * CAP, D), bf16),
                pltpu.VMEM((sources, n_local * CAP, D), bf16),
                pltpu.VMEM((sources, TAIL, tokens), f32),
            ],
        ),
        out_shape=[
            jax.ShapeDtypeStruct((n_local, chunks, rows, columns), bf16) for columns in widths
        ]
        + [jax.ShapeDtypeStruct((tokens, D + TAIL), bf16)] * sources
        + [jax.ShapeDtypeStruct((tokens, D), bf16)] * sources,
        input_output_aliases={3 + 2 * sources + i: i for i in range(len(kept))},
        compiler_params=pltpu.CompilerParams(vmem_limit_bytes=VMEM_BYTES),
        cost_estimate=pl.CostEstimate(
            flops=4 * n_local * rows * D * (4 * tokens + 9 * FFE),
            bytes_accessed=n_local * D * FFE * 6 + tokens * sources * D * 8,
            transcendentals=0,
        ),
        name="experts",
    )(ids, *xs, *gs, own_in, own_out, *kept)
    return results[:4], results[4 : 4 + sources], results[4 + sources :]


def cut_rows_kernel(extra, left_ref, right_ref, *refs):
    out_ref = refs[-1]
    parts, rows = out_ref.shape[0], out_ref.shape[2]
    width = right_ref.shape[1]
    product = dot_tn(left_ref[...], right_ref[...])
    out_ref[:, 0, :, :width] = product.reshape(parts, rows, width).astype(out_ref.dtype)
    if extra:
        normed_ref, logits_ref, gain_ref = refs[:3]
        rest = logits_ref[...]
        tail = jnp.zeros((left_ref.shape[1], TAIL), jnp.float32)
        for _ in range(3):
            term = rest.astype(jnp.bfloat16)
            rest = rest - term.astype(jnp.float32)
            tail = tail + dot_tn(normed_ref[...], term)
        lane = lax.broadcasted_iota(jnp.int32, tail.shape, 1)
        tail = jnp.where(lane == E, gain_ref[...], tail)
        out_ref[:, 0, :, width:] = tail.reshape(parts, rows, TAIL).astype(out_ref.dtype)


def cut_rows(left, right, n_heads, parts, extra=()):
    depth, height = left.shape
    each = height // n_heads
    width = right.shape[1]
    columns = width + (TAIL if extra else 0)
    extra_specs = (
        [
            pl.BlockSpec((depth, each), lambda h: (0, h)),
            pl.BlockSpec((depth, TAIL), lambda h: (0, 0)),
            pl.BlockSpec((each, 1), lambda h: (h, 0)),
        ]
        if extra
        else []
    )
    return pl.pallas_call(
        functools.partial(cut_rows_kernel, bool(extra)),
        grid=(n_heads,),
        in_specs=[
            pl.BlockSpec((depth, each), lambda h: (0, h)),
            pl.BlockSpec((depth, width), lambda h: (0, 0)),
        ]
        + extra_specs,
        out_specs=pl.BlockSpec((parts, 1, each // parts, columns), lambda h: (0, h, 0, 0)),
        out_shape=jax.ShapeDtypeStruct(
            (parts, n_heads, each // parts, columns),
            jnp.bfloat16 if each // parts % 16 == 0 else jnp.float32,
        ),
        compiler_params=pltpu.CompilerParams(vmem_limit_bytes=VMEM_BYTES),
        cost_estimate=pl.CostEstimate(
            flops=4 * depth * height * columns,
            bytes_accessed=depth * (height + width) * 2 + height * columns * 4,
            transcendentals=0,
        ),
        name="cut_rows",
    )(left, right, *extra)


def expert_grads_kernel(order_ref, left_ref, right_ref, own_ref, *others):
    product = dot_tn(left_ref[0], right_ref[0])
    step = pl.program_id(0)

    @pl.when(step == 0)
    def _():
        own_ref[...] = product

    for at, other in enumerate(others):

        @pl.when(step == at + 1)
        def _():
            other[...] = product.astype(jnp.bfloat16)


def expert_grads(order, left, right):
    count, depth, height = left.shape
    width = right.shape[2]
    return pl.pallas_call(
        expert_grads_kernel,
        grid_spec=pltpu.PrefetchScalarGridSpec(
            num_scalar_prefetch=1,
            grid=(count,),
            in_specs=[
                pl.BlockSpec((1, depth, height), lambda i, order: (order[i], 0, 0)),
                pl.BlockSpec((1, depth, width), lambda i, order: (order[i], 0, 0)),
            ],
            out_specs=[pl.BlockSpec((height, width), lambda i, order: (0, 0))] * count,
        ),
        out_shape=[jax.ShapeDtypeStruct((height, width), jnp.float32)]
        + [jax.ShapeDtypeStruct((height, width), jnp.bfloat16)] * (count - 1),
        compiler_params=pltpu.CompilerParams(vmem_limit_bytes=VMEM_BYTES),
        cost_estimate=pl.CostEstimate(
            flops=4 * count * depth * height * width,
            bytes_accessed=2 * count * depth * (height + width) + height * width * (2 * count + 2),
            transcendentals=0,
        ),
        name="expert_grads",
    )(order, left, right)


def plain_grads_kernel(left_ref, right_ref, out_ref):
    out_ref[0] = dot_tn(left_ref[0], right_ref[0]).astype(out_ref.dtype)


def plain_grads(left, right):
    count, depth, height = left.shape
    width = right.shape[2]
    return pl.pallas_call(
        plain_grads_kernel,
        grid=(count,),
        in_specs=[
            pl.BlockSpec((1, depth, height), lambda i: (i, 0, 0)),
            pl.BlockSpec((1, depth, width), lambda i: (i, 0, 0)),
        ],
        out_specs=pl.BlockSpec((1, height, width), lambda i: (i, 0, 0)),
        out_shape=jax.ShapeDtypeStruct((count, height, width), jnp.bfloat16),
        compiler_params=pltpu.CompilerParams(vmem_limit_bytes=VMEM_BYTES),
        cost_estimate=pl.CostEstimate(
            flops=4 * count * depth * height * width,
            bytes_accessed=2 * count * (depth * (height + width) + height * width),
            transcendentals=0,
        ),
        name="plain_grads",
    )(left, right)


def make_local(n_heads, chip, core):
    everyone = ("heads", "chip", "core")
    group_size = n_heads * core
    n_local = E // group_size
    groups_local = KEY_VALUE_HEADS // n_heads
    ring = [(i, (i + 1) % n_heads) for i in range(n_heads)]
    crossed = [(i, core - 1 - i) for i in range(core)]

    def onward(value):
        return lax.ppermute(value, "heads", ring)

    def across(value):
        return lax.ppermute(value, "core", crossed)

    def around(value):
        values = [value]
        for _ in range(n_heads - 1):
            values.append(onward(values[-1]))
        return values

    def both(value):
        return [value] if core == 1 else [value, across(value)]

    def joined(parts):
        total = parts[0].astype(jnp.float32)
        if core > 1:
            total = total + across(parts[1]).astype(jnp.float32)
        return total

    def after(value, *others):
        return lax.optimization_barrier((value,) + others)[0]

    def paired(value, other):
        return lax.ppermute(value, "chip", [(i, i ^ other) for i in range(chip)])

    def spread_rows(cut):
        part = lax.psum_scatter(
            cut.reshape(-1, cut.shape[3]), ("chip", "core"), scatter_dimension=0, tiled=True
        )
        return part.reshape(cut.shape[1:])

    def local(
        tokens,
        cotangent,
        lengths,
        routes,
        attention_input_weight,
        attn_out,
        router,
        gain_attn,
        gain_ffn,
        expert_in,
        expert_out,
    ):
        slots, span, width = tokens.shape
        token_rows = slots * span
        length = span * n_heads
        rank = lax.axis_index("heads")
        qkv_width = attention_input_weight.shape[1]
        own_columns = groups_local * GROUP
        rings = around(tokens)
        small = jnp.concatenate(
            [
                attention_input_weight,
                attn_out,
                router,
                gain_attn[:, None],
                gain_ffn[:, None],
                jnp.zeros((router.shape[0], TAIL - E - 2), jnp.bfloat16),
            ],
            1,
        )
        column = lax.all_to_all(
            jnp.broadcast_to(after(small, rings[1])[None], (n_heads,) + small.shape),
            "heads",
            split_axis=0,
            concat_axis=0,
            tiled=True,
        )

        own_out = lax.all_gather(expert_out, "chip", axis=0, tiled=True).reshape(n_local, D, FFE)

        def plane(value):
            value = lax.all_gather(value, ("chip", "core"), axis=1, tiled=True)
            return value.reshape(-1, value.shape[2])

        first = plane(
            after(
                jnp.concatenate(
                    [
                        lax.dynamic_slice_in_dim(column, rank * own_columns, own_columns, 2),
                        column[:, :, qkv_width + D :],
                    ],
                    2,
                ),
                own_out,
                rings[2],
            )
        )
        w_own = first
        gain_one = first[:, own_columns + E].astype(jnp.float32)
        w_proj = plane(column[:, :, qkv_width:])
        w_router = w_proj[:, D : D + E]
        gain_two = w_proj[:, D + E + 1].astype(jnp.float32)
        w_proj = w_proj[:, :D]
        own_grads = cotangent.reshape(token_rows, width)
        own_in = lax.all_gather(after(expert_in, first, rings[-1]), "chip", axis=0, tiled=True).reshape(
            n_local, D, 2 * FFE
        )

        positions = rank * span + jnp.arange(span, dtype=jnp.int32)
        valid = (positions[None, :] < lengths[:, None]).reshape(token_rows)
        valid_float = valid.astype(jnp.float32)[:, None]
        route_rows = routes.reshape(token_rows, TOPK)
        routed = jnp.any(
            route_rows[:, :, None] == jnp.arange(E, dtype=jnp.int32)[None, None, :], 1
        )
        live = (routed & valid[:, None]).astype(jnp.bfloat16)
        earlier = (
            jnp.arange(token_rows)[:, None] > jnp.arange(token_rows)[None, :]
        ).astype(jnp.bfloat16)
        count = jnp.dot(earlier, live, preferred_element_type=jnp.float32)
        kept = (live > 0) & (count < CAP)
        code = jnp.where(kept, count, -1.0).astype(jnp.bfloat16)
        ids = (rank * n_local + jnp.arange(n_local, dtype=jnp.int32)) * core + lax.axis_index("core")

        tables = rotary_tables(length)
        places = (rank + n_heads - jnp.arange(n_heads, dtype=jnp.int32)) % n_heads
        packed, context_heads, lse, normed_whole = attention_forward(
            rings, places, gain_one[None, :], w_own, tables, groups_local
        )
        grad_ring = [own_grads, onward(after(own_grads, rings[-1]))]
        context_heads = after(context_heads, grad_ring[1])
        context = lax.all_to_all(context_heads, "heads", split_axis=0, concat_axis=0, tiled=True)
        grad_ring.append(onward(after(grad_ring[1], context)))
        heads_width = groups_local * PAIR
        context = context.reshape(n_heads, token_rows, heads_width)

        state = tokens.astype(jnp.float32).reshape(token_rows, width)
        mid_state = state
        for h in range(n_heads):
            mid_state = mid_state + dot_nn(
                context[h], w_proj[h * heads_width : (h + 1) * heads_width]
            )
        factor_two = norm_factor(mid_state)
        normed_ffn = (mid_state * factor_two * gain_two).astype(jnp.bfloat16)
        logits = jnp.dot(normed_ffn, w_router, preferred_element_type=jnp.float32)
        highest = jnp.max(jnp.where(routed, logits, NEGATIVE), -1, keepdims=True)
        weights = jnp.where(routed, jnp.exp(jnp.where(routed, logits - highest, 0.0)), 0.0)
        gates = weights / jnp.sum(weights, -1, keepdims=True)
        gates_high = lax.reduce_precision(gates, 8, 7)
        payload = jnp.concatenate(
            [
                normed_ffn,
                code,
                gates_high.astype(jnp.bfloat16),
                (gates - gates_high).astype(jnp.bfloat16),
                jnp.zeros((token_rows, TAIL - 3 * E), jnp.bfloat16),
            ],
            1,
        )
        payloads = around(after(payload, grad_ring[2]))
        for step in range(2, n_heads - 1):
            grad_ring.append(onward(after(grad_ring[-1], payloads[1])))
        saved, backs, mixes, moving = (), [], [], None
        for step, value in enumerate(payloads):
            xs, gs = both(value), both(grad_ring[step])
            ahead = min(step + 1, n_heads - 1)
            if step:
                xs[0] = after(xs[0], payloads[ahead], grad_ring[min(step + 2, n_heads - 1)])
            if moving is not None:
                xs[0] = after(xs[0], moving)
            saved, back, mix = experts(
                step, n_heads, ids, xs, gs, own_in, own_out, tuple(saved)
            )
            backs.append(back)
            mixes.append(mix)
            if step:
                total = joined(back)
                if moving is not None:
                    total = total + onward(moving).astype(jnp.float32)
                moving = total.astype(jnp.bfloat16)
        buffer, grad_outputs, hidden, grad_pre = [
            value.reshape(n_local, group_size * CAP, value.shape[3]) for value in saved
        ]
        hidden = after(hidden, moving)
        last_back = onward(moving)
        grad_pre = after(grad_pre, last_back)
        if expert_in.shape[0] == D:
            order = lax.axis_index("chip") ^ jnp.arange(chip, dtype=jnp.int32)
            parts_in = expert_grads(order, buffer, grad_pre)
        else:
            parts_in = [plain_grads(buffer, grad_pre)]
        parts_out = plain_grads(grad_outputs, hidden)
        grad_expert_out = lax.psum_scatter(
            parts_out.reshape(-1, FFE), "chip", scatter_dimension=0, tiled=True
        ).astype(jnp.float32)
        w_qkv = plane(after(column[:, :, :qkv_width], context))
        mix_moving = joined(mixes[1]).astype(jnp.bfloat16)
        mix_received = onward(after(mix_moving, last_back))
        back_sum = joined(backs[0]) + after(last_back, w_qkv, parts_out, *parts_in).astype(jnp.float32)

        grad_gates = back_sum[:, width : width + E] + back_sum[:, width + E : width + 2 * E]
        grad_logits = gates * (grad_gates - jnp.sum(gates * grad_gates, -1, keepdims=True))
        grad_logits = grad_logits * valid_float
        grad_out = cotangent.astype(jnp.float32).reshape(token_rows, width) * valid_float
        grad_normed_ffn = back_sum[:, :width] + jnp.dot(
            grad_logits, w_router.astype(jnp.float32).T, precision=TOP_PRECISION
        )
        grad_mid_norm, gain_two_term = norm_back(grad_normed_ffn, mid_state, factor_two, gain_two)
        grad_mid = grad_out + grad_mid_norm
        grad_mid_low = grad_mid.astype(jnp.bfloat16)
        context_gradient = jnp.stack(
            [
                dot_nt(grad_mid_low, w_proj[h * heads_width : (h + 1) * heads_width])
                for h in range(n_heads)
            ]
        ).astype(jnp.bfloat16)
        context_gradient = after(context_gradient, mix_received)
        grad_context_heads = lax.all_to_all(
            context_gradient.reshape(n_heads, slots, span, heads_width),
            "heads",
            split_axis=0,
            concat_axis=0,
            tiled=True,
        )
        logits_padded = jnp.concatenate(
            [grad_logits, jnp.zeros((token_rows, TAIL - E), jnp.float32)], 1
        )
        second = cut_rows(
            jnp.concatenate([context[h] for h in range(n_heads)], 1),
            after(grad_mid_low, context_gradient),
            n_heads,
            chip * core,
            (normed_ffn, logits_padded, gain_two_term[:, None]),
        )
        grad_context_heads = after(grad_context_heads, second)
        second = spread_rows(second)

        grad_before = None
        for chunk in range(2, n_heads):
            mix_moving = (joined(mixes[chunk]) + mix_received.astype(jnp.float32)).astype(
                jnp.bfloat16
            )
            if chunk == 2:
                grad_before = attention_backward(
                    packed, lse, after(grad_context_heads, mix_moving), tables, groups_local
                )
            if chunk < n_heads - 1:
                mix_received = onward(after(mix_moving, grad_context_heads))
        received = []
        if len(parts_in) > 1:
            received = [paired(parts_in[1], 1), paired(parts_in[2], 2)]
        grad_before = after(grad_before, mix_moving, grad_expert_out, *received)
        grad_mine = lax.all_to_all(
            grad_before, "heads", split_axis=0, concat_axis=0, tiled=True
        ).reshape(n_heads, token_rows, own_columns)
        qkv_part = spread_rows(
            cut_rows(
                normed_whole.reshape(-1, width),
                grad_before.reshape(-1, own_columns),
                n_heads,
                chip * core,
            )
        )
        if received:
            received.append(paired(after(parts_in[3], *received), 3))
        else:
            grad_expert_in = lax.psum_scatter(
                parts_in[0].reshape(-1, 2 * FFE), "chip", scatter_dimension=0, tiled=True
            ).astype(jnp.float32)
        grad_normed_attn = dot_nt(grad_mine[0], w_qkv[:, :own_columns])
        for h in range(1, n_heads):
            grad_normed_attn = grad_normed_attn + dot_nt(
                grad_mine[h], w_qkv[:, h * own_columns : (h + 1) * own_columns]
            )
        grad_state_norm, _ = norm_back(grad_normed_attn, state, norm_factor(state), gain_one)
        grad_tokens = (grad_mid + grad_state_norm).astype(jnp.bfloat16).reshape(tokens.shape)
        if received:
            received[-1] = after(received[-1], grad_tokens)
            grad_expert_in = parts_in[0]
            for value in received:
                grad_expert_in = grad_expert_in + value.astype(jnp.float32)
        mixture = joined(mixes[0]) + onward(after(mix_moving, grad_mine)).astype(jnp.float32)
        mixed = (valid_float * (mid_state + mixture)).astype(jnp.bfloat16)

        last = lax.all_to_all(
            after(jnp.concatenate([second, qkv_part], 2), grad_mine),
            "heads",
            split_axis=0,
            concat_axis=0,
            tiled=True,
        ).astype(jnp.float32)
        second = jnp.sum(last[:, :, : D + TAIL], 0)
        grad_attn_out = second[:, :D]
        grad_router = second[:, D : D + E]
        grad_gain_ffn = second[:, D + E]
        grad_attn_in = jnp.concatenate([last[h, :, D + TAIL :] for h in range(n_heads)], 1)
        grad_gain_attn = jnp.sum(
            grad_attn_in * attention_input_weight.astype(jnp.float32), -1
        ) / gain_attn.astype(jnp.float32)
        return (
            mixed.reshape(tokens.shape),
            grad_tokens,
            grad_attn_in,
            grad_attn_out,
            grad_router,
            grad_gain_attn,
            grad_gain_ffn,
            grad_expert_in,
            grad_expert_out,
        )

    return local


def solution(mesh):
    n_heads, n_shard = mesh.shape["heads"], mesh.shape["shard"]
    core = 2 if n_heads * n_shard == E else 1
    chip = n_shard // core
    split = jax.sharding.Mesh(
        mesh.devices.reshape(n_heads, chip, core), ("heads", "chip", "core")
    )
    shard = ("chip", "core")
    everyone = ("heads", "chip", "core")
    token_spec = P(shard, "heads", None)
    rows = P(everyone, None)
    in_specs = (
        token_spec,
        token_spec,
        P(shard),
        token_spec,
        rows,
        rows,
        rows,
        P(everyone),
        P(everyone),
        rows,
        rows,
    )
    out_specs = (token_spec, token_spec, rows, rows, rows, P(everyone), P(everyone), rows, rows)
    return jax.shard_map(
        make_local(n_heads, chip, core),
        mesh=split,
        in_specs=in_specs,
        out_specs=out_specs,
        check_vma=False,
    )
```

time: 1370 us -> 643 us (0.47)
  waiting for transfers between devices: 786 us -> 321 us
  matrix products: 282 us -> 11.9 us
  Pallas kernels: 0 us -> 178 us
  local copies, waits for them, and re-layouts: 104 us -> 22.2 us
  blocking collectives: 53.8 us -> 0 us
  other arithmetic: 94.2 us -> 46.8 us
  starting transfers between devices: 17.6 us -> 39.1 us
    reduce_scatter x5 -> x3, waiting for transfers between devices: 370 us -> 40 us  [the longest x2 40 us: spread_rows(): lax.psum_scatter(cut.reshape(-1, cut.shape[3]), ('chip', 'core'), scatter...]
    dot_general x57 -> x13, matrix products: 277 us -> 9.22 us  [the longest x8 5.26 us: dot_nt(): lax.dot_general(left, right, (((1,), (1,)), ((), ())), preferred_element_...]
    all_gather x5 -> x4, waiting for transfers between devices: 264 us -> 0.03 us  [the longest x1 0.02 us: local(): lax.all_gather(after(expert_in, first, rings[-1]), 'chip', axis=0, tiled=...]
    ppermute x0 -> x34, waiting for transfers between devices: none -> 194 us  [the longest x15 179 us: onward(): return lax.ppermute(value, 'heads', ring)]
    pallas_call x0 -> x10, Pallas kernels: none -> 178 us  [the longest x4 93.8 us: experts(): pl.pallas_call(functools.partial(expert_kernel, sources, n_local, len(kep...]
    all_to_all x1 -> x0, blocking collectives: 53.8 us -> none  [local(): lax.all_to_all(context_heads, 'heads', split_axis=1, concat_axis=2, tiled...]
    all_gather x1, waiting for transfers between devices: 46.8 us -> 0.01 us  [local(): lax.all_gather(expert_out, 'chip', axis=0, tiled=True)]
    reduce_sum x7 -> x2, other arithmetic: 19 us -> 0.27 us  [the longest x1 0.24 us: local(): gates = weights / jnp.sum(weights, -1, keepdims=True)]
  transfers between devices with their start and end apart: 16 -> 47, of which waited for: 14 -> 20; matrix products, arithmetic and copies ran while one was open for 19% -> 11% of each run, Pallas kernels for 0% -> 28%
where the time goes in v2:
time: 643 us; the launch traced here: 634 us
  waiting for transfers between devices  321 us (50%)
  Pallas kernels  178 us (28%)
  other arithmetic  46.8 us (7%)
  starting transfers between devices  39.1 us (6%)
  local copies, waits for them, and re-layouts  22.2 us (3%)
  between operations  15.1 us (2%)
  matrix products  11.9 us (2%)
    ppermute x15, waiting for transfers between devices, onward(): return lax.ppermute(value, 'heads', ring)  179 us
    pallas_call x4, Pallas kernels, experts(): pl.pallas_call(functools.partial(expert_kernel, sources, n_local, len(kep...  93.8 us
    all_to_all x1, waiting for transfers between devices, local(): lax.all_to_all(jnp.broadcast_to(after(small, rings[1])[None], (n_heads,)...  41 us
    reduce_scatter x2, waiting for transfers between devices, spread_rows(): lax.psum_scatter(cut.reshape(-1, cut.shape[3]), ('chip', 'core'), scatter...  40 us
    pallas_call x1, Pallas kernels, attention_backward(): pl.pallas_call(attention_backward_kernel, grid=(slots, groups_local), in_...  21.2 us
    all_to_all x1, waiting for transfers between devices, local(): lax.all_to_all(context_heads, 'heads', split_axis=0, concat_axis=0, tiled...  20.6 us
    pallas_call x1, Pallas kernels, attention_forward(): pl.pallas_call(functools.partial(attention_forward_kernel, pieces), grid_...  20.5 us
    pallas_call x1, Pallas kernels, expert_grads(): pl.pallas_call(expert_grads_kernel, grid_spec=pltpu.PrefetchScalarGridSpe...  20.1 us
  transfers between devices with their start and end apart: 47, of which 20 were waited for; matrix products, arithmetic and copies ran while one was open for 11% of the time, Pallas kernels for 28%

profile of v2, /device:TPU:0, one launch (start us, length us, event | category | flops | bytes accessed | tf_op | source)
XLA Modules:
  0.0 634.3 jit_solution(1339029716361734524)
XLA Ops:
  13.5 22.9 %collective-permute-done.refs_1_ = bf16[2,256,1024]{2,1,0:T(8,128)(2,1)S(1)} collective-permute-done((bf16[2,256,1024]{2,1,0:T(8,128)(2,1)}, bf16[2,256,1024]{2,1,0:T(8,128)(2,1)S(1)}, u32[]{:S(2)}, u32[]{:S(2)}) %collective-permute-start) | collective-permute-done | bytes 1048608 | tf_op jit(solution)/shard_map/ppermute | solution.py:526
  42.9 41.0 %all-to-all-done = bf16[4,32,3200]{2,1,0:T(8,128)(2,1)S(1)} async-done(((bf16[4,32,3200]{2,1,0:T(8,128)(2,1)}), bf16[4,32,3200]{2,1,0:T(8,128)(2,1)S(1)}, u32[]{:S(2)}, u32[]{:S(2)}) %all-to-all-start) | async-done | bytes 819232 | tf_op jit(solution)/shard_map/all_to_all | solution.py:589
  85.7 25.9 %collective-permute-done.2.refs_3_ = bf16[2,256,1024]{2,1,0:T(8,128)(2,1)S(1)} collective-permute-done((bf16[2,256,1024]{2,1,0:T(8,128)(2,1)S(1)}, bf16[2,256,1024]{2,1,0:T(8,128)(2,1)S(1)}, u32[]{:S(2)}, u32[]{:S(2)}) %collective-permute-start.2) | collective-permute-done | bytes 1048608 | tf_op jit(solution)/shard_map/ppermute | solution.py:526
  114.1 20.5 %attention_forward.1 = (bf16[2,1024,512]{2,1,0:T(8,128)(2,1)}, bf16[4,2,256,256]{3,2,1,0:T(8,128)(2,1)}, f32[2,2,8,1024]{3,2,1,0:T(8,128)}, bf16[4,2,256,1024]{3,2,1,0:T(8,128)(2,1)}) custom-call(s32[4]{0:T(128)} %and_select_fusion.place_ref, bf16[2,256,1024]{2,1,0:T(8,128)(2,1)} %refs_0_.1, bf16[2,256,1024]{2,1,0:T(8,128)(2,1)} %copy-done.21, ...), custom_call_target="tpu_custom_call" | custom-call | flops 1024 | bytes 1024 | tf_op jit(solution)/shard_map/attention_forward/pallas_call | solution.py:165
  143.2 20.6 %all-to-all-done.1 = bf16[4,2,256,256]{3,2,1,0:T(8,128)(2,1)S(1)} async-done(((bf16[4,2,256,256]{3,2,1,0:T(8,128)(2,1)}), bf16[4,2,256,256]{3,2,1,0:T(8,128)(2,1)S(1)}, u32[]{:S(2)}, u32[]{:S(2)}) %all-to-all-start.1) | async-done | bytes 1048608 | tf_op jit(solution)/shard_map/all_to_all | solution.py:650
  173.4 16.7 %collective-permute-done.4.refs_2_ = bf16[512,1024]{1,0:T(8,128)(2,1)} collective-permute-done((bf16[512,1024]{1,0:T(8,128)(2,1)}, bf16[512,1024]{1,0:T(8,128)(2,1)}, u32[]{:S(2)}, u32[]{:S(2)}) %collective-permute-start.4) | collective-permute-done | bytes 1048608 | tf_op jit(solution)/shard_map/ppermute | solution.py:526
  190.0 27.9 %collective-permute-done.8.refs_0_ = bf16[512,1152]{1,0:T(8,128)(2,1)} collective-permute-done((bf16[512,1152]{1,0:T(8,128)(2,1)S(1)}, bf16[512,1152]{1,0:T(8,128)(2,1)}, u32[]{:S(2)}, u32[]{:S(2)}) %collective-permute-start.8) | collective-permute-done | bytes 1179680 | tf_op jit(solution)/shard_map/ppermute | solution.py:526
  219.0 48.4 %collective-permute-done.11.refs_2_ = bf16[512,1024]{1,0:T(8,128)(2,1)S(1)} collective-permute-done((bf16[512,1024]{1,0:T(8,128)(2,1)}, bf16[512,1024]{1,0:T(8,128)(2,1)S(1)}, u32[]{:S(2)}, u32[]{:S(2)}) %collective-permute-start.11) | collective-permute-done | bytes 1048608 | tf_op jit(solution)/shard_map/ppermute | solution.py:526
  268.2 23.5 %experts.4 = (bf16[4,4,320,1024]{3,2,1,0:T(8,128)(2,1)}, bf16[4,4,320,1024]{3,2,1,0:T(8,128)(2,1)}, bf16[4,4,320,512]{3,2,1,0:T(8,128)(2,1)}, bf16[4,4,320,1024]...) custom-call(s32[4]{0:T(128)} %multiply_add_fusion.1.ids_ref, ...), custom_call_target="tpu_custom_call" | custom-call | flops 34896609280 | bytes 20971520 | tf_op jit(solution)/shard_map/experts/pallas_call | solution.py:360
  291.6 23.3 %experts.5 = (bf16[4,4,320,1024]{3,2,1,0:T(8,128)(2,1)}, bf16[4,4,320,1024]{3,2,1,0:T(8,128)(2,1)}, bf16[4,4,320,512]{3,2,1,0:T(8,128)(2,1)}, bf16[4,4,320,1024]...) custom-call(s32[4]{0:T(128)} %multiply_add_fusion.1.ids_ref, ...), custom_call_target="tpu_custom_call", output_to_operand_aliasing={{0}: (7, {}), {1}: (8, {}), {2}: (9, {}), {3}: (10, {})} | custom-call | flops 34896609280 | bytes 20971520 | tf_op jit(solution)/shard_map/experts/pallas_call | solution.py:360
  322.7 23.3 %experts.6 = (bf16[4,4,320,1024]{3,2,1,0:T(8,128)(2,1)}, bf16[4,4,320,1024]{3,2,1,0:T(8,128)(2,1)}, bf16[4,4,320,512]{3,2,1,0:T(8,128)(2,1)}, bf16[4,4,320,1024]...) custom-call(s32[4]{0:T(128)} %multiply_add_fusion.1.ids_ref, ...), custom_call_target="tpu_custom_call", output_to_operand_aliasing={{0}: (7, {}), {1}: (8, {}), {2}: (9, {}), {3}: (10, {})} | custom-call | flops 34896609280 | bytes 20971520 | tf_op jit(solution)/shard_map/experts/pallas_call | solution.py:360
  353.7 23.7 %experts.7 = (bf16[4,4,320,1024]{3,2,1,0:T(8,128)(2,1)}, bf16[4,4,320,1024]{3,2,1,0:T(8,128)(2,1)}, bf16[4,4,320,512]{3,2,1,0:T(8,128)(2,1)}, bf16[4,4,320,1024]...) custom-call(s32[4]{0:T(128)} %multiply_add_fusion.1.ids_ref, ...), custom_call_target="tpu_custom_call", output_to_operand_aliasing={{0}: (7, {}), {1}: (8, {}), {2}: (9, {}), {3}: (10, {})} | custom-call | flops 34896609280 | bytes 20971520 | tf_op jit(solution)/shard_map/experts/pallas_call | solution.py:360
  383.3 10.5 %plain_grads.1 = bf16[4,1024,512]{2,1,0:T(8,128)(2,1)} custom-call(bf16[4,1280,1024]{2,1,0:T(8,128)(2,1)} %bitcast.154, bf16[4,1280,512]{2,1,0:T(8,128)(2,1)} %bitcast.156), custom_call_target="tpu_custom_call" | custom-call | flops 10737418240 | bytes 19922944 | tf_op jit(solution)/shard_map/plain_grads/pallas_call | solution.py:498
  399.5 24.6 %collective-permute-done.26 = bf16[512,1152]{1,0:T(8,128)(2,1)S(1)} collective-permute-done((bf16[512,1152]{1,0:T(8,128)(2,1)S(1)}, bf16[512,1152]{1,0:T(8,128)(2,1)S(1)}, u32[]{:S(2)}, u32[]{:S(2)}) %collective-permute-start.26) | collective-permute-done | bytes 1179680 | tf_op jit(solution)/shard_map/ppermute | solution.py:526
  424.3 20.1 %expert_grads.1 = (f32[1024,1024]{1,0:T(8,128)}, bf16[1024,1024]{1,0:T(8,128)(2,1)}, bf16[1024,1024]{1,0:T(8,128)(2,1)}, bf16[1024,1024]{1,0:T(8,128)(2,1)}) custom-call(s32[4]{0:T(128)} %iota_xor_fusion.order_ref, bf16[4,1280,1024]{2,1,0:T(8,128)(2,1)} %bitcast.153, bf16[4,1280,1024]{2,1,0:T(8,128)(2,1)} %bitcast.155), custom_call_target="tpu_custom_call" | custom-call | flops 21474836480 | bytes 31457280 | tf_op jit(solution)/shard_map/expert_grads/pallas_call | solution.py:468
  463.4 5.8 cut_rows.2
  475.5 9.1 %all-to-all-done.2.grad_ref = bf16[4,2,256,256]{3,2,1,0:T(8,128)(2,1)S(1)} async-done(((bf16[4,2,256,256]{3,2,1,0:T(8,128)(2,1)}), bf16[4,2,256,256]{3,2,1,0:T(8,128)(2,1)S(1)}, u32[]{:S(2)}, u32[]{:S(2)}) %all-to-all-start.2) | async-done | bytes 1048608 | tf_op jit(solution)/shard_map/all_to_all | solution.py:736
  485.7 21.2 %attention_backward.1 = bf16[4,2,256,512]{3,2,1,0:T(8,128)(2,1)} custom-call(bf16[2,1024,512]{2,1,0:T(8,128)(2,1)} %get-tuple-element.134.packed_ref, f32[2,2,8,1024]{3,2,1,0:T(8,128)} %get-tuple-element.135.lse_ref, bf16[4,2,256,256]{3,2,1,0:T(8,128)(2,1)} %copy-done.8, f32[1024,256]{1,0:T(8,128)} %constant.63.clone.refs_6_.own_ref, ...), custom_call_target="tpu_custom_call" | custom-call | flops 1024 | bytes 1024 | tf_op jit(solution)/shard_map/attention_backward/pallas_call | solution.py:257
  516.9 10.3 %collective-permute-done.30 = bf16[1024,1024]{1,0:T(8,128)(2,1)} collective-permute-done((bf16[1024,1024]{1,0:T(8,128)(2,1)}, bf16[1024,1024]{1,0:T(8,128)(2,1)}, u32[]{:S(2)}, u32[]{:S(2)}) %collective-permute-start.30) | collective-permute-done | bytes 2097184 | tf_op jit(solution)/shard_map/ppermute | solution.py:550
  528.2 5.1 all-to-all-start.3
  533.3 6.4 %cut_rows.3 = bf16[8,4,32,512]{3,2,1,0:T(8,128)(2,1)} custom-call(bf16[2048,1024]{1,0:T(8,128)(2,1)} %bitcast.148, bf16[2048,512]{1,0:T(8,128)(2,1)} %bitcast.93), custom_call_target="tpu_custom_call" | custom-call | flops 4294967296 | bytes 8388608 | tf_op jit(solution)/shard_map/cut_rows/pallas_call | solution.py:427
  541.6 40.0 %reduce-scatter.8.cloned.1.call-done = bf16[128,512]{1,0:T(8,128)(2,1)} async-done(((bf16[1024,512]{1,0:T(8,128)(2,1)}), bf16[128,512]{1,0:T(8,128)(2,1)}) %reduce-scatter.8.cloned.1.call-update) | async-done | bytes 131088 | tf_op jit(solution)/shard_map/reduce_scatter | solution.py:553
  598.4 6.5 %convert_add_fusion = f32[1024,1024]{1,0:T(8,128)} fusion(bf16[1024,1024]{1,0:T(8,128)(2,1)} %collective-permute-done.33, bf16[1024,1024]{1,0:T(8,128)(2,1)} %collective-permute-done.31, f32[1024,1024]{1,0:T(8,128)S(1)} %copy-done.7, bf16[1024,1024]{1,0:T(8,128)(2,1)} %collective-permute-done.30), kind=kLoop, calls=%fused_computation | loop fusion | flops 6291456 | bytes 14680064 | tf_op jit(solution)/shard_map/add | solution.py:799
  604.9 14.8 %all-to-all-done.4 = bf16[4,32,1664]{2,1,0:T(8,128)(2,1)} async-done(((bf16[4,32,1664]{2,1,0:T(8,128)(2,1)}), bf16[4,32,1664]{2,1,0:T(8,128)(2,1)}, u32[]{:S(2)}, u32[]{:S(2)}) %all-to-all-start.4) | async-done | bytes 426016 | tf_op jit(solution)/shard_map/all_to_all | solution.py:803
  (255 shorter events, 127.1 us)
Async XLA Ops:
  7.2 77.4 %all-gather.6.cloned.1.call-start = ((), (), s32[]{:S(2)}) async-start(), calls=%async_computation.8 | async-start | bytes 5242880 | tf_op jit(solution)/shard_map/all_gather | solution.py:597
  37.4 46.5 %all-to-all-start = ((bf16[4,32,3200]{2,1,0:T(8,128)(2,1)}), bf16[4,32,3200]{2,1,0:T(8,128)(2,1)S(1)}, u32[]{:S(2)}, u32[]{:S(2)}) async-start(bf16[4,32,3200]{2,1,0:T(8,128)(2,1)} %broadcast_in_dim.24), calls=%async_computation | async-start | bytes 1638400 | tf_op jit(solution)/shard_map/all_to_all | solution.py:589
  40.9 70.6 %all-gather.8.cloned.1.call-start = ((), (), s32[]{:S(2)}) async-start(), calls=%async_computation.9 | async-start | bytes 1474560 | tf_op jit(solution)/shard_map/all_gather | solution.py:600
  41.0 43.6 %collective-permute-start.1 = (bf16[2,256,1024]{2,1,0:T(8,128)(2,1)S(1)}, bf16[2,256,1024]{2,1,0:T(8,128)(2,1)S(1)}, u32[]{:S(2)}, u32[]{:S(2)}) collective-permute-start(bf16[2,256,1024]{2,1,0:T(8,128)(2,1)S(1)} %collective-permute-done.refs_1_), channel_id=1, source_target_pairs={{0,8},{8,16},{16,24},{24,0},{1,9},{9,17},{17,25},{25,1},{2,10},{10... | collective-permute-start | bytes 3145736 | tf_op jit(solution)/shard_map/ppermute | solution.py:526
  84.6 57.3 %all-gather.10.cloned.1.call-start = ((), (), s32[]{:S(2)}) async-start(), calls=%async_computation.10 | async-start | bytes 2654208 | tf_op jit(solution)/shard_map/all_gather | solution.py:600
  85.6 182.6 %all-gather.12.cloned.1.call-start = ((), (), s32[]{:S(2)}) async-start(), calls=%async_computation.11 | async-start | bytes 10485760 | tf_op jit(solution)/shard_map/all_gather | solution.py:623
  140.5 304.0 %all-gather.14.cloned.1.call-start = ((), (), s32[]{:S(2)}) async-start(), calls=%async_computation.12 | async-start | bytes 4718592 | tf_op jit(solution)/shard_map/all_gather | solution.py:600
  217.9 49.6 %collective-permute-start.9 = (bf16[512,1152]{1,0:T(8,128)(2,1)}, bf16[512,1152]{1,0:T(8,128)(2,1)}, u32[]{:S(2)}, u32[]{:S(2)}) collective-permute-start(bf16[512,1152]{1,0:T(8,128)(2,1)} %collective-permute-done.8.refs_0_), channel_id=1, source_target_pairs={{0,8},{8,16},{16,24},{24,0},{1,9},{9,17},{17,25},{25,1},{2,10},{10... | collective-permute-start | bytes 3538952 | tf_op jit(solution)/shard_map/ppermute | solution.py:526
  217.9 50.2 %collective-permute-start.5 = (bf16[512,1152]{1,0:T(8,128)(2,1)S(1)}, bf16[512,1152]{1,0:T(8,128)(2,1)}, u32[]{:S(2)}, u32[]{:S(2)}) collective-permute-start(bf16[512,1152]{1,0:T(8,128)(2,1)S(1)} %concatenate.23.refs_0_), channel_id=1, source_target_pairs={{0,1},{1,0},{2,3},{3,2},{4,5},{5,4},{6,7},{7,6},{8,9},{9,8},{10,11... | collective-permute-start | bytes 3538952 | tf_op jit(solution)/shard_map/ppermute | solution.py:529
  217.9 49.5 %collective-permute-start.11 = (bf16[512,1024]{1,0:T(8,128)(2,1)}, bf16[512,1024]{1,0:T(8,128)(2,1)S(1)}, u32[]{:S(2)}, u32[]{:S(2)}) collective-permute-start(bf16[512,1024]{1,0:T(8,128)(2,1)} %collective-permute-done.4.refs_2_), channel_id=1, source_target_pairs={{0,8},{8,16},{16,24},{24,0},{1,9},{9,17},{17,25},{25,1},{2,10},{10... | collective-permute-start | bytes 3145736 | tf_op jit(solution)/shard_map/ppermute | solution.py:526
  218.0 50.1 %collective-permute-start.6 = (bf16[512,1024]{1,0:T(8,128)(2,1)}, bf16[512,1024]{1,0:T(8,128)(2,1)}, u32[]{:S(2)}, u32[]{:S(2)}) collective-permute-start(bf16[512,1024]{1,0:T(8,128)(2,1)} %bitcast.130), channel_id=1, source_target_pairs={{0,1},{1,0},{2,3},{3,2},{4,5},{5,4},{6,7},{7,6},{8,9},{9,8},{10,11... | collective-permute-start | bytes 3145736 | tf_op jit(solution)/shard_map/ppermute | solution.py:529
  219.0 72.7 %collective-permute-start.13 = (bf16[512,1024]{1,0:T(8,128)(2,1)}, bf16[512,1024]{1,0:T(8,128)(2,1)}, u32[]{:S(2)}, u32[]{:S(2)}) collective-permute-start(bf16[512,1024]{1,0:T(8,128)(2,1)} %collective-permute-done.3.refs_2_), channel_id=1, source_target_pairs={{0,1},{1,0},{2,3},{3,2},{4,5},{5,4},{6,7},{7,6},{8,9},{9,8},{10,11... | collective-permute-start | bytes 3145736 | tf_op jit(solution)/shard_map/ppermute | solution.py:529
  267.5 48.5 %collective-permute-start.10 = (bf16[512,1152]{1,0:T(8,128)(2,1)}, bf16[512,1152]{1,0:T(8,128)(2,1)}, u32[]{:S(2)}, u32[]{:S(2)}) collective-permute-start(bf16[512,1152]{1,0:T(8,128)(2,1)} %collective-permute-done.9.refs_0_), channel_id=1, source_target_pairs={{0,8},{8,16},{16,24},{24,0},{1,9},{9,17},{17,25},{25,1},{2,10},{10... | collective-permute-start | bytes 3538952 | tf_op jit(solution)/shard_map/ppermute | solution.py:526
  347.3 166.7 %reduce-scatter.4.cloned.1.call-start = ((), (), s32[]{:S(2)}) async-start(), calls=%async_computation.13 | async-start | bytes 5242880 | tf_op jit(solution)/shard_map/reduce_scatter | solution.py:711
  396.1 48.4 %collective-permute-start.28 = (bf16[512,1152]{1,0:T(8,128)(2,1)}, bf16[512,1152]{1,0:T(8,128)(2,1)}, u32[]{:S(2)}, u32[]{:S(2)}) collective-permute-start(bf16[512,1152]{1,0:T(8,128)(2,1)} %get-tuple-element.118), channel_id=1, source_target_pairs={{0,1},{1,0},{2,3},{3,2},{4,5},{5,4},{6,7},{7,6},{8,9},{9,8},{10,11... | collective-permute-start | bytes 3538952 | tf_op jit(solution)/shard_map/ppermute | solution.py:529
  459.4 82.2 %reduce-scatter.6.cloned.1.call-start = ((), (), s32[]{:S(2)}) async-start(), calls=%async_computation.14 | async-start | bytes 2654208 | tf_op jit(solution)/shard_map/reduce_scatter | solution.py:553
  469.3 57.9 %collective-permute-start.30 = (bf16[1024,1024]{1,0:T(8,128)(2,1)}, bf16[1024,1024]{1,0:T(8,128)(2,1)}, u32[]{:S(2)}, u32[]{:S(2)}) collective-permute-start(bf16[1024,1024]{1,0:T(8,128)(2,1)} %get-tuple-element.126), channel_id=1, source_target_pairs={{0,2},{2,0},{4,6},{6,4},{1,3},{3,1},{5,7},{7,5},{8,10},{10,8},{12,... | collective-permute-start | bytes 6291464 | tf_op jit(solution)/shard_map/ppermute | solution.py:550
  470.7 57.6 %collective-permute-start.31 = (bf16[1024,1024]{1,0:T(8,128)(2,1)}, bf16[1024,1024]{1,0:T(8,128)(2,1)}, u32[]{:S(2)}, u32[]{:S(2)}) collective-permute-start(bf16[1024,1024]{1,0:T(8,128)(2,1)} %get-tuple-element.127), channel_id=1, source_target_pairs={{0,4},{2,6},{4,0},{6,2},{1,5},{3,7},{5,1},{7,3},{8,12},{10,14},{12... | collective-permute-start | bytes 6291464 | tf_op jit(solution)/shard_map/ppermute | solution.py:550
  528.2 55.2 %all-to-all-start.3 = ((bf16[4,2,256,512]{3,2,1,0:T(8,128)(2,1)}), bf16[4,2,256,512]{3,2,1,0:T(8,128)(2,1)}, u32[]{:S(2)}, u32[]{:S(2)}) async-start(bf16[4,2,256,512]{3,2,1,0:T(8,128)(2,1)} %attention_backward.1), calls=%async_computation.4 | async-start | bytes 4194304 | tf_op jit(solution)/shard_map/all_to_all | solution.py:771
  533.3 48.3 %reduce-scatter.8.cloned.1.call-start = ((), (), s32[]{:S(2)}) async-start(), calls=%async_computation.15 | async-start | bytes 1179648 | tf_op jit(solution)/shard_map/reduce_scatter | solution.py:553
  540.0 84.2 %collective-permute-start.7 = (bf16[512,1024]{1,0:T(8,128)(2,1)}, bf16[512,1024]{1,0:T(8,128)(2,1)}, u32[]{:S(2)}, u32[]{:S(2)}) collective-permute-start(bf16[512,1024]{1,0:T(8,128)(2,1)} %get-tuple-element.85), channel_id=1, source_target_pairs={{0,1},{1,0},{2,3},{3,2},{4,5},{5,4},{6,7},{7,6},{8,9},{9,8},{10,11... | collective-permute-start | bytes 3145736 | tf_op jit(solution)/shard_map/ppermute | solution.py:529
  540.1 57.2 %collective-permute-start.33 = (bf16[1024,1024]{1,0:T(8,128)(2,1)}, bf16[1024,1024]{1,0:T(8,128)(2,1)}, u32[]{:S(2)}, u32[]{:S(2)}) collective-permute-start(bf16[1024,1024]{1,0:T(8,128)(2,1)} %get-tuple-element.141), channel_id=1, source_target_pairs={{0,6},{2,4},{4,2},{6,0},{1,7},{3,5},{5,3},{7,1},{8,14},{10,12},{12... | collective-permute-start | bytes 6291464 | tf_op jit(solution)/shard_map/ppermute | solution.py:550
  583.4 40.8 %collective-permute-start.32 = (bf16[512,1024]{1,0:T(8,128)(2,1)}, bf16[512,1024]{1,0:T(8,128)(2,1)}, u32[]{:S(2)}, u32[]{:S(2)}) collective-permute-start(bf16[512,1024]{1,0:T(8,128)(2,1)} %add_convert_fusion.3), channel_id=1, source_target_pairs={{0,8},{8,16},{16,24},{24,0},{1,9},{9,17},{17,25},{25,1},{2,10},{10... | collective-permute-start | bytes 3145736 | tf_op jit(solution)/shard_map/ppermute | solution.py:526
  584.8 34.9 %all-to-all-start.4 = ((bf16[4,32,1664]{2,1,0:T(8,128)(2,1)}), bf16[4,32,1664]{2,1,0:T(8,128)(2,1)}, u32[]{:S(2)}, u32[]{:S(2)}) async-start(bf16[4,32,1664]{2,1,0:T(8,128)(2,1)} %pad_maximum_fusion.2), calls=%async_computation.7 | async-start | bytes 851968 | tf_op jit(solution)/shard_map/all_to_all | solution.py:803
  (67 other events, 870.3 us)
Sparse Core Ops, SparseCore 0:
  9.9 55.3 all-gather.5
  84.8 22.5 all-gather.7
  109.3 29.0 all-gather.9
  140.0 87.5 all-gather.11
  347.4 37.6 all-gather.13
  394.0 52.8 reduce-scatter.3
  469.4 53.5 reduce-scatter.5
  539.8 41.6 reduce-scatter.7

commit v3 on v2

--- a/solution.py
+++ b/solution.py
@@ -194,7 +194,16 @@
 
 
 def attention_backward_kernel(
-    packed_ref, lse_ref, grad_ref, own_ref, other_ref, out_ref, total_ref
+    packed_ref,
+    lse_ref,
+    grad_ref,
+    normed_ref,
+    own_ref,
+    other_ref,
+    out_ref,
+    cut_ref,
+    total_ref,
+    product_ref,
 ):
     length, span = packed_ref.shape[1], grad_ref.shape[2]
     low = lax.broadcasted_iota(jnp.int32, (BLOCK, PAIR), 1) < HEAD_SIZE
@@ -250,27 +259,53 @@
             total_ref[rows, :], slice(PAIR, GROUP), rows
         )
 
-
-def attention_backward(packed, lse, grads, tables, groups_local):
+    @pl.when(pl.program_id(1) == 0)
+    def _():
+        product_ref[...] = jnp.zeros_like(product_ref)
+
+    for at in range(length // span):
+        product_ref[...] += dot_tn(normed_ref[at, 0], out_ref[at, 0])
+
+    @pl.when(pl.program_id(1) == pl.num_programs(1) - 1)
+    def _():
+        parts, heads, each = cut_ref.shape[:3]
+        for h in range(heads):
+            block = product_ref[h * parts * each : (h + 1) * parts * each, :]
+            cut_ref[:, h] = block.reshape(parts, each, GROUP).astype(cut_ref.dtype)
+
+
+def attention_backward(packed, lse, grads, normed, tables, groups_local, parts):
     slots, length = packed.shape[:2]
-    pieces, span = grads.shape[0], grads.shape[2]
+    pieces, span, width = grads.shape[0], grads.shape[2], normed.shape[3]
+    each = width // (pieces * parts)
+    kind = jnp.bfloat16 if each % 16 == 0 else jnp.float32
     return pl.pallas_call(
         attention_backward_kernel,
-        grid=(slots, groups_local),
+        grid=(groups_local, slots),
         in_specs=[
-            pl.BlockSpec((1, length, GROUP), lambda s, g: (s, 0, g)),
-            pl.BlockSpec((1, 1, 8, length), lambda s, g: (s, g, 0, 0)),
-            pl.BlockSpec((pieces, 1, span, PAIR), lambda s, g: (0, s, 0, g)),
-            pl.BlockSpec((length, GROUP), lambda s, g: (0, 0)),
-            pl.BlockSpec((length, GROUP), lambda s, g: (0, 0)),
+            pl.BlockSpec((1, length, GROUP), lambda g, s: (s, 0, g)),
+            pl.BlockSpec((1, 1, 8, length), lambda g, s: (s, g, 0, 0)),
+            pl.BlockSpec((pieces, 1, span, PAIR), lambda g, s: (0, s, 0, g)),
+            pl.BlockSpec((pieces, 1, span, width), lambda g, s: (0, s, 0, 0)),
+            pl.BlockSpec((length, GROUP), lambda g, s: (0, 0)),
+            pl.BlockSpec((length, GROUP), lambda g, s: (0, 0)),
         ],
-        out_specs=pl.BlockSpec((pieces, 1, span, GROUP), lambda s, g: (0, s, 0, g)),
-        out_shape=jax.ShapeDtypeStruct((pieces, slots, span, packed.shape[2]), jnp.bfloat16),
-        scratch_shapes=[pltpu.VMEM((length, PAIR), jnp.float32)],
+        out_specs=[
+            pl.BlockSpec((pieces, 1, span, GROUP), lambda g, s: (0, s, 0, g)),
+            pl.BlockSpec((parts, pieces, each, GROUP), lambda g, s: (0, 0, 0, g)),
+        ],
+        out_shape=[
+            jax.ShapeDtypeStruct((pieces, slots, span, packed.shape[2]), jnp.bfloat16),
+            jax.ShapeDtypeStruct((parts, pieces, each, packed.shape[2]), kind),
+        ],
+        scratch_shapes=[
+            pltpu.VMEM((length, PAIR), jnp.float32),
+            pltpu.VMEM((width, GROUP), jnp.float32),
+        ],
         compiler_params=pltpu.CompilerParams(vmem_limit_bytes=VMEM_BYTES),
         cost_estimate=SHORT,
         name="attention_backward",
-    )(packed, lse, grads, *tables)
+    )(packed, lse, grads, normed, *tables)
 
 
 def expert_kernel(sources, n_local, kept, ids_ref, *refs):
@@ -382,7 +417,7 @@
         input_output_aliases={3 + 2 * sources + i: i for i in range(len(kept))},
         compiler_params=pltpu.CompilerParams(vmem_limit_bytes=VMEM_BYTES),
         cost_estimate=pl.CostEstimate(
-            flops=4 * n_local * rows * D * (4 * tokens + 9 * FFE),
+            flops=n_local * rows * D * (4 * tokens + 9 * FFE),
             bytes_accessed=n_local * D * FFE * 6 + tokens * sources * D * 8,
             transcendentals=0,
         ),
@@ -447,24 +482,40 @@
     )(left, right, *extra)
 
 
-def expert_grads_kernel(order_ref, left_ref, right_ref, own_ref, *others):
+def expert_grads_kernel(
+    order_ref, left_ref, right_ref, own_ref, first_send, second_send, first_keep, second_keep
+):
     product = dot_tn(left_ref[0], right_ref[0])
     step = pl.program_id(0)
+    half = product.shape[0] // 2
+    low = jnp.bfloat16
 
     @pl.when(step == 0)
     def _():
         own_ref[...] = product
 
-    for at, other in enumerate(others):
-
-        @pl.when(step == at + 1)
-        def _():
-            other[...] = product.astype(jnp.bfloat16)
+    @pl.when(step == 1)
+    def _():
+        first_send[0] = product[:half].astype(low)
+        second_keep[...] = product[half:]
+
+    @pl.when(step == 2)
+    def _():
+        first_keep[...] = product[:half]
+        second_send[0] = product[half:].astype(low)
+
+    @pl.when(step == 3)
+    def _():
+        first_send[1] = product[:half].astype(low)
+        second_send[1] = product[half:].astype(low)
 
 
 def expert_grads(order, left, right):
     count, depth, height = left.shape
     width = right.shape[2]
+    half = height // 2
+    bf16, f32 = jnp.bfloat16, jnp.float32
+    whole, pair, one = (height, width), (2, half, width), (half, width)
     return pl.pallas_call(
         expert_grads_kernel,
         grid_spec=pltpu.PrefetchScalarGridSpec(
@@ -474,16 +525,23 @@
                 pl.BlockSpec((1, depth, height), lambda i, order: (order[i], 0, 0)),
                 pl.BlockSpec((1, depth, width), lambda i, order: (order[i], 0, 0)),
             ],
-            out_specs=[pl.BlockSpec((height, width), lambda i, order: (0, 0))] * count,
+            out_specs=[
+                pl.BlockSpec(whole, lambda i, order: (0, 0)),
+                pl.BlockSpec(pair, lambda i, order: (0, 0, 0)),
+                pl.BlockSpec(pair, lambda i, order: (0, 0, 0)),
+                pl.BlockSpec(one, lambda i, order: (0, 0)),
+                pl.BlockSpec(one, lambda i, order: (0, 0)),
+            ],
         ),
-        out_shape=[jax.ShapeDtypeStruct((height, width), jnp.float32)]
-        + [jax.ShapeDtypeStruct((height, width), jnp.bfloat16)] * (count - 1),
+        out_shape=[
+            jax.ShapeDtypeStruct(whole, f32),
+            jax.ShapeDtypeStruct(pair, bf16),
+            jax.ShapeDtypeStruct(pair, bf16),
+            jax.ShapeDtypeStruct(one, f32),
+            jax.ShapeDtypeStruct(one, f32),
+        ],
         compiler_params=pltpu.CompilerParams(vmem_limit_bytes=VMEM_BYTES),
-        cost_estimate=pl.CostEstimate(
-            flops=4 * count * depth * height * width,
-            bytes_accessed=2 * count * depth * (height + width) + height * width * (2 * count + 2),
-            transcendentals=0,
-        ),
+        cost_estimate=SHORT,
         name="expert_grads",
     )(order, left, right)
 
@@ -543,8 +601,24 @@
             total = total + across(parts[1]).astype(jnp.float32)
         return total
 
+    def first_phase(parts):
+        return (paired(parts[1], 1), paired(parts[2], 2))
+
+    def second_phase(parts, got):
+        own, _, _, first_keep, second_keep = parts
+        first_next = (first_keep + got[0][1].astype(jnp.float32)).astype(jnp.bfloat16)
+        second_next = (second_keep + got[1][1].astype(jnp.float32)).astype(jnp.bfloat16)
+        return (paired(first_next, 2), paired(second_next, 1))
+
+    def finished(parts, got, last):
+        own = parts[0]
+        half = own.shape[0] // 2
+        first = own[:half] + got[0][0].astype(jnp.float32) + last[0].astype(jnp.float32)
+        second = own[half:] + got[1][0].astype(jnp.float32) + last[1].astype(jnp.float32)
+        return jnp.concatenate([first, second], 0)
+
     def after(value, *others):
-        return lax.optimization_barrier((value,) + others)[0]
+        return lax.optimization_barrier((value, others))[0]
 
     def paired(value, other):
         return lax.ppermute(value, "chip", [(i, i ^ other) for i in range(chip)])
@@ -675,22 +749,20 @@
             ],
             1,
         )
-        payloads = around(after(payload, grad_ring[2]))
-        for step in range(2, n_heads - 1):
-            grad_ring.append(onward(after(grad_ring[-1], payloads[1])))
-        saved, backs, mixes, moving = (), [], [], None
-        for step, value in enumerate(payloads):
-            xs, gs = both(value), both(grad_ring[step])
-            ahead = min(step + 1, n_heads - 1)
-            if step:
-                xs[0] = after(xs[0], payloads[ahead], grad_ring[min(step + 2, n_heads - 1)])
-            if moving is not None:
+        while len(grad_ring) < n_heads:
+            grad_ring.append(onward(grad_ring[-1]))
+        payloads = around(after(payload, grad_ring[-1]))
+        sequence = list(range(1, n_heads - 1)) + [0, n_heads - 1]
+        saved, moving = (), None
+        backs, mixes = {}, {}
+        for step in sequence:
+            xs, gs = both(payloads[step]), both(grad_ring[step])
+            if moving is not None and step:
                 xs[0] = after(xs[0], moving)
             saved, back, mix = experts(
                 step, n_heads, ids, xs, gs, own_in, own_out, tuple(saved)
             )
-            backs.append(back)
-            mixes.append(mix)
+            backs[step], mixes[step] = back, mix
             if step:
                 total = joined(back)
                 if moving is not None:
@@ -699,22 +771,17 @@
         buffer, grad_outputs, hidden, grad_pre = [
             value.reshape(n_local, group_size * CAP, value.shape[3]) for value in saved
         ]
-        hidden = after(hidden, moving)
+        grad_pre = after(grad_pre, moving)
         last_back = onward(moving)
-        grad_pre = after(grad_pre, last_back)
         if expert_in.shape[0] == D:
             order = lax.axis_index("chip") ^ jnp.arange(chip, dtype=jnp.int32)
             parts_in = expert_grads(order, buffer, grad_pre)
         else:
             parts_in = [plain_grads(buffer, grad_pre)]
-        parts_out = plain_grads(grad_outputs, hidden)
-        grad_expert_out = lax.psum_scatter(
-            parts_out.reshape(-1, FFE), "chip", scatter_dimension=0, tiled=True
-        ).astype(jnp.float32)
         w_qkv = plane(after(column[:, :, :qkv_width], context))
         mix_moving = joined(mixes[1]).astype(jnp.bfloat16)
         mix_received = onward(after(mix_moving, last_back))
-        back_sum = joined(backs[0]) + after(last_back, w_qkv, parts_out, *parts_in).astype(jnp.float32)
+        back_sum = joined(backs[0]) + after(last_back, w_qkv, *parts_in).astype(jnp.float32)
 
         grad_gates = back_sum[:, width : width + E] + back_sum[:, width + E : width + 2 * E]
         grad_logits = gates * (grad_gates - jnp.sum(gates * grad_gates, -1, keepdims=True))
@@ -733,6 +800,14 @@
             ]
         ).astype(jnp.bfloat16)
         context_gradient = after(context_gradient, mix_received)
+        hidden = after(hidden, context_gradient)
+        if len(parts_in) > 1:
+            parts_out = expert_grads(order, grad_outputs, hidden)
+        else:
+            parts_out = [plain_grads(grad_outputs, hidden)]
+        near, near_out = (), ()
+        if len(parts_in) > 1:
+            near, near_out = first_phase(parts_in), first_phase(parts_out)
         grad_context_heads = lax.all_to_all(
             context_gradient.reshape(n_heads, slots, span, heads_width),
             "heads",
@@ -745,7 +820,7 @@
         )
         second = cut_rows(
             jnp.concatenate([context[h] for h in range(n_heads)], 1),
-            after(grad_mid_low, context_gradient),
+            after(grad_mid_low, context_gradient, *near),
             n_heads,
             chip * core,
             (normed_ffn, logits_padded, gain_two_term[:, None]),
@@ -753,38 +828,28 @@
         grad_context_heads = after(grad_context_heads, second)
         second = spread_rows(second)
 
-        grad_before = None
         for chunk in range(2, n_heads):
             mix_moving = (joined(mixes[chunk]) + mix_received.astype(jnp.float32)).astype(
                 jnp.bfloat16
             )
             if chunk == 2:
-                grad_before = attention_backward(
-                    packed, lse, after(grad_context_heads, mix_moving), tables, groups_local
+                grad_before, cut = attention_backward(
+                    packed,
+                    lse,
+                    after(grad_context_heads, mix_moving, *parts_out),
+                    normed_whole,
+                    tables,
+                    groups_local,
+                    chip * core,
                 )
             if chunk < n_heads - 1:
                 mix_received = onward(after(mix_moving, grad_context_heads))
-        received = []
-        if len(parts_in) > 1:
-            received = [paired(parts_in[1], 1), paired(parts_in[2], 2)]
-        grad_before = after(grad_before, mix_moving, grad_expert_out, *received)
         grad_mine = lax.all_to_all(
-            grad_before, "heads", split_axis=0, concat_axis=0, tiled=True
+            after(grad_before, mix_received, *near_out), "heads", split_axis=0, concat_axis=0, tiled=True
         ).reshape(n_heads, token_rows, own_columns)
-        qkv_part = spread_rows(
-            cut_rows(
-                normed_whole.reshape(-1, width),
-                grad_before.reshape(-1, own_columns),
-                n_heads,
-                chip * core,
-            )
-        )
-        if received:
-            received.append(paired(after(parts_in[3], *received), 3))
-        else:
-            grad_expert_in = lax.psum_scatter(
-                parts_in[0].reshape(-1, 2 * FFE), "chip", scatter_dimension=0, tiled=True
-            ).astype(jnp.float32)
+        qkv_part = spread_rows(after(cut, second))
+        if near:
+            far_in, far_out = second_phase(parts_in, near), second_phase(parts_out, near_out)
         grad_normed_attn = dot_nt(grad_mine[0], w_qkv[:, :own_columns])
         for h in range(1, n_heads):
             grad_normed_attn = grad_normed_attn + dot_nt(
@@ -792,11 +857,19 @@
             )
         grad_state_norm, _ = norm_back(grad_normed_attn, state, norm_factor(state), gain_one)
         grad_tokens = (grad_mid + grad_state_norm).astype(jnp.bfloat16).reshape(tokens.shape)
-        if received:
-            received[-1] = after(received[-1], grad_tokens)
-            grad_expert_in = parts_in[0]
-            for value in received:
-                grad_expert_in = grad_expert_in + value.astype(jnp.float32)
+        if near:
+            grad_expert_in = finished(parts_in, near, after(far_in, grad_tokens))
+            grad_expert_out = finished(parts_out, near_out, after(far_out, grad_tokens))
+        else:
+            grad_expert_in, grad_expert_out = [
+                lax.psum_scatter(
+                    value[0].reshape(-1, value[0].shape[2]),
+                    "chip",
+                    scatter_dimension=0,
+                    tiled=True,
+                ).astype(jnp.float32)
+                for value in (parts_in, parts_out)
+            ]
         mixture = joined(mixes[0]) + onward(after(mix_moving, grad_mine)).astype(jnp.float32)
         mixed = (valid_float * (mid_state + mixture)).astype(jnp.bfloat16)
 

time: 643 us -> 620 us (0.964)
  waiting for transfers between devices: 321 us -> 262 us
  other arithmetic: 46.8 us -> 60.4 us
  matrix products: 11.9 us -> 24.9 us
  starting transfers between devices: 39.1 us -> 46 us
    ppermute x15, waiting for transfers between devices: 179 us -> 134 us  [onward(): return lax.ppermute(value, 'heads', ring)]
    pallas_call x1 -> x2, Pallas kernels: 20.1 us -> 33.5 us  [expert_grads(): pl.pallas_call(expert_grads_kernel, grid_spec=pltpu.PrefetchScalarGridSpe...]
    reduce_scatter x2, waiting for transfers between devices: 40 us -> 27 us  [spread_rows(): lax.psum_scatter(cut.reshape(-1, cut.shape[3]), ('chip', 'core'), scatter...]
    dot_general x8, matrix products: 5.26 us -> 17.2 us  [dot_nt(): lax.dot_general(left, right, (((1,), (1,)), ((), ())), preferred_element_...]
    all_to_all x1, waiting for transfers between devices: 9.13 us -> 0.01 us  [local(): lax.all_to_all(context_gradient.reshape(n_heads, slots, span, heads_width...]
    convert_element_type x1 -> x4, other arithmetic: 2.84 us -> 9.9 us  [the longest x2 5.26 us: second_phase(): (first_keep + got[0][1].astype(jnp.float32)).astype(jnp.bfloat16)]
    pallas_call x2 -> x1, Pallas kernels: 31.8 us -> 27.4 us  [attention_backward(): pl.pallas_call(attention_backward_kernel, grid=(groups_local, slots), in_...]
    ppermute x3 -> x8, waiting for transfers between devices: 11.3 us -> 14.7 us  [paired(): return lax.ppermute(value, 'chip', [(i, i ^ other) for i in range(chip)])]
  transfers between devices with their start and end apart: 47 -> 51, of which waited for: 20 -> 19; matrix products, arithmetic and copies ran while one was open for 11% -> 16% of each run, Pallas kernels for 28% -> 30%
where the time goes in v3:
time: 620 us; the launch traced here: 611 us
  waiting for transfers between devices  262 us (42%)
  Pallas kernels  181 us (29%)
  other arithmetic  60.4 us (10%)
  starting transfers between devices  46 us (7%)
  matrix products  24.9 us (4%)
  local copies, waits for them, and re-layouts  21.7 us (4%)
  between operations  15.4 us (2%)
    ppermute x15, waiting for transfers between devices, onward(): return lax.ppermute(value, 'heads', ring)  134 us
    pallas_call x4, Pallas kernels, experts(): pl.pallas_call(functools.partial(expert_kernel, sources, n_local, len(kep...  93.6 us
    all_to_all x1, waiting for transfers between devices, local(): lax.all_to_all(jnp.broadcast_to(after(small, rings[1])[None], (n_heads,)...  41 us
    pallas_call x2, Pallas kernels, expert_grads(): pl.pallas_call(expert_grads_kernel, grid_spec=pltpu.PrefetchScalarGridSpe...  33.5 us
    pallas_call x1, Pallas kernels, attention_backward(): pl.pallas_call(attention_backward_kernel, grid=(groups_local, slots), in_...  27.4 us
    reduce_scatter x2, waiting for transfers between devices, spread_rows(): lax.psum_scatter(cut.reshape(-1, cut.shape[3]), ('chip', 'core'), scatter...  27 us
    all_to_all x1, waiting for transfers between devices, local(): lax.all_to_all(context_heads, 'heads', split_axis=0, concat_axis=0, tiled...  20.6 us
    pallas_call x1, Pallas kernels, attention_forward(): pl.pallas_call(functools.partial(attention_forward_kernel, pieces), grid_...  20.5 us
  transfers between devices with their start and end apart: 51, of which 19 were waited for; matrix products, arithmetic and copies ran while one was open for 16% of the time, Pallas kernels for 30%

profile of v3, /device:TPU:0, one launch (start us, length us, event | category | flops | bytes accessed | tf_op | source)
XLA Modules:
  0.0 611.2 jit_solution(10879021410077796786)
XLA Ops:
  13.5 22.9 %collective-permute-done.refs_1_ = bf16[2,256,1024]{2,1,0:T(8,128)(2,1)S(1)} collective-permute-done((bf16[2,256,1024]{2,1,0:T(8,128)(2,1)}, bf16[2,256,1024]{2,1,0:T(8,128)(2,1)S(1)}, u32[]{:S(2)}, u32[]{:S(2)}) %collective-permute-start) | collective-permute-done | bytes 1048608 | tf_op jit(solution)/shard_map/ppermute | solution.py:584
  42.9 41.0 %all-to-all-done = bf16[4,32,3200]{2,1,0:T(8,128)(2,1)S(1)} async-done(((bf16[4,32,3200]{2,1,0:T(8,128)(2,1)}), bf16[4,32,3200]{2,1,0:T(8,128)(2,1)S(1)}, u32[]{:S(2)}, u32[]{:S(2)}) %all-to-all-start) | async-done | bytes 819232 | tf_op jit(solution)/shard_map/all_to_all | solution.py:663
  85.7 26.1 %collective-permute-done.2.refs_3_ = bf16[2,256,1024]{2,1,0:T(8,128)(2,1)S(1)} collective-permute-done((bf16[2,256,1024]{2,1,0:T(8,128)(2,1)}, bf16[2,256,1024]{2,1,0:T(8,128)(2,1)S(1)}, u32[]{:S(2)}, u32[]{:S(2)}) %collective-permute-start.2) | collective-permute-done | bytes 1048608 | tf_op jit(solution)/shard_map/ppermute | solution.py:584
  114.3 20.5 %attention_forward.1 = (bf16[2,1024,512]{2,1,0:T(8,128)(2,1)}, bf16[4,2,256,256]{3,2,1,0:T(8,128)(2,1)}, f32[2,2,8,1024]{3,2,1,0:T(8,128)}, bf16[4,2,256,1024]{3,2,1,0:T(8,128)(2,1)}) custom-call(s32[4]{0:T(128)} %and_select_fusion.place_ref, bf16[2,256,1024]{2,1,0:T(8,128)(2,1)} %refs_0_.1, bf16[2,256,1024]{2,1,0:T(8,128)(2,1)} %copy-done.21, ...), custom_call_target="tpu_custom_call" | custom-call | flops 1024 | bytes 1024 | tf_op jit(solution)/shard_map/attention_forward/pallas_call | solution.py:165
  143.3 20.6 %all-to-all-done.1 = bf16[4,2,256,256]{3,2,1,0:T(8,128)(2,1)S(1)} async-done(((bf16[4,2,256,256]{3,2,1,0:T(8,128)(2,1)}), bf16[4,2,256,256]{3,2,1,0:T(8,128)(2,1)S(1)}, u32[]{:S(2)}, u32[]{:S(2)}) %all-to-all-start.1) | async-done | bytes 1048608 | tf_op jit(solution)/shard_map/all_to_all | solution.py:724
  168.5 21.6 %collective-permute-done.4.refs_2_ = bf16[512,1024]{1,0:T(8,128)(2,1)} collective-permute-done((bf16[512,1024]{1,0:T(8,128)(2,1)}, bf16[512,1024]{1,0:T(8,128)(2,1)}, u32[]{:S(2)}, u32[]{:S(2)}) %collective-permute-start.4) | collective-permute-done | bytes 1048608 | tf_op jit(solution)/shard_map/ppermute | solution.py:584
  198.4 16.9 %collective-permute-done.5.refs_2_ = bf16[512,1024]{1,0:T(8,128)(2,1)} collective-permute-done((bf16[512,1024]{1,0:T(8,128)(2,1)}, bf16[512,1024]{1,0:T(8,128)(2,1)}, u32[]{:S(2)}, u32[]{:S(2)}) %collective-permute-start.5) | collective-permute-done | bytes 1048608 | tf_op jit(solution)/shard_map/ppermute | solution.py:584
  215.4 27.2 %collective-permute-done.8.refs_0_ = bf16[512,1152]{1,0:T(8,128)(2,1)} collective-permute-done((bf16[512,1152]{1,0:T(8,128)(2,1)}, bf16[512,1152]{1,0:T(8,128)(2,1)}, u32[]{:S(2)}, u32[]{:S(2)}) %collective-permute-start.8) | collective-permute-done | bytes 1179680 | tf_op jit(solution)/shard_map/ppermute | solution.py:584
  247.3 23.4 %experts.4 = (bf16[4,4,320,1024]{3,2,1,0:T(8,128)(2,1)}, bf16[4,4,320,1024]{3,2,1,0:T(8,128)(2,1)}, bf16[4,4,320,512]{3,2,1,0:T(8,128)(2,1)}, bf16[4,4,320,1024]...) custom-call(s32[4]{0:T(128)} %multiply_add_fusion.1.ids_ref, ...), custom_call_target="tpu_custom_call" | custom-call | flops 8724152320 | bytes 20971520 | tf_op jit(solution)/shard_map/experts/pallas_call | solution.py:395
  280.4 23.4 %experts.5 = (bf16[4,4,320,1024]{3,2,1,0:T(8,128)(2,1)}, bf16[4,4,320,1024]{3,2,1,0:T(8,128)(2,1)}, bf16[4,4,320,512]{3,2,1,0:T(8,128)(2,1)}, bf16[4,4,320,1024]...) custom-call(s32[4]{0:T(128)} %multiply_add_fusion.1.ids_ref, ...), custom_call_target="tpu_custom_call", output_to_operand_aliasing={{0}: (7, {}), {1}: (8, {}), {2}: (9, {}), {3}: (10, {})} | custom-call | flops 8724152320 | bytes 20971520 | tf_op jit(solution)/shard_map/experts/pallas_call | solution.py:395
  307.7 23.4 %experts.6 = (bf16[4,4,320,1024]{3,2,1,0:T(8,128)(2,1)}, bf16[4,4,320,1024]{3,2,1,0:T(8,128)(2,1)}, bf16[4,4,320,512]{3,2,1,0:T(8,128)(2,1)}, bf16[4,4,320,1024]...) custom-call(s32[4]{0:T(128)} %multiply_add_fusion.1.ids_ref, ...), custom_call_target="tpu_custom_call", output_to_operand_aliasing={{0}: (7, {}), {1}: (8, {}), {2}: (9, {}), {3}: (10, {})} | custom-call | flops 8724152320 | bytes 20971520 | tf_op jit(solution)/shard_map/experts/pallas_call | solution.py:395
  334.8 23.4 %experts.7 = (bf16[4,4,320,1024]{3,2,1,0:T(8,128)(2,1)}, bf16[4,4,320,1024]{3,2,1,0:T(8,128)(2,1)}, bf16[4,4,320,512]{3,2,1,0:T(8,128)(2,1)}, bf16[4,4,320,1024]...) custom-call(s32[4]{0:T(128)} %multiply_add_fusion.1.ids_ref, ...), custom_call_target="tpu_custom_call", output_to_operand_aliasing={{0}: (7, {}), {1}: (8, {}), {2}: (9, {}), {3}: (10, {})} | custom-call | flops 8724152320 | bytes 20971520 | tf_op jit(solution)/shard_map/experts/pallas_call | solution.py:395
  358.8 5.0 collective-permute-done.25
  372.5 20.4 %expert_grads.2 = (f32[1024,1024]{1,0:T(8,128)}, bf16[2,512,1024]{2,1,0:T(8,128)(2,1)}, bf16[2,512,1024]{2,1,0:T(8,128)(2,1)}, f32[512,1024]{1,0:T(8,128)}, f32[512,1024]{1,0:T(8,128)}) custom-call(s32[4]{0:T(128)} %iota_xor_fusion.order_ref, bf16[4,1280,1024]{2,1,0:T(8,128)(2,1)} %bitcast.130, bf16[4,1280,1024]{2,1,0:T(8,128)(2,1)} %bitcast.132), custom_call_target="tpu_custom_call" | custom-call | flops 1024 | bytes 1024 | tf_op jit(solution)/shard_map/expert_grads/pallas_call | solution.py:519
  415.3 7.5 %collective-permute-done.27 = bf16[512,1024]{1,0:T(8,128)(2,1)} collective-permute-done((bf16[512,1024]{1,0:T(8,128)(2,1)}, bf16[512,1024]{1,0:T(8,128)(2,1)}, u32[]{:S(2)}, u32[]{:S(2)}) %collective-permute-start.27) | collective-permute-done | bytes 1048608 | tf_op jit(solution)/shard_map/ppermute | solution.py:584
  427.1 13.7 %collective-permute-done.29 = bf16[2,512,1024]{2,1,0:T(8,128)(2,1)} collective-permute-done((bf16[2,512,1024]{2,1,0:T(8,128)(2,1)}, bf16[2,512,1024]{2,1,0:T(8,128)(2,1)}, u32[]{:S(2)}, u32[]{:S(2)}) %collective-permute-start.29) | collective-permute-done | bytes 2097184 | tf_op jit(solution)/shard_map/ppermute | solution.py:624
  441.8 5.8 cut_rows.1
  447.7 13.0 %expert_grads.3 = (f32[1024,512]{1,0:T(8,128)}, bf16[2,512,512]{2,1,0:T(8,128)(2,1)}, bf16[2,512,512]{2,1,0:T(8,128)(2,1)}, f32[512,512]{1,0:T(8,128)}, f32[512,512]{1,0:T(8,128)}) custom-call(s32[4]{0:T(128)} %iota_xor_fusion.order_ref, bf16[4,1280,1024]{2,1,0:T(8,128)(2,1)} %bitcast.131, bf16[4,1280,512]{2,1,0:T(8,128)(2,1)} %bitcast.133), custom_call_target="tpu_custom_call" | custom-call | flops 1024 | bytes 1024 | tf_op jit(solution)/shard_map/expert_grads/pallas_call | solution.py:519
  468.0 27.4 %attention_backward.1 = (bf16[4,2,256,512]{3,2,1,0:T(8,128)(2,1)}, bf16[8,4,32,512]{3,2,1,0:T(8,128)(2,1)}) custom-call(bf16[2,1024,512]{2,1,0:T(8,128)(2,1)} %get-tuple-element.135.packed_ref, f32[2,2,8,1024]{3,2,1,0:T(8,128)} %get-tuple-element.136.lse_ref, bf16[4,2,256,256]{3,2,1,0:T(8,128)(2,1)} %all-to-all-done.2.grad_ref, ...), custom_call_target="tpu_custom_call" | custom-call | flops 1024 | bytes 1024 | tf_op jit(solution)/shard_map/attention_backward/pallas_call | solution.py:282
  495.4 4.4 all-to-all-start.3
  518.3 26.9 %reduce-scatter.5.cloned.1.call-done = bf16[128,512]{1,0:T(8,128)(2,1)} async-done(((bf16[1024,512]{1,0:T(8,128)(2,1)}), bf16[128,512]{1,0:T(8,128)(2,1)}) %reduce-scatter.5.cloned.1.call-update) | async-done | bytes 131088 | tf_op jit(solution)/shard_map/reduce_scatter | solution.py:627
  556.2 4.9 all-to-all-start.4
  561.1 4.5 fusion.6
  578.6 17.7 %all-to-all-done.4 = bf16[4,32,1664]{2,1,0:T(8,128)(2,1)} async-done(((bf16[4,32,1664]{2,1,0:T(8,128)(2,1)}), bf16[4,32,1664]{2,1,0:T(8,128)(2,1)}, u32[]{:S(2)}, u32[]{:S(2)}) %all-to-all-start.4) | async-done | bytes 426016 | tf_op jit(solution)/shard_map/all_to_all | solution.py:876
  (251 shorter events, 154.2 us)
Async XLA Ops:
  7.2 77.6 %all-gather.6.cloned.1.call-start = ((), (), s32[]{:S(2)}) async-start(), calls=%async_computation.7 | async-start | bytes 5242880 | tf_op jit(solution)/shard_map/all_gather | solution.py:671
  37.4 46.5 %all-to-all-start = ((bf16[4,32,3200]{2,1,0:T(8,128)(2,1)}), bf16[4,32,3200]{2,1,0:T(8,128)(2,1)S(1)}, u32[]{:S(2)}, u32[]{:S(2)}) async-start(bf16[4,32,3200]{2,1,0:T(8,128)(2,1)} %broadcast_in_dim.24), calls=%async_computation | async-start | bytes 1638400 | tf_op jit(solution)/shard_map/all_to_all | solution.py:663
  40.9 70.9 %all-gather.8.cloned.1.call-start = ((), (), s32[]{:S(2)}) async-start(), calls=%async_computation.8 | async-start | bytes 1474560 | tf_op jit(solution)/shard_map/all_gather | solution.py:674
  41.0 43.8 %collective-permute-start.1 = (bf16[2,256,1024]{2,1,0:T(8,128)(2,1)S(1)}, bf16[2,256,1024]{2,1,0:T(8,128)(2,1)}, u32[]{:S(2)}, u32[]{:S(2)}) collective-permute-start(bf16[2,256,1024]{2,1,0:T(8,128)(2,1)S(1)} %collective-permute-done.refs_1_), channel_id=1, source_target_pairs={{0,8},{8,16},{16,24},{24,0},{1,9},{9,17},{17,25},{25,1},{2,10},{10... | collective-permute-start | bytes 3145736 | tf_op jit(solution)/shard_map/ppermute | solution.py:584
  84.8 57.2 %all-gather.10.cloned.1.call-start = ((), (), s32[]{:S(2)}) async-start(), calls=%async_computation.9 | async-start | bytes 2654208 | tf_op jit(solution)/shard_map/all_gather | solution.py:674
  85.6 161.7 %all-gather.12.cloned.1.call-start = ((), (), s32[]{:S(2)}) async-start(), calls=%async_computation.10 | async-start | bytes 10485760 | tf_op jit(solution)/shard_map/all_gather | solution.py:697
  140.5 257.6 %all-gather.14.cloned.1.call-start = ((), (), s32[]{:S(2)}) async-start(), calls=%async_computation.11 | async-start | bytes 4718592 | tf_op jit(solution)/shard_map/all_gather | solution.py:674
  280.0 51.1 %collective-permute-start.18 = (bf16[512,1152]{1,0:T(8,128)(2,1)S(1)}, bf16[512,1152]{1,0:T(8,128)(2,1)}, u32[]{:S(2)}, u32[]{:S(2)}) collective-permute-start(bf16[512,1152]{1,0:T(8,128)(2,1)S(1)} %add_convert_fusion.2), channel_id=1, source_target_pairs={{0,8},{8,16},{16,24},{24,0},{1,9},{9,17},{17,25},{25,1},{2,10},{10... | collective-permute-start | bytes 3538952 | tf_op jit(solution)/shard_map/ppermute | solution.py:584
  372.0 90.6 %collective-permute-start.22 = (bf16[512,1024]{1,0:T(8,128)(2,1)}, bf16[512,1024]{1,0:T(8,128)(2,1)}, u32[]{:S(2)}, u32[]{:S(2)}) collective-permute-start(bf16[512,1024]{1,0:T(8,128)(2,1)} %get-tuple-element.114), channel_id=1, source_target_pairs={{0,1},{1,0},{2,3},{3,2},{4,5},{5,4},{6,7},{7,6},{8,9},{9,8},{10,11... | collective-permute-start | bytes 3145736 | tf_op jit(solution)/shard_map/ppermute | solution.py:587
  393.0 47.9 %collective-permute-start.29 = (bf16[2,512,1024]{2,1,0:T(8,128)(2,1)}, bf16[2,512,1024]{2,1,0:T(8,128)(2,1)}, u32[]{:S(2)}, u32[]{:S(2)}) collective-permute-start(bf16[2,512,1024]{2,1,0:T(8,128)(2,1)} %get-tuple-element.126), channel_id=1, source_target_pairs={{0,2},{2,0},{4,6},{6,4},{1,3},{3,1},{5,7},{7,5},{8,10},{10,8},{12,... | collective-permute-start | bytes 6291464 | tf_op jit(solution)/shard_map/ppermute | solution.py:624
  394.3 47.6 %collective-permute-start.30 = (bf16[2,512,1024]{2,1,0:T(8,128)(2,1)}, bf16[2,512,1024]{2,1,0:T(8,128)(2,1)}, u32[]{:S(2)}, u32[]{:S(2)}) collective-permute-start(bf16[2,512,1024]{2,1,0:T(8,128)(2,1)} %get-tuple-element.127), channel_id=1, source_target_pairs={{0,4},{2,6},{4,0},{6,2},{1,5},{3,7},{5,1},{7,3},{8,12},{10,14},{12... | collective-permute-start | bytes 6291464 | tf_op jit(solution)/shard_map/ppermute | solution.py:624
  422.8 43.0 %all-to-all-start.2 = ((bf16[4,2,256,256]{3,2,1,0:T(8,128)(2,1)}), bf16[4,2,256,256]{3,2,1,0:T(8,128)(2,1)}, u32[]{:S(2)}, u32[]{:S(2)}) async-start(bf16[4,2,256,256]{3,2,1,0:T(8,128)(2,1)} %bitcast.146), calls=%async_computation.2 | async-start | bytes 2097152 | tf_op jit(solution)/shard_map/all_to_all | solution.py:811
  427.1 73.2 %reduce-scatter.3.cloned.1.call-start = ((), (), s32[]{:S(2)}) async-start(), calls=%async_computation.12 | async-start | bytes 2654208 | tf_op jit(solution)/shard_map/reduce_scatter | solution.py:627
  460.7 34.7 %collective-permute-start.32 = (bf16[2,512,512]{2,1,0:T(8,128)(2,1)}, bf16[2,512,512]{2,1,0:T(8,128)(2,1)}, u32[]{:S(2)}, u32[]{:S(2)}) collective-permute-start(bf16[2,512,512]{2,1,0:T(8,128)(2,1)} %get-tuple-element.141), channel_id=1, source_target_pairs={{0,2},{2,0},{4,6},{6,4},{1,3},{3,1},{5,7},{7,5},{8,10},{10,8},{12,... | collective-permute-start | bytes 3145736 | tf_op jit(solution)/shard_map/ppermute | solution.py:624
  461.3 34.1 %collective-permute-start.33 = (bf16[2,512,512]{2,1,0:T(8,128)(2,1)}, bf16[2,512,512]{2,1,0:T(8,128)(2,1)}, u32[]{:S(2)}, u32[]{:S(2)}) collective-permute-start(bf16[2,512,512]{2,1,0:T(8,128)(2,1)} %get-tuple-element.142), channel_id=1, source_target_pairs={{0,4},{2,6},{4,0},{6,2},{1,5},{3,7},{5,1},{7,3},{8,12},{10,14},{12... | collective-permute-start | bytes 3145736 | tf_op jit(solution)/shard_map/ppermute | solution.py:624
  495.4 51.5 %all-to-all-start.3 = ((bf16[4,2,256,512]{3,2,1,0:T(8,128)(2,1)}), bf16[4,2,256,512]{3,2,1,0:T(8,128)(2,1)}, u32[]{:S(2)}, u32[]{:S(2)}) async-start(bf16[4,2,256,512]{3,2,1,0:T(8,128)(2,1)} %get-tuple-element.148), calls=%async_computation.3 | async-start | bytes 4194304 | tf_op jit(solution)/shard_map/all_to_all | solution.py:847
  499.9 45.4 %reduce-scatter.5.cloned.1.call-start = ((), (), s32[]{:S(2)}) async-start(), calls=%async_computation.13 | async-start | bytes 1179648 | tf_op jit(solution)/shard_map/reduce_scatter | solution.py:627
  500.7 100.1 %collective-permute-start.15 = (bf16[512,1024]{1,0:T(8,128)(2,1)}, bf16[512,1024]{1,0:T(8,128)(2,1)}, u32[]{:S(2)}, u32[]{:S(2)}) collective-permute-start(bf16[512,1024]{1,0:T(8,128)(2,1)} %get-tuple-element.103), channel_id=1, source_target_pairs={{0,1},{1,0},{2,3},{3,2},{4,5},{5,4},{6,7},{7,6},{8,9},{9,8},{10,11... | collective-permute-start | bytes 3145736 | tf_op jit(solution)/shard_map/ppermute | solution.py:587
  504.5 62.6 %collective-permute-start.35 = (bf16[512,1024]{1,0:T(8,128)(2,1)}, bf16[512,1024]{1,0:T(8,128)(2,1)}, u32[]{:S(2)}, u32[]{:S(2)}) collective-permute-start(bf16[512,1024]{1,0:T(8,128)(2,1)} %fusion.2), channel_id=1, source_target_pairs={{0,4},{2,6},{4,0},{6,2},{1,5},{3,7},{5,1},{7,3},{8,12},{10,14},{12... | collective-permute-start | bytes 3145736 | tf_op jit(solution)/shard_map/ppermute | solution.py:624
  507.5 61.7 %collective-permute-start.36 = (bf16[512,1024]{1,0:T(8,128)(2,1)}, bf16[512,1024]{1,0:T(8,128)(2,1)}, u32[]{:S(2)}, u32[]{:S(2)}) collective-permute-start(bf16[512,1024]{1,0:T(8,128)(2,1)} %fusion.1), channel_id=1, source_target_pairs={{0,2},{2,0},{4,6},{6,4},{1,3},{3,1},{5,7},{7,5},{8,10},{10,8},{12,... | collective-permute-start | bytes 3145736 | tf_op jit(solution)/shard_map/ppermute | solution.py:624
  511.1 58.1 %collective-permute-start.37 = (bf16[512,512]{1,0:T(8,128)(2,1)}, bf16[512,512]{1,0:T(8,128)(2,1)}, u32[]{:S(2)}, u32[]{:S(2)}) collective-permute-start(bf16[512,512]{1,0:T(8,128)(2,1)} %fusion.28), channel_id=1, source_target_pairs={{0,4},{2,6},{4,0},{6,2},{1,5},{3,7},{5,1},{7,3},{8,12},{10,14},{12... | collective-permute-start | bytes 1572872 | tf_op jit(solution)/shard_map/ppermute | solution.py:624
  514.9 54.3 %collective-permute-start.38 = (bf16[512,512]{1,0:T(8,128)(2,1)}, bf16[512,512]{1,0:T(8,128)(2,1)}, u32[]{:S(2)}, u32[]{:S(2)}) collective-permute-start(bf16[512,512]{1,0:T(8,128)(2,1)} %fusion.27), channel_id=1, source_target_pairs={{0,2},{2,0},{4,6},{6,4},{1,3},{3,1},{5,7},{7,5},{8,10},{10,8},{12,... | collective-permute-start | bytes 1572872 | tf_op jit(solution)/shard_map/ppermute | solution.py:624
  556.2 40.1 %all-to-all-start.4 = ((bf16[4,32,1664]{2,1,0:T(8,128)(2,1)}), bf16[4,32,1664]{2,1,0:T(8,128)(2,1)}, u32[]{:S(2)}, u32[]{:S(2)}) async-start(bf16[4,32,1664]{2,1,0:T(8,128)(2,1)} %pad_maximum_fusion.4), calls=%async_computation.6 | async-start | bytes 851968 | tf_op jit(solution)/shard_map/all_to_all | solution.py:876
  567.1 33.7 %collective-permute-start.34 = (bf16[512,1024]{1,0:T(8,128)(2,1)}, bf16[512,1024]{1,0:T(8,128)(2,1)}, u32[]{:S(2)}, u32[]{:S(2)}) collective-permute-start(bf16[512,1024]{1,0:T(8,128)(2,1)} %add_convert_fusion.3), channel_id=1, source_target_pairs={{0,8},{8,16},{16,24},{24,0},{1,9},{9,17},{17,25},{25,1},{2,10},{10... | collective-permute-start | bytes 3145736 | tf_op jit(solution)/shard_map/ppermute | solution.py:584
  (63 other events, 993.8 us)
Sparse Core Ops, SparseCore 0:
  9.9 55.3 all-gather.5
  84.9 22.5 all-gather.7
  109.4 29.0 all-gather.9
  140.2 87.5 all-gather.11
  275.3 35.3 all-gather.13
  447.8 49.4 reduce-scatter.2
  504.2 40.9 reduce-scatter.4

commit v4 on v3

--- a/solution.py
+++ b/solution.py
@@ -200,6 +200,7 @@
     normed_ref,
     own_ref,
     other_ref,
+    filled_ref,
     out_ref,
     cut_ref,
     total_ref,
@@ -274,11 +275,10 @@
             cut_ref[:, h] = block.reshape(parts, each, GROUP).astype(cut_ref.dtype)
 
 
-def attention_backward(packed, lse, grads, normed, tables, groups_local, parts):
+def attention_backward(packed, lse, grads, normed, tables, groups_local, cut):
     slots, length = packed.shape[:2]
     pieces, span, width = grads.shape[0], grads.shape[2], normed.shape[3]
-    each = width // (pieces * parts)
-    kind = jnp.bfloat16 if each % 16 == 0 else jnp.float32
+    parts, _, each, _ = cut.shape
     return pl.pallas_call(
         attention_backward_kernel,
         grid=(groups_local, slots),
@@ -289,6 +289,7 @@
             pl.BlockSpec((pieces, 1, span, width), lambda g, s: (0, s, 0, 0)),
             pl.BlockSpec((length, GROUP), lambda g, s: (0, 0)),
             pl.BlockSpec((length, GROUP), lambda g, s: (0, 0)),
+            pl.BlockSpec(memory_space=pl.ANY),
         ],
         out_specs=[
             pl.BlockSpec((pieces, 1, span, GROUP), lambda g, s: (0, s, 0, g)),
@@ -296,8 +297,9 @@
         ],
         out_shape=[
             jax.ShapeDtypeStruct((pieces, slots, span, packed.shape[2]), jnp.bfloat16),
-            jax.ShapeDtypeStruct((parts, pieces, each, packed.shape[2]), kind),
+            jax.ShapeDtypeStruct(cut.shape, cut.dtype),
         ],
+        input_output_aliases={6: 1},
         scratch_shapes=[
             pltpu.VMEM((length, PAIR), jnp.float32),
             pltpu.VMEM((width, GROUP), jnp.float32),
@@ -305,7 +307,7 @@
         compiler_params=pltpu.CompilerParams(vmem_limit_bytes=VMEM_BYTES),
         cost_estimate=SHORT,
         name="attention_backward",
-    )(packed, lse, grads, normed, *tables)
+    )(packed, lse, grads, normed, *tables, cut)
 
 
 def expert_kernel(sources, n_local, kept, ids_ref, *refs):
@@ -426,47 +428,39 @@
     return results[:4], results[4 : 4 + sources], results[4 + sources :]
 
 
-def cut_rows_kernel(extra, left_ref, right_ref, *refs):
-    out_ref = refs[-1]
+def cut_rows_kernel(offset, left_ref, right_ref, normed_ref, logits_ref, gain_ref, out_ref):
     parts, rows = out_ref.shape[0], out_ref.shape[2]
     width = right_ref.shape[1]
     product = dot_tn(left_ref[...], right_ref[...])
-    out_ref[:, 0, :, :width] = product.reshape(parts, rows, width).astype(out_ref.dtype)
-    if extra:
-        normed_ref, logits_ref, gain_ref = refs[:3]
-        rest = logits_ref[...]
-        tail = jnp.zeros((left_ref.shape[1], TAIL), jnp.float32)
-        for _ in range(3):
-            term = rest.astype(jnp.bfloat16)
-            rest = rest - term.astype(jnp.float32)
-            tail = tail + dot_tn(normed_ref[...], term)
-        lane = lax.broadcasted_iota(jnp.int32, tail.shape, 1)
-        tail = jnp.where(lane == E, gain_ref[...], tail)
-        out_ref[:, 0, :, width:] = tail.reshape(parts, rows, TAIL).astype(out_ref.dtype)
-
-
-def cut_rows(left, right, n_heads, parts, extra=()):
-    depth, height = left.shape
-    each = height // n_heads
+    out_ref[:, 0, :, :offset] = jnp.zeros((parts, rows, offset), out_ref.dtype)
+    out_ref[:, 0, :, offset : offset + width] = product.reshape(parts, rows, width).astype(
+        out_ref.dtype
+    )
+    rest = logits_ref[...]
+    tail = jnp.zeros((left_ref.shape[1], TAIL), jnp.float32)
+    for _ in range(3):
+        term = rest.astype(jnp.bfloat16)
+        rest = rest - term.astype(jnp.float32)
+        tail = tail + dot_tn(normed_ref[...], term)
+    lane = lax.broadcasted_iota(jnp.int32, tail.shape, 1)
+    tail = jnp.where(lane == E, gain_ref[...], tail)
+    out_ref[:, 0, :, offset + width :] = tail.reshape(parts, rows, TAIL).astype(out_ref.dtype)
+
+
+def cut_rows(left, right, normed, logits, gain_term, parts, offset):
+    n_heads, depth, each = left.shape
     width = right.shape[1]
-    columns = width + (TAIL if extra else 0)
-    extra_specs = (
-        [
+    columns = offset + width + TAIL
+    return pl.pallas_call(
+        functools.partial(cut_rows_kernel, offset),
+        grid=(n_heads,),
+        in_specs=[
+            pl.BlockSpec((pl.squeezed, depth, each), lambda h: (h, 0, 0)),
+            pl.BlockSpec((depth, width), lambda h: (0, 0)),
             pl.BlockSpec((depth, each), lambda h: (0, h)),
             pl.BlockSpec((depth, TAIL), lambda h: (0, 0)),
             pl.BlockSpec((each, 1), lambda h: (h, 0)),
-        ]
-        if extra
-        else []
-    )
-    return pl.pallas_call(
-        functools.partial(cut_rows_kernel, bool(extra)),
-        grid=(n_heads,),
-        in_specs=[
-            pl.BlockSpec((depth, each), lambda h: (0, h)),
-            pl.BlockSpec((depth, width), lambda h: (0, 0)),
-        ]
-        + extra_specs,
+        ],
         out_specs=pl.BlockSpec((parts, 1, each // parts, columns), lambda h: (0, h, 0, 0)),
         out_shape=jax.ShapeDtypeStruct(
             (parts, n_heads, each // parts, columns),
@@ -474,12 +468,12 @@
         ),
         compiler_params=pltpu.CompilerParams(vmem_limit_bytes=VMEM_BYTES),
         cost_estimate=pl.CostEstimate(
-            flops=4 * depth * height * columns,
-            bytes_accessed=depth * (height + width) * 2 + height * columns * 4,
+            flops=4 * depth * each * n_heads * columns,
+            bytes_accessed=depth * (each * n_heads + width) * 2 + each * n_heads * columns * 4,
             transcendentals=0,
         ),
         name="cut_rows",
-    )(left, right, *extra)
+    )(left, right, normed, logits, gain_term)
 
 
 def expert_grads_kernel(
@@ -773,6 +767,7 @@
         ]
         grad_pre = after(grad_pre, moving)
         last_back = onward(moving)
+        hidden, last_back = lax.optimization_barrier((hidden, last_back))
         if expert_in.shape[0] == D:
             order = lax.axis_index("chip") ^ jnp.arange(chip, dtype=jnp.int32)
             parts_in = expert_grads(order, buffer, grad_pre)
@@ -800,14 +795,15 @@
             ]
         ).astype(jnp.bfloat16)
         context_gradient = after(context_gradient, mix_received)
-        hidden = after(hidden, context_gradient)
+        near, near_out = (), ()
         if len(parts_in) > 1:
+            near = first_phase(parts_in)
             parts_out = expert_grads(order, grad_outputs, hidden)
         else:
             parts_out = [plain_grads(grad_outputs, hidden)]
-        near, near_out = (), ()
-        if len(parts_in) > 1:
-            near, near_out = first_phase(parts_in), first_phase(parts_out)
+        context_gradient, parts_out = lax.optimization_barrier((context_gradient, parts_out))
+        if near:
+            near_out = first_phase(parts_out)
         grad_context_heads = lax.all_to_all(
             context_gradient.reshape(n_heads, slots, span, heads_width),
             "heads",
@@ -819,15 +815,16 @@
             [grad_logits, jnp.zeros((token_rows, TAIL - E), jnp.float32)], 1
         )
         second = cut_rows(
-            jnp.concatenate([context[h] for h in range(n_heads)], 1),
-            after(grad_mid_low, context_gradient, *near),
-            n_heads,
+            context,
+            after(grad_mid_low, context_gradient),
+            normed_ffn,
+            logits_padded,
+            gain_two_term[:, None],
             chip * core,
-            (normed_ffn, logits_padded, gain_two_term[:, None]),
-        )
-        grad_context_heads = after(grad_context_heads, second)
-        second = spread_rows(second)
-
+            own_columns,
+        )
+
+        mix_received, near, second = lax.optimization_barrier((mix_received, near, second))
         for chunk in range(2, n_heads):
             mix_moving = (joined(mixes[chunk]) + mix_received.astype(jnp.float32)).astype(
                 jnp.bfloat16
@@ -836,20 +833,22 @@
                 grad_before, cut = attention_backward(
                     packed,
                     lse,
-                    after(grad_context_heads, mix_moving, *parts_out),
+                    after(grad_context_heads, mix_moving),
                     normed_whole,
                     tables,
                     groups_local,
-                    chip * core,
+                    second,
                 )
             if chunk < n_heads - 1:
                 mix_received = onward(after(mix_moving, grad_context_heads))
         grad_mine = lax.all_to_all(
-            after(grad_before, mix_received, *near_out), "heads", split_axis=0, concat_axis=0, tiled=True
+            after(grad_before, mix_received), "heads", split_axis=0, concat_axis=0, tiled=True
         ).reshape(n_heads, token_rows, own_columns)
-        qkv_part = spread_rows(after(cut, second))
+        part = spread_rows(cut)
         if near:
             far_in, far_out = second_phase(parts_in, near), second_phase(parts_out, near_out)
+        mix_moving, grad_mine = lax.optimization_barrier((mix_moving, grad_mine))
+        mix_last = onward(mix_moving)
         grad_normed_attn = dot_nt(grad_mine[0], w_qkv[:, :own_columns])
         for h in range(1, n_heads):
             grad_normed_attn = grad_normed_attn + dot_nt(
@@ -858,8 +857,8 @@
         grad_state_norm, _ = norm_back(grad_normed_attn, state, norm_factor(state), gain_one)
         grad_tokens = (grad_mid + grad_state_norm).astype(jnp.bfloat16).reshape(tokens.shape)
         if near:
-            grad_expert_in = finished(parts_in, near, after(far_in, grad_tokens))
-            grad_expert_out = finished(parts_out, near_out, after(far_out, grad_tokens))
+            grad_expert_in = finished(parts_in, near, after(far_in, mix_last))
+            grad_expert_out = finished(parts_out, near_out, after(far_out, mix_last))
         else:
             grad_expert_in, grad_expert_out = [
                 lax.psum_scatter(
@@ -870,21 +869,17 @@
                 ).astype(jnp.float32)
                 for value in (parts_in, parts_out)
             ]
-        mixture = joined(mixes[0]) + onward(after(mix_moving, grad_mine)).astype(jnp.float32)
+        mixture = joined(mixes[0]) + mix_last.astype(jnp.float32)
         mixed = (valid_float * (mid_state + mixture)).astype(jnp.bfloat16)
 
         last = lax.all_to_all(
-            after(jnp.concatenate([second, qkv_part], 2), grad_mine),
-            "heads",
-            split_axis=0,
-            concat_axis=0,
-            tiled=True,
+            part, "heads", split_axis=0, concat_axis=0, tiled=True
         ).astype(jnp.float32)
-        second = jnp.sum(last[:, :, : D + TAIL], 0)
+        second = jnp.sum(last[:, :, own_columns:], 0)
         grad_attn_out = second[:, :D]
         grad_router = second[:, D : D + E]
         grad_gain_ffn = second[:, D + E]
-        grad_attn_in = jnp.concatenate([last[h, :, D + TAIL :] for h in range(n_heads)], 1)
+        grad_attn_in = jnp.concatenate([last[h, :, :own_columns] for h in range(n_heads)], 1)
         grad_gain_attn = jnp.sum(
             grad_attn_in * attention_input_weight.astype(jnp.float32), -1
         ) / gain_attn.astype(jnp.float32)

time: 620 us -> 589 us (0.950)
  waiting for transfers between devices: 262 us -> 253 us
  matrix products: 24.9 us -> 18.4 us
  other arithmetic: 60.4 us -> 53.9 us
    reduce_scatter x2 -> x1, waiting for transfers between devices: 27 us -> 9.32 us  [spread_rows(): lax.psum_scatter(cut.reshape(-1, cut.shape[3]), ('chip', 'core'), scatter...]
    ppermute x8, waiting for transfers between devices: 14.7 us -> 22.9 us  [paired(): return lax.ppermute(value, 'chip', [(i, i ^ other) for i in range(chip)])]
    all_to_all x1, waiting for transfers between devices: 0.01 us -> 7.65 us  [local(): lax.all_to_all(context_gradient.reshape(n_heads, slots, span, heads_width...]
    dot_general x8, matrix products: 17.2 us -> 10.6 us  [dot_nt(): lax.dot_general(left, right, (((1,), (1,)), ((), ())), preferred_element_...]
  transfers between devices with their start and end apart: 51 -> 50, of which waited for: 19 -> 23; matrix products, arithmetic and copies ran while one was open for 16% -> 14% of each run, Pallas kernels for 30% -> 31%
where the time goes in v4:
time: 589 us; the launch traced here: 581 us
  waiting for transfers between devices  253 us (43%)
  Pallas kernels  180 us (31%)
  other arithmetic  53.9 us (9%)
  starting transfers between devices  40.8 us (7%)
  local copies, waits for them, and re-layouts  19.1 us (3%)
  matrix products  18.4 us (3%)
  between operations  15.3 us (3%)
    ppermute x15, waiting for transfers between devices, onward(): return lax.ppermute(value, 'heads', ring)  132 us
    pallas_call x4, Pallas kernels, experts(): pl.pallas_call(functools.partial(expert_kernel, sources, n_local, len(kep...  93.6 us
    all_to_all x1, waiting for transfers between devices, local(): lax.all_to_all(jnp.broadcast_to(after(small, rings[1])[None], (n_heads,)...  41 us
    pallas_call x2, Pallas kernels, expert_grads(): pl.pallas_call(expert_grads_kernel, grid_spec=pltpu.PrefetchScalarGridSpe...  33.2 us
    pallas_call x1, Pallas kernels, attention_backward(): pl.pallas_call(attention_backward_kernel, grid=(groups_local, slots), in_...  27.1 us
    ppermute x8, waiting for transfers between devices, paired(): return lax.ppermute(value, 'chip', [(i, i ^ other) for i in range(chip)])  22.9 us
    all_to_all x1, waiting for transfers between devices, local(): lax.all_to_all(context_heads, 'heads', split_axis=0, concat_axis=0, tiled...  20.6 us
    pallas_call x1, Pallas kernels, attention_forward(): pl.pallas_call(functools.partial(attention_forward_kernel, pieces), grid_...  20.5 us
  transfers between devices with their start and end apart: 50, of which 23 were waited for; matrix products, arithmetic and copies ran while one was open for 14% of the time, Pallas kernels for 31%

profile of v4, /device:TPU:0, one launch (start us, length us, event | category | flops | bytes accessed | tf_op | source)
XLA Modules:
  0.0 580.6 jit_solution(13162646714237518057)
XLA Ops:
  13.5 22.9 %collective-permute-done.refs_1_ = bf16[2,256,1024]{2,1,0:T(8,128)(2,1)S(1)} collective-permute-done((bf16[2,256,1024]{2,1,0:T(8,128)(2,1)}, bf16[2,256,1024]{2,1,0:T(8,128)(2,1)S(1)}, u32[]{:S(2)}, u32[]{:S(2)}) %collective-permute-start) | collective-permute-done | bytes 1048608 | tf_op jit(solution)/shard_map/ppermute | solution.py:578
  42.9 41.0 %all-to-all-done = bf16[4,32,3200]{2,1,0:T(8,128)(2,1)S(1)} async-done(((bf16[4,32,3200]{2,1,0:T(8,128)(2,1)}), bf16[4,32,3200]{2,1,0:T(8,128)(2,1)S(1)}, u32[]{:S(2)}, u32[]{:S(2)}) %all-to-all-start) | async-done | bytes 819232 | tf_op jit(solution)/shard_map/all_to_all | solution.py:657
  85.7 26.1 %collective-permute-done.2.refs_3_ = bf16[2,256,1024]{2,1,0:T(8,128)(2,1)S(1)} collective-permute-done((bf16[2,256,1024]{2,1,0:T(8,128)(2,1)}, bf16[2,256,1024]{2,1,0:T(8,128)(2,1)S(1)}, u32[]{:S(2)}, u32[]{:S(2)}) %collective-permute-start.2) | collective-permute-done | bytes 1048608 | tf_op jit(solution)/shard_map/ppermute | solution.py:578
  114.3 20.5 %attention_forward.1 = (bf16[2,1024,512]{2,1,0:T(8,128)(2,1)}, bf16[4,2,256,256]{3,2,1,0:T(8,128)(2,1)}, f32[2,2,8,1024]{3,2,1,0:T(8,128)}, bf16[4,2,256,1024]{3,2,1,0:T(8,128)(2,1)}) custom-call(s32[4]{0:T(128)} %and_select_fusion.place_ref, bf16[2,256,1024]{2,1,0:T(8,128)(2,1)} %refs_0_.1, bf16[2,256,1024]{2,1,0:T(8,128)(2,1)} %copy-done.19, ...), custom_call_target="tpu_custom_call" | custom-call | flops 1024 | bytes 1024 | tf_op jit(solution)/shard_map/attention_forward/pallas_call | solution.py:165
  143.2 20.6 %all-to-all-done.1 = bf16[4,2,256,256]{3,2,1,0:T(8,128)(2,1)S(1)} async-done(((bf16[4,2,256,256]{3,2,1,0:T(8,128)(2,1)}), bf16[4,2,256,256]{3,2,1,0:T(8,128)(2,1)S(1)}, u32[]{:S(2)}, u32[]{:S(2)}) %all-to-all-start.1) | async-done | bytes 1048608 | tf_op jit(solution)/shard_map/all_to_all | solution.py:718
  169.4 20.6 %collective-permute-done.4.refs_2_ = bf16[512,1024]{1,0:T(8,128)(2,1)} collective-permute-done((bf16[512,1024]{1,0:T(8,128)(2,1)}, bf16[512,1024]{1,0:T(8,128)(2,1)}, u32[]{:S(2)}, u32[]{:S(2)}) %collective-permute-start.4) | collective-permute-done | bytes 1048608 | tf_op jit(solution)/shard_map/ppermute | solution.py:578
  198.4 16.9 %collective-permute-done.5.refs_2_ = bf16[512,1024]{1,0:T(8,128)(2,1)} collective-permute-done((bf16[512,1024]{1,0:T(8,128)(2,1)}, bf16[512,1024]{1,0:T(8,128)(2,1)}, u32[]{:S(2)}, u32[]{:S(2)}) %collective-permute-start.5) | collective-permute-done | bytes 1048608 | tf_op jit(solution)/shard_map/ppermute | solution.py:578
  215.3 27.2 %collective-permute-done.8.refs_0_ = bf16[512,1152]{1,0:T(8,128)(2,1)} collective-permute-done((bf16[512,1152]{1,0:T(8,128)(2,1)}, bf16[512,1152]{1,0:T(8,128)(2,1)}, u32[]{:S(2)}, u32[]{:S(2)}) %collective-permute-start.8) | collective-permute-done | bytes 1179680 | tf_op jit(solution)/shard_map/ppermute | solution.py:578
  247.2 23.5 %experts.4 = (bf16[4,4,320,1024]{3,2,1,0:T(8,128)(2,1)}, bf16[4,4,320,1024]{3,2,1,0:T(8,128)(2,1)}, bf16[4,4,320,512]{3,2,1,0:T(8,128)(2,1)}, bf16[4,4,320,1024]...) custom-call(s32[4]{0:T(128)} %multiply_add_fusion.1.ids_ref, ...), custom_call_target="tpu_custom_call" | custom-call | flops 8724152320 | bytes 20971520 | tf_op jit(solution)/shard_map/experts/pallas_call | solution.py:397
  280.3 23.4 %experts.5 = (bf16[4,4,320,1024]{3,2,1,0:T(8,128)(2,1)}, bf16[4,4,320,1024]{3,2,1,0:T(8,128)(2,1)}, bf16[4,4,320,512]{3,2,1,0:T(8,128)(2,1)}, bf16[4,4,320,1024]...) custom-call(s32[4]{0:T(128)} %multiply_add_fusion.1.ids_ref, ...), custom_call_target="tpu_custom_call", output_to_operand_aliasing={{0}: (7, {}), {1}: (8, {}), {2}: (9, {}), {3}: (10, {})} | custom-call | flops 8724152320 | bytes 20971520 | tf_op jit(solution)/shard_map/experts/pallas_call | solution.py:397
  307.6 23.5 %experts.6 = (bf16[4,4,320,1024]{3,2,1,0:T(8,128)(2,1)}, bf16[4,4,320,1024]{3,2,1,0:T(8,128)(2,1)}, bf16[4,4,320,512]{3,2,1,0:T(8,128)(2,1)}, bf16[4,4,320,1024]...) custom-call(s32[4]{0:T(128)} %multiply_add_fusion.1.ids_ref, ...), custom_call_target="tpu_custom_call", output_to_operand_aliasing={{0}: (7, {}), {1}: (8, {}), {2}: (9, {}), {3}: (10, {})} | custom-call | flops 8724152320 | bytes 20971520 | tf_op jit(solution)/shard_map/experts/pallas_call | solution.py:397
  334.8 23.2 %experts.7 = (bf16[4,4,320,1024]{3,2,1,0:T(8,128)(2,1)}, bf16[4,4,320,1024]{3,2,1,0:T(8,128)(2,1)}, bf16[4,4,320,512]{3,2,1,0:T(8,128)(2,1)}, bf16[4,4,320,1024]...) custom-call(s32[4]{0:T(128)} %multiply_add_fusion.1.ids_ref, ...), custom_call_target="tpu_custom_call", output_to_operand_aliasing={{0}: (7, {}), {1}: (8, {}), {2}: (9, {}), {3}: (10, {})} | custom-call | flops 8724152320 | bytes 20971520 | tf_op jit(solution)/shard_map/experts/pallas_call | solution.py:397
  358.6 5.2 collective-permute-done.25
  370.0 20.4 %expert_grads.2 = (f32[1024,1024]{1,0:T(8,128)}, bf16[2,512,1024]{2,1,0:T(8,128)(2,1)}, bf16[2,512,1024]{2,1,0:T(8,128)(2,1)}, f32[512,1024]{1,0:T(8,128)}, f32[512,1024]{1,0:T(8,128)}) custom-call(s32[4]{0:T(128)} %iota_xor_fusion.order_ref, bf16[4,1280,1024]{2,1,0:T(8,128)(2,1)} %bitcast.127, bf16[4,1280,1024]{2,1,0:T(8,128)(2,1)} %bitcast.129), custom_call_target="tpu_custom_call" | custom-call | flops 1024 | bytes 1024 | tf_op jit(solution)/shard_map/expert_grads/pallas_call | solution.py:513
  403.6 12.8 %expert_grads.3 = (f32[1024,512]{1,0:T(8,128)}, bf16[2,512,512]{2,1,0:T(8,128)(2,1)}, bf16[2,512,512]{2,1,0:T(8,128)(2,1)}, f32[512,512]{1,0:T(8,128)}, f32[512,512]{1,0:T(8,128)}) custom-call(s32[4]{0:T(128)} %iota_xor_fusion.order_ref, bf16[4,1280,1024]{2,1,0:T(8,128)(2,1)} %bitcast.128, bf16[4,1280,512]{2,1,0:T(8,128)(2,1)} %bitcast.130), custom_call_target="tpu_custom_call" | custom-call | flops 1024 | bytes 1024 | tf_op jit(solution)/shard_map/expert_grads/pallas_call | solution.py:513
  428.3 6.0 %cut_rows.1.filled_ref = bf16[8,4,32,1664]{3,2,1,0:T(8,128)(2,1)} custom-call(bf16[4,512,256]{2,1,0:T(8,128)(2,1)} %bitcast.144, bf16[512,1024]{1,0:T(8,128)(2,1)} %copy-done.29, bf16[512,1024]{1,0:T(8,128)(2,1)} %copy-done.1, f32[512,128]{1,0:T(8,128)} %concatenate.24.logits_ref, f32[1024,1]{1,0:T(8,128)} %copy.59.gain_ref), custom_call_target="tpu_custom_call" | custom-call | flops 3489660928 | bytes 8912896 | tf_op jit(solution)/shard_map/cut_rows/pallas_call | solution.py:454
  434.4 4.4 collective-permute-done.28
  442.9 7.6 %all-to-all-done.2.grad_ref = bf16[4,2,256,256]{3,2,1,0:T(8,128)(2,1)} async-done(((bf16[4,2,256,256]{3,2,1,0:T(8,128)(2,1)}), bf16[4,2,256,256]{3,2,1,0:T(8,128)(2,1)}, u32[]{:S(2)}, u32[]{:S(2)}) %all-to-all-start.2) | async-done | bytes 1048608 | tf_op jit(solution)/shard_map/all_to_all | solution.py:807
  450.8 27.1 %attention_backward.1 = (bf16[4,2,256,512]{3,2,1,0:T(8,128)(2,1)}, bf16[8,4,32,1664]{3,2,1,0:T(8,128)(2,1)}) custom-call(bf16[2,1024,512]{2,1,0:T(8,128)(2,1)} %get-tuple-element.156.packed_ref, f32[2,2,8,1024]{3,2,1,0:T(8,128)} %get-tuple-element.157.lse_ref, bf16[4,2,256,256]{3,2,1,0:T(8,128)(2,1)} %all-to-all-done.2.grad_ref, ...), custom_call_target="tpu_custom_call", output_to_operand_aliasing={{1}: (6, {})} | custom-call | flops 1024 | bytes 1024 | tf_op jit(solution)/shard_map/attention_backward/pallas_call | solution.py:282
  477.9 5.0 all-to-all-start.3
  494.0 15.9 %collective-permute-done.35 = bf16[2,512,512]{2,1,0:T(8,128)(2,1)S(1)} collective-permute-done((bf16[2,512,512]{2,1,0:T(8,128)(2,1)}, bf16[2,512,512]{2,1,0:T(8,128)(2,1)S(1)}, u32[]{:S(2)}, u32[]{:S(2)}) %collective-permute-start.35) | collective-permute-done | bytes 1048608 | tf_op jit(solution)/shard_map/ppermute | solution.py:618
  517.9 12.3 %all-to-all-done.3 = bf16[4,2,256,512]{3,2,1,0:T(8,128)(2,1)} async-done(((bf16[4,2,256,512]{3,2,1,0:T(8,128)(2,1)}), bf16[4,2,256,512]{3,2,1,0:T(8,128)(2,1)}, u32[]{:S(2)}, u32[]{:S(2)}) %all-to-all-start.3) | async-done | bytes 2097184 | tf_op jit(solution)/shard_map/all_to_all | solution.py:844
  540.5 9.3 %reduce-scatter.2.cloned.1.call-done = bf16[128,1664]{1,0:T(8,128)(2,1)} async-done(((bf16[1024,1664]{1,0:T(8,128)(2,1)}), bf16[128,1664]{1,0:T(8,128)(2,1)}) %reduce-scatter.2.cloned.1.call-update) | async-done | bytes 426000 | tf_op jit(solution)/shard_map/reduce_scatter | solution.py:621
  549.8 4.9 all-to-all-start.4
  (243 shorter events, 144.9 us)
Async XLA Ops:
  7.2 77.5 %all-gather.6.cloned.1.call-start = ((), (), s32[]{:S(2)}) async-start(), calls=%async_computation.6 | async-start | bytes 5242880 | tf_op jit(solution)/shard_map/all_gather | solution.py:665
  37.4 46.5 %all-to-all-start = ((bf16[4,32,3200]{2,1,0:T(8,128)(2,1)}), bf16[4,32,3200]{2,1,0:T(8,128)(2,1)S(1)}, u32[]{:S(2)}, u32[]{:S(2)}) async-start(bf16[4,32,3200]{2,1,0:T(8,128)(2,1)} %broadcast_in_dim.24), calls=%async_computation | async-start | bytes 1638400 | tf_op jit(solution)/shard_map/all_to_all | solution.py:657
  40.9 70.9 %all-gather.8.cloned.1.call-start = ((), (), s32[]{:S(2)}) async-start(), calls=%async_computation.7 | async-start | bytes 1474560 | tf_op jit(solution)/shard_map/all_gather | solution.py:668
  41.0 43.7 %collective-permute-start.1 = (bf16[2,256,1024]{2,1,0:T(8,128)(2,1)S(1)}, bf16[2,256,1024]{2,1,0:T(8,128)(2,1)}, u32[]{:S(2)}, u32[]{:S(2)}) collective-permute-start(bf16[2,256,1024]{2,1,0:T(8,128)(2,1)S(1)} %collective-permute-done.refs_1_), channel_id=1, source_target_pairs={{0,8},{8,16},{16,24},{24,0},{1,9},{9,17},{17,25},{25,1},{2,10},{10... | collective-permute-start | bytes 3145736 | tf_op jit(solution)/shard_map/ppermute | solution.py:578
  84.7 57.3 %all-gather.10.cloned.1.call-start = ((), (), s32[]{:S(2)}) async-start(), calls=%async_computation.8 | async-start | bytes 2654208 | tf_op jit(solution)/shard_map/all_gather | solution.py:668
  85.5 161.7 %all-gather.12.cloned.1.call-start = ((), (), s32[]{:S(2)}) async-start(), calls=%async_computation.9 | async-start | bytes 10485760 | tf_op jit(solution)/shard_map/all_gather | solution.py:691
  140.5 255.9 %all-gather.14.cloned.1.call-start = ((), (), s32[]{:S(2)}) async-start(), calls=%async_computation.10 | async-start | bytes 4718592 | tf_op jit(solution)/shard_map/all_gather | solution.py:668
  243.6 30.2 %collective-permute-start.9 = (bf16[512,1152]{1,0:T(8,128)(2,1)}, bf16[512,1152]{1,0:T(8,128)(2,1)}, u32[]{:S(2)}, u32[]{:S(2)}) collective-permute-start(bf16[512,1152]{1,0:T(8,128)(2,1)} %collective-permute-done.8.refs_0_), channel_id=1, source_target_pairs={{0,8},{8,16},{16,24},{24,0},{1,9},{9,17},{17,25},{25,1},{2,10},{10... | collective-permute-start | bytes 3538952 | tf_op jit(solution)/shard_map/ppermute | solution.py:578
  275.1 28.9 %collective-permute-start.7 = (bf16[512,1024]{1,0:T(8,128)(2,1)}, bf16[512,1024]{1,0:T(8,128)(2,1)S(1)}, u32[]{:S(2)}, u32[]{:S(2)}) collective-permute-start(bf16[512,1024]{1,0:T(8,128)(2,1)} %bitcast.146), channel_id=1, source_target_pairs={{0,1},{1,0},{2,3},{3,2},{4,5},{5,4},{6,7},{7,6},{8,9},{9,8},{10,11... | collective-permute-start | bytes 3145736 | tf_op jit(solution)/shard_map/ppermute | solution.py:581
  275.2 31.3 %collective-permute-start.6 = (bf16[512,1152]{1,0:T(8,128)(2,1)}, bf16[512,1152]{1,0:T(8,128)(2,1)S(1)}, u32[]{:S(2)}, u32[]{:S(2)}) collective-permute-start(bf16[512,1152]{1,0:T(8,128)(2,1)} %concatenate.23.refs_0_), channel_id=1, source_target_pairs={{0,1},{1,0},{2,3},{3,2},{4,5},{5,4},{6,7},{7,6},{8,9},{9,8},{10,11... | collective-permute-start | bytes 3538952 | tf_op jit(solution)/shard_map/ppermute | solution.py:581
  275.7 30.8 %collective-permute-start.16 = (bf16[512,1152]{1,0:T(8,128)(2,1)}, bf16[512,1152]{1,0:T(8,128)(2,1)S(1)}, u32[]{:S(2)}, u32[]{:S(2)}) collective-permute-start(bf16[512,1152]{1,0:T(8,128)(2,1)} %collective-permute-done.9.refs_0_), channel_id=1, source_target_pairs={{0,8},{8,16},{16,24},{24,0},{1,9},{9,17},{17,25},{25,1},{2,10},{10... | collective-permute-start | bytes 3538952 | tf_op jit(solution)/shard_map/ppermute | solution.py:578
  279.9 51.1 %collective-permute-start.18 = (bf16[512,1152]{1,0:T(8,128)(2,1)S(1)}, bf16[512,1152]{1,0:T(8,128)(2,1)}, u32[]{:S(2)}, u32[]{:S(2)}) collective-permute-start(bf16[512,1152]{1,0:T(8,128)(2,1)S(1)} %add_convert_fusion.2), channel_id=1, source_target_pairs={{0,8},{8,16},{16,24},{24,0},{1,9},{9,17},{17,25},{25,1},{2,10},{10... | collective-permute-start | bytes 3538952 | tf_op jit(solution)/shard_map/ppermute | solution.py:578
  304.0 29.7 %collective-permute-start.20 = (bf16[512,1024]{1,0:T(8,128)(2,1)}, bf16[512,1024]{1,0:T(8,128)(2,1)}, u32[]{:S(2)}, u32[]{:S(2)}) collective-permute-start(bf16[512,1024]{1,0:T(8,128)(2,1)} %collective-permute-done.5.refs_2_), channel_id=1, source_target_pairs={{0,1},{1,0},{2,3},{3,2},{4,5},{5,4},{6,7},{7,6},{8,9},{9,8},{10,11... | collective-permute-start | bytes 3145736 | tf_op jit(solution)/shard_map/ppermute | solution.py:581
  333.5 30.3 %collective-permute-start.25 = (bf16[512,1152]{1,0:T(8,128)(2,1)S(1)}, bf16[512,1152]{1,0:T(8,128)(2,1)S(1)}, u32[]{:S(2)}, u32[]{:S(2)}) collective-permute-start(bf16[512,1152]{1,0:T(8,128)(2,1)S(1)} %add_convert_fusion.1), channel_id=1, source_target_pairs={{0,8},{8,16},{16,24},{24,0},{1,9},{9,17},{17,25},{25,1},{2,10},{10... | collective-permute-start | bytes 3538952 | tf_op jit(solution)/shard_map/ppermute | solution.py:578
  366.5 29.6 %collective-permute-start.26 = (bf16[512,1152]{1,0:T(8,128)(2,1)}, bf16[512,1152]{1,0:T(8,128)(2,1)}, u32[]{:S(2)}, u32[]{:S(2)}) collective-permute-start(bf16[512,1152]{1,0:T(8,128)(2,1)} %add_convert_fusion), channel_id=1, source_target_pairs={{0,8},{8,16},{16,24},{24,0},{1,9},{9,17},{17,25},{25,1},{2,10},{10... | collective-permute-start | bytes 3538952 | tf_op jit(solution)/shard_map/ppermute | solution.py:578
  366.5 29.9 %collective-permute-start.30 = (bf16[512,1152]{1,0:T(8,128)(2,1)}, bf16[512,1152]{1,0:T(8,128)(2,1)}, u32[]{:S(2)}, u32[]{:S(2)}) collective-permute-start(bf16[512,1152]{1,0:T(8,128)(2,1)} %get-tuple-element.138), channel_id=1, source_target_pairs={{0,1},{1,0},{2,3},{3,2},{4,5},{5,4},{6,7},{7,6},{8,9},{9,8},{10,11... | collective-permute-start | bytes 3538952 | tf_op jit(solution)/shard_map/ppermute | solution.py:581
  390.4 48.4 %collective-permute-start.28 = (bf16[2,512,1024]{2,1,0:T(8,128)(2,1)}, bf16[2,512,1024]{2,1,0:T(8,128)(2,1)}, u32[]{:S(2)}, u32[]{:S(2)}) collective-permute-start(bf16[2,512,1024]{2,1,0:T(8,128)(2,1)} %get-tuple-element.135), channel_id=1, source_target_pairs={{0,2},{2,0},{4,6},{6,4},{1,3},{3,1},{5,7},{7,5},{8,10},{10,8},{12,... | collective-permute-start | bytes 6291464 | tf_op jit(solution)/shard_map/ppermute | solution.py:618
  391.7 48.1 %collective-permute-start.29 = (bf16[2,512,1024]{2,1,0:T(8,128)(2,1)}, bf16[2,512,1024]{2,1,0:T(8,128)(2,1)}, u32[]{:S(2)}, u32[]{:S(2)}) collective-permute-start(bf16[2,512,1024]{2,1,0:T(8,128)(2,1)} %get-tuple-element.136), channel_id=1, source_target_pairs={{0,4},{2,6},{4,0},{6,2},{1,5},{3,7},{5,1},{7,3},{8,12},{10,14},{12... | collective-permute-start | bytes 6291464 | tf_op jit(solution)/shard_map/ppermute | solution.py:618
  477.9 52.3 %all-to-all-start.3 = ((bf16[4,2,256,512]{3,2,1,0:T(8,128)(2,1)}), bf16[4,2,256,512]{3,2,1,0:T(8,128)(2,1)}, u32[]{:S(2)}, u32[]{:S(2)}) async-start(bf16[4,2,256,512]{3,2,1,0:T(8,128)(2,1)} %get-tuple-element.162), calls=%async_computation.3 | async-start | bytes 4194304 | tf_op jit(solution)/shard_map/all_to_all | solution.py:844
  483.0 66.8 %reduce-scatter.2.cloned.1.call-start = ((), (), s32[]{:S(2)}) async-start(), calls=%async_computation.11 | async-start | bytes 3833856 | tf_op jit(solution)/shard_map/reduce_scatter | solution.py:621
  490.3 68.9 %collective-permute-start.33 = (bf16[512,1024]{1,0:T(8,128)(2,1)}, bf16[512,1024]{1,0:T(8,128)(2,1)}, u32[]{:S(2)}, u32[]{:S(2)}) collective-permute-start(bf16[512,1024]{1,0:T(8,128)(2,1)} %fusion.2), channel_id=1, source_target_pairs={{0,4},{2,6},{4,0},{6,2},{1,5},{3,7},{5,1},{7,3},{8,12},{10,14},{12... | collective-permute-start | bytes 3145736 | tf_op jit(solution)/shard_map/ppermute | solution.py:618
  493.4 65.8 %collective-permute-start.34 = (bf16[512,1024]{1,0:T(8,128)(2,1)}, bf16[512,1024]{1,0:T(8,128)(2,1)}, u32[]{:S(2)}, u32[]{:S(2)}) collective-permute-start(bf16[512,1024]{1,0:T(8,128)(2,1)} %fusion.1), channel_id=1, source_target_pairs={{0,2},{2,0},{4,6},{6,4},{1,3},{3,1},{5,7},{7,5},{8,10},{10,8},{12,... | collective-permute-start | bytes 3145736 | tf_op jit(solution)/shard_map/ppermute | solution.py:618
  511.0 45.3 %collective-permute-start.36 = (bf16[512,512]{1,0:T(8,128)(2,1)}, bf16[512,512]{1,0:T(8,128)(2,1)}, u32[]{:S(2)}, u32[]{:S(2)}) collective-permute-start(bf16[512,512]{1,0:T(8,128)(2,1)} %fusion.28), channel_id=1, source_target_pairs={{0,4},{2,6},{4,0},{6,2},{1,5},{3,7},{5,1},{7,3},{8,12},{10,14},{12... | collective-permute-start | bytes 1572872 | tf_op jit(solution)/shard_map/ppermute | solution.py:618
  513.5 42.8 %collective-permute-start.38 = (bf16[512,512]{1,0:T(8,128)(2,1)}, bf16[512,512]{1,0:T(8,128)(2,1)}, u32[]{:S(2)}, u32[]{:S(2)}) collective-permute-start(bf16[512,512]{1,0:T(8,128)(2,1)} %fusion.27), channel_id=1, source_target_pairs={{0,2},{2,0},{4,6},{6,4},{1,3},{3,1},{5,7},{7,5},{8,10},{10,8},{12,... | collective-permute-start | bytes 1572872 | tf_op jit(solution)/shard_map/ppermute | solution.py:618
  (61 other events, 892.5 us)
Sparse Core Ops, SparseCore 0:
  9.9 55.3 all-gather.5
  84.8 22.5 all-gather.7
  109.3 29.0 all-gather.9
  140.1 87.6 all-gather.11
  275.2 35.4 all-gather.13
  486.9 62.8 reduce-scatter.1

commit v5 on v4

--- a/solution.py
+++ b/solution.py
@@ -841,6 +841,7 @@
                 )
             if chunk < n_heads - 1:
                 mix_received = onward(after(mix_moving, grad_context_heads))
+        grad_before, near_out = lax.optimization_barrier((grad_before, near_out))
         grad_mine = lax.all_to_all(
             after(grad_before, mix_received), "heads", split_axis=0, concat_axis=0, tiled=True
         ).reshape(n_heads, token_rows, own_columns)
@@ -857,7 +858,7 @@
         grad_state_norm, _ = norm_back(grad_normed_attn, state, norm_factor(state), gain_one)
         grad_tokens = (grad_mid + grad_state_norm).astype(jnp.bfloat16).reshape(tokens.shape)
         if near:
-            grad_expert_in = finished(parts_in, near, after(far_in, mix_last))
+            grad_expert_in = finished(parts_in, near, after(far_in, grad_tokens))
             grad_expert_out = finished(parts_out, near_out, after(far_out, mix_last))
         else:
             grad_expert_in, grad_expert_out = [

time: 589 us -> 585 us (level)
  waiting for transfers between devices: 253 us -> 247 us
    all_to_all x1, waiting for transfers between devices: 12.3 us -> 29.5 us  [local(): lax.all_to_all(after(grad_before, mix_received), 'heads', split_axis=0, c...]
    ppermute x8, waiting for transfers between devices: 22.9 us -> 7.34 us  [paired(): return lax.ppermute(value, 'chip', [(i, i ^ other) for i in range(chip)])]
    reduce_scatter x1, waiting for transfers between devices: 9.32 us -> 0.01 us  [spread_rows(): lax.psum_scatter(cut.reshape(-1, cut.shape[3]), ('chip', 'core'), scatter...]
  transfers between devices with their start and end apart: 50 -> 50, of which waited for: 23 -> 22; matrix products, arithmetic and copies ran while one was open for 14% -> 15% of each run, Pallas kernels for 31% -> 31%
where the time goes in v5:
time: 585 us; the launch traced here: 576 us
  waiting for transfers between devices  247 us (42%)
  Pallas kernels  180 us (31%)
  other arithmetic  55.8 us (10%)
  starting transfers between devices  41.4 us (7%)
  local copies, waits for them, and re-layouts  18.6 us (3%)
  matrix products  18.2 us (3%)
  between operations  15.4 us (3%)
    ppermute x15, waiting for transfers between devices, onward(): return lax.ppermute(value, 'heads', ring)  134 us
    pallas_call x4, Pallas kernels, experts(): pl.pallas_call(functools.partial(expert_kernel, sources, n_local, len(kep...  93.5 us
    all_to_all x1, waiting for transfers between devices, local(): lax.all_to_all(jnp.broadcast_to(after(small, rings[1])[None], (n_heads,)...  41 us
    pallas_call x2, Pallas kernels, expert_grads(): pl.pallas_call(expert_grads_kernel, grid_spec=pltpu.PrefetchScalarGridSpe...  33.2 us
    all_to_all x1, waiting for transfers between devices, local(): lax.all_to_all(after(grad_before, mix_received), 'heads', split_axis=0, c...  29.5 us
    pallas_call x1, Pallas kernels, attention_backward(): pl.pallas_call(attention_backward_kernel, grid=(groups_local, slots), in_...  27.1 us
    all_to_all x1, waiting for transfers between devices, local(): lax.all_to_all(context_heads, 'heads', split_axis=0, concat_axis=0, tiled...  20.6 us
    pallas_call x1, Pallas kernels, attention_forward(): pl.pallas_call(functools.partial(attention_forward_kernel, pieces), grid_...  20.5 us
  transfers between devices with their start and end apart: 50, of which 22 were waited for; matrix products, arithmetic and copies ran while one was open for 15% of the time, Pallas kernels for 31%

profile of v5, /device:TPU:0, one launch (start us, length us, event | category | flops | bytes accessed | tf_op | source)
XLA Modules:
  0.0 576.5 jit_solution(15627157669609569791)
XLA Ops:
  13.5 22.9 %collective-permute-done.refs_1_ = bf16[2,256,1024]{2,1,0:T(8,128)(2,1)S(1)} collective-permute-done((bf16[2,256,1024]{2,1,0:T(8,128)(2,1)}, bf16[2,256,1024]{2,1,0:T(8,128)(2,1)S(1)}, u32[]{:S(2)}, u32[]{:S(2)}) %collective-permute-start) | collective-permute-done | bytes 1048608 | tf_op jit(solution)/shard_map/ppermute | solution.py:578
  42.9 41.0 %all-to-all-done = bf16[4,32,3200]{2,1,0:T(8,128)(2,1)S(1)} async-done(((bf16[4,32,3200]{2,1,0:T(8,128)(2,1)}), bf16[4,32,3200]{2,1,0:T(8,128)(2,1)S(1)}, u32[]{:S(2)}, u32[]{:S(2)}) %all-to-all-start) | async-done | bytes 819232 | tf_op jit(solution)/shard_map/all_to_all | solution.py:657
  85.6 26.1 %collective-permute-done.2.refs_3_ = bf16[2,256,1024]{2,1,0:T(8,128)(2,1)S(1)} collective-permute-done((bf16[2,256,1024]{2,1,0:T(8,128)(2,1)}, bf16[2,256,1024]{2,1,0:T(8,128)(2,1)S(1)}, u32[]{:S(2)}, u32[]{:S(2)}) %collective-permute-start.2) | collective-permute-done | bytes 1048608 | tf_op jit(solution)/shard_map/ppermute | solution.py:578
  114.3 20.5 %attention_forward.1 = (bf16[2,1024,512]{2,1,0:T(8,128)(2,1)}, bf16[4,2,256,256]{3,2,1,0:T(8,128)(2,1)}, f32[2,2,8,1024]{3,2,1,0:T(8,128)}, bf16[4,2,256,1024]{3,2,1,0:T(8,128)(2,1)}) custom-call(s32[4]{0:T(128)} %and_select_fusion.place_ref, bf16[2,256,1024]{2,1,0:T(8,128)(2,1)} %refs_0_.1, bf16[2,256,1024]{2,1,0:T(8,128)(2,1)} %copy-done.19, ...), custom_call_target="tpu_custom_call" | custom-call | flops 1024 | bytes 1024 | tf_op jit(solution)/shard_map/attention_forward/pallas_call | solution.py:165
  143.2 20.6 %all-to-all-done.1 = bf16[4,2,256,256]{3,2,1,0:T(8,128)(2,1)S(1)} async-done(((bf16[4,2,256,256]{3,2,1,0:T(8,128)(2,1)}), bf16[4,2,256,256]{3,2,1,0:T(8,128)(2,1)S(1)}, u32[]{:S(2)}, u32[]{:S(2)}) %all-to-all-start.1) | async-done | bytes 1048608 | tf_op jit(solution)/shard_map/all_to_all | solution.py:718
  169.4 20.6 %collective-permute-done.4.refs_2_ = bf16[512,1024]{1,0:T(8,128)(2,1)} collective-permute-done((bf16[512,1024]{1,0:T(8,128)(2,1)}, bf16[512,1024]{1,0:T(8,128)(2,1)}, u32[]{:S(2)}, u32[]{:S(2)}) %collective-permute-start.4) | collective-permute-done | bytes 1048608 | tf_op jit(solution)/shard_map/ppermute | solution.py:578
  198.4 16.9 %collective-permute-done.5.refs_2_ = bf16[512,1024]{1,0:T(8,128)(2,1)} collective-permute-done((bf16[512,1024]{1,0:T(8,128)(2,1)}, bf16[512,1024]{1,0:T(8,128)(2,1)}, u32[]{:S(2)}, u32[]{:S(2)}) %collective-permute-start.5) | collective-permute-done | bytes 1048608 | tf_op jit(solution)/shard_map/ppermute | solution.py:578
  215.3 27.2 %collective-permute-done.8.refs_0_ = bf16[512,1152]{1,0:T(8,128)(2,1)} collective-permute-done((bf16[512,1152]{1,0:T(8,128)(2,1)}, bf16[512,1152]{1,0:T(8,128)(2,1)}, u32[]{:S(2)}, u32[]{:S(2)}) %collective-permute-start.8) | collective-permute-done | bytes 1179680 | tf_op jit(solution)/shard_map/ppermute | solution.py:578
  247.2 23.5 %experts.4 = (bf16[4,4,320,1024]{3,2,1,0:T(8,128)(2,1)}, bf16[4,4,320,1024]{3,2,1,0:T(8,128)(2,1)}, bf16[4,4,320,512]{3,2,1,0:T(8,128)(2,1)}, bf16[4,4,320,1024]...) custom-call(s32[4]{0:T(128)} %multiply_add_fusion.1.ids_ref, ...), custom_call_target="tpu_custom_call" | custom-call | flops 8724152320 | bytes 20971520 | tf_op jit(solution)/shard_map/experts/pallas_call | solution.py:397
  280.3 23.4 %experts.5 = (bf16[4,4,320,1024]{3,2,1,0:T(8,128)(2,1)}, bf16[4,4,320,1024]{3,2,1,0:T(8,128)(2,1)}, bf16[4,4,320,512]{3,2,1,0:T(8,128)(2,1)}, bf16[4,4,320,1024]...) custom-call(s32[4]{0:T(128)} %multiply_add_fusion.1.ids_ref, ...), custom_call_target="tpu_custom_call", output_to_operand_aliasing={{0}: (7, {}), {1}: (8, {}), {2}: (9, {}), {3}: (10, {})} | custom-call | flops 8724152320 | bytes 20971520 | tf_op jit(solution)/shard_map/experts/pallas_call | solution.py:397
  307.6 23.4 %experts.6 = (bf16[4,4,320,1024]{3,2,1,0:T(8,128)(2,1)}, bf16[4,4,320,1024]{3,2,1,0:T(8,128)(2,1)}, bf16[4,4,320,512]{3,2,1,0:T(8,128)(2,1)}, bf16[4,4,320,1024]...) custom-call(s32[4]{0:T(128)} %multiply_add_fusion.1.ids_ref, ...), custom_call_target="tpu_custom_call", output_to_operand_aliasing={{0}: (7, {}), {1}: (8, {}), {2}: (9, {}), {3}: (10, {})} | custom-call | flops 8724152320 | bytes 20971520 | tf_op jit(solution)/shard_map/experts/pallas_call | solution.py:397
  334.8 23.2 %experts.7 = (bf16[4,4,320,1024]{3,2,1,0:T(8,128)(2,1)}, bf16[4,4,320,1024]{3,2,1,0:T(8,128)(2,1)}, bf16[4,4,320,512]{3,2,1,0:T(8,128)(2,1)}, bf16[4,4,320,1024]...) custom-call(s32[4]{0:T(128)} %multiply_add_fusion.1.ids_ref, ...), custom_call_target="tpu_custom_call", output_to_operand_aliasing={{0}: (7, {}), {1}: (8, {}), {2}: (9, {}), {3}: (10, {})} | custom-call | flops 8724152320 | bytes 20971520 | tf_op jit(solution)/shard_map/experts/pallas_call | solution.py:397
  358.5 5.2 collective-permute-done.25
  369.9 20.4 %expert_grads.2 = (f32[1024,1024]{1,0:T(8,128)}, bf16[2,512,1024]{2,1,0:T(8,128)(2,1)}, bf16[2,512,1024]{2,1,0:T(8,128)(2,1)}, f32[512,1024]{1,0:T(8,128)}, f32[512,1024]{1,0:T(8,128)}) custom-call(s32[4]{0:T(128)} %iota_xor_fusion.order_ref, bf16[4,1280,1024]{2,1,0:T(8,128)(2,1)} %bitcast.119, bf16[4,1280,1024]{2,1,0:T(8,128)(2,1)} %bitcast.121), custom_call_target="tpu_custom_call" | custom-call | flops 1024 | bytes 1024 | tf_op jit(solution)/shard_map/expert_grads/pallas_call | solution.py:513
  403.5 12.7 %expert_grads.3 = (f32[1024,512]{1,0:T(8,128)}, bf16[2,512,512]{2,1,0:T(8,128)(2,1)}, bf16[2,512,512]{2,1,0:T(8,128)(2,1)}, f32[512,512]{1,0:T(8,128)}, f32[512,512]{1,0:T(8,128)}) custom-call(s32[4]{0:T(128)} %iota_xor_fusion.order_ref, bf16[4,1280,1024]{2,1,0:T(8,128)(2,1)} %bitcast.120, bf16[4,1280,512]{2,1,0:T(8,128)(2,1)} %bitcast.122), custom_call_target="tpu_custom_call" | custom-call | flops 1024 | bytes 1024 | tf_op jit(solution)/shard_map/expert_grads/pallas_call | solution.py:513
  422.2 4.2 all-to-all-start.2
  428.3 6.1 %cut_rows.1.filled_ref = bf16[8,4,32,1664]{3,2,1,0:T(8,128)(2,1)} custom-call(bf16[4,512,256]{2,1,0:T(8,128)(2,1)} %bitcast.136, bf16[512,1024]{1,0:T(8,128)(2,1)} %copy-done.27, bf16[512,1024]{1,0:T(8,128)(2,1)} %copy-done.1, f32[512,128]{1,0:T(8,128)} %concatenate.24.logits_ref, f32[1024,1]{1,0:T(8,128)} %copy.59.gain_ref), custom_call_target="tpu_custom_call" | custom-call | flops 3489660928 | bytes 8912896 | tf_op jit(solution)/shard_map/cut_rows/pallas_call | solution.py:454
  434.4 4.4 collective-permute-done.28
  444.9 5.6 all-to-all-done.2.grad_ref
  450.8 27.1 %attention_backward.1 = (bf16[4,2,256,512]{3,2,1,0:T(8,128)(2,1)}, bf16[8,4,32,1664]{3,2,1,0:T(8,128)(2,1)}) custom-call(bf16[2,1024,512]{2,1,0:T(8,128)(2,1)} %get-tuple-element.159.packed_ref, f32[2,2,8,1024]{3,2,1,0:T(8,128)} %get-tuple-element.160.lse_ref, bf16[4,2,256,256]{3,2,1,0:T(8,128)(2,1)} %all-to-all-done.2.grad_ref, ...), custom_call_target="tpu_custom_call", output_to_operand_aliasing={{1}: (6, {})} | custom-call | flops 1024 | bytes 1024 | tf_op jit(solution)/shard_map/attention_backward/pallas_call | solution.py:282
  477.9 5.0 all-to-all-start.3
  500.6 29.5 %all-to-all-done.3 = bf16[4,2,256,512]{3,2,1,0:T(8,128)(2,1)} async-done(((bf16[4,2,256,512]{3,2,1,0:T(8,128)(2,1)}), bf16[4,2,256,512]{3,2,1,0:T(8,128)(2,1)}, u32[]{:S(2)}, u32[]{:S(2)}) %all-to-all-start.3) | async-done | bytes 2097184 | tf_op jit(solution)/shard_map/all_to_all | solution.py:845
  542.2 3.5 fusion.3
  548.0 5.0 all-to-all-start.4
  (239 shorter events, 143.0 us)
Async XLA Ops:
  7.2 77.5 %all-gather.6.cloned.1.call-start = ((), (), s32[]{:S(2)}) async-start(), calls=%async_computation.6 | async-start | bytes 5242880 | tf_op jit(solution)/shard_map/all_gather | solution.py:665
  37.4 46.5 %all-to-all-start = ((bf16[4,32,3200]{2,1,0:T(8,128)(2,1)}), bf16[4,32,3200]{2,1,0:T(8,128)(2,1)S(1)}, u32[]{:S(2)}, u32[]{:S(2)}) async-start(bf16[4,32,3200]{2,1,0:T(8,128)(2,1)} %broadcast_in_dim.24), calls=%async_computation | async-start | bytes 1638400 | tf_op jit(solution)/shard_map/all_to_all | solution.py:657
  40.9 70.8 %all-gather.8.cloned.1.call-start = ((), (), s32[]{:S(2)}) async-start(), calls=%async_computation.7 | async-start | bytes 1474560 | tf_op jit(solution)/shard_map/all_gather | solution.py:668
  41.0 43.7 %collective-permute-start.1 = (bf16[2,256,1024]{2,1,0:T(8,128)(2,1)S(1)}, bf16[2,256,1024]{2,1,0:T(8,128)(2,1)}, u32[]{:S(2)}, u32[]{:S(2)}) collective-permute-start(bf16[2,256,1024]{2,1,0:T(8,128)(2,1)S(1)} %collective-permute-done.refs_1_), channel_id=1, source_target_pairs={{0,8},{8,16},{16,24},{24,0},{1,9},{9,17},{17,25},{25,1},{2,10},{10... | collective-permute-start | bytes 3145736 | tf_op jit(solution)/shard_map/ppermute | solution.py:578
  84.7 57.2 %all-gather.10.cloned.1.call-start = ((), (), s32[]{:S(2)}) async-start(), calls=%async_computation.8 | async-start | bytes 2654208 | tf_op jit(solution)/shard_map/all_gather | solution.py:668
  85.5 161.7 %all-gather.12.cloned.1.call-start = ((), (), s32[]{:S(2)}) async-start(), calls=%async_computation.9 | async-start | bytes 10485760 | tf_op jit(solution)/shard_map/all_gather | solution.py:691
  140.5 255.9 %all-gather.14.cloned.1.call-start = ((), (), s32[]{:S(2)}) async-start(), calls=%async_computation.10 | async-start | bytes 4718592 | tf_op jit(solution)/shard_map/all_gather | solution.py:668
  243.5 30.2 %collective-permute-start.9 = (bf16[512,1152]{1,0:T(8,128)(2,1)}, bf16[512,1152]{1,0:T(8,128)(2,1)}, u32[]{:S(2)}, u32[]{:S(2)}) collective-permute-start(bf16[512,1152]{1,0:T(8,128)(2,1)} %collective-permute-done.8.refs_0_), channel_id=1, source_target_pairs={{0,8},{8,16},{16,24},{24,0},{1,9},{9,17},{17,25},{25,1},{2,10},{10... | collective-permute-start | bytes 3538952 | tf_op jit(solution)/shard_map/ppermute | solution.py:578
  275.2 31.3 %collective-permute-start.6 = (bf16[512,1152]{1,0:T(8,128)(2,1)}, bf16[512,1152]{1,0:T(8,128)(2,1)S(1)}, u32[]{:S(2)}, u32[]{:S(2)}) collective-permute-start(bf16[512,1152]{1,0:T(8,128)(2,1)} %concatenate.23.refs_0_), channel_id=1, source_target_pairs={{0,1},{1,0},{2,3},{3,2},{4,5},{5,4},{6,7},{7,6},{8,9},{9,8},{10,11... | collective-permute-start | bytes 3538952 | tf_op jit(solution)/shard_map/ppermute | solution.py:581
  275.7 30.8 %collective-permute-start.16 = (bf16[512,1152]{1,0:T(8,128)(2,1)}, bf16[512,1152]{1,0:T(8,128)(2,1)S(1)}, u32[]{:S(2)}, u32[]{:S(2)}) collective-permute-start(bf16[512,1152]{1,0:T(8,128)(2,1)} %collective-permute-done.9.refs_0_), channel_id=1, source_target_pairs={{0,8},{8,16},{16,24},{24,0},{1,9},{9,17},{17,25},{25,1},{2,10},{10... | collective-permute-start | bytes 3538952 | tf_op jit(solution)/shard_map/ppermute | solution.py:578
  279.9 51.1 %collective-permute-start.18 = (bf16[512,1152]{1,0:T(8,128)(2,1)S(1)}, bf16[512,1152]{1,0:T(8,128)(2,1)}, u32[]{:S(2)}, u32[]{:S(2)}) collective-permute-start(bf16[512,1152]{1,0:T(8,128)(2,1)S(1)} %add_convert_fusion.2), channel_id=1, source_target_pairs={{0,8},{8,16},{16,24},{24,0},{1,9},{9,17},{17,25},{25,1},{2,10},{10... | collective-permute-start | bytes 3538952 | tf_op jit(solution)/shard_map/ppermute | solution.py:578
  304.0 29.7 %collective-permute-start.20 = (bf16[512,1024]{1,0:T(8,128)(2,1)}, bf16[512,1024]{1,0:T(8,128)(2,1)}, u32[]{:S(2)}, u32[]{:S(2)}) collective-permute-start(bf16[512,1024]{1,0:T(8,128)(2,1)} %collective-permute-done.5.refs_2_), channel_id=1, source_target_pairs={{0,1},{1,0},{2,3},{3,2},{4,5},{5,4},{6,7},{7,6},{8,9},{9,8},{10,11... | collective-permute-start | bytes 3145736 | tf_op jit(solution)/shard_map/ppermute | solution.py:581
  333.4 30.3 %collective-permute-start.25 = (bf16[512,1152]{1,0:T(8,128)(2,1)S(1)}, bf16[512,1152]{1,0:T(8,128)(2,1)S(1)}, u32[]{:S(2)}, u32[]{:S(2)}) collective-permute-start(bf16[512,1152]{1,0:T(8,128)(2,1)S(1)} %add_convert_fusion.1), channel_id=1, source_target_pairs={{0,8},{8,16},{16,24},{24,0},{1,9},{9,17},{17,25},{25,1},{2,10},{10... | collective-permute-start | bytes 3538952 | tf_op jit(solution)/shard_map/ppermute | solution.py:578
  366.5 29.9 %collective-permute-start.30 = (bf16[512,1152]{1,0:T(8,128)(2,1)}, bf16[512,1152]{1,0:T(8,128)(2,1)}, u32[]{:S(2)}, u32[]{:S(2)}) collective-permute-start(bf16[512,1152]{1,0:T(8,128)(2,1)} %get-tuple-element.141), channel_id=1, source_target_pairs={{0,1},{1,0},{2,3},{3,2},{4,5},{5,4},{6,7},{7,6},{8,9},{9,8},{10,11... | collective-permute-start | bytes 3538952 | tf_op jit(solution)/shard_map/ppermute | solution.py:581
  390.4 48.4 %collective-permute-start.28 = (bf16[2,512,1024]{2,1,0:T(8,128)(2,1)}, bf16[2,512,1024]{2,1,0:T(8,128)(2,1)}, u32[]{:S(2)}, u32[]{:S(2)}) collective-permute-start(bf16[2,512,1024]{2,1,0:T(8,128)(2,1)} %get-tuple-element.138), channel_id=1, source_target_pairs={{0,2},{2,0},{4,6},{6,4},{1,3},{3,1},{5,7},{7,5},{8,10},{10,8},{12,... | collective-permute-start | bytes 6291464 | tf_op jit(solution)/shard_map/ppermute | solution.py:618
  391.6 48.1 %collective-permute-start.29 = (bf16[2,512,1024]{2,1,0:T(8,128)(2,1)}, bf16[2,512,1024]{2,1,0:T(8,128)(2,1)}, u32[]{:S(2)}, u32[]{:S(2)}) collective-permute-start(bf16[2,512,1024]{2,1,0:T(8,128)(2,1)} %get-tuple-element.139), channel_id=1, source_target_pairs={{0,4},{2,6},{4,0},{6,2},{1,5},{3,7},{5,1},{7,3},{8,12},{10,14},{12... | collective-permute-start | bytes 6291464 | tf_op jit(solution)/shard_map/ppermute | solution.py:618
  439.7 38.1 %collective-permute-start.32 = (bf16[2,512,512]{2,1,0:T(8,128)(2,1)}, bf16[2,512,512]{2,1,0:T(8,128)(2,1)}, u32[]{:S(2)}, u32[]{:S(2)}) collective-permute-start(bf16[2,512,512]{2,1,0:T(8,128)(2,1)} %get-tuple-element.165), channel_id=1, source_target_pairs={{0,2},{2,0},{4,6},{6,4},{1,3},{3,1},{5,7},{7,5},{8,10},{10,8},{12,... | collective-permute-start | bytes 3145736 | tf_op jit(solution)/shard_map/ppermute | solution.py:618
  440.5 37.4 %collective-permute-start.33 = (bf16[2,512,512]{2,1,0:T(8,128)(2,1)}, bf16[2,512,512]{2,1,0:T(8,128)(2,1)}, u32[]{:S(2)}, u32[]{:S(2)}) collective-permute-start(bf16[2,512,512]{2,1,0:T(8,128)(2,1)} %get-tuple-element.166), channel_id=1, source_target_pairs={{0,4},{2,6},{4,0},{6,2},{1,5},{3,7},{5,1},{7,3},{8,12},{10,14},{12... | collective-permute-start | bytes 3145736 | tf_op jit(solution)/shard_map/ppermute | solution.py:618
  477.9 52.3 %all-to-all-start.3 = ((bf16[4,2,256,512]{3,2,1,0:T(8,128)(2,1)}), bf16[4,2,256,512]{3,2,1,0:T(8,128)(2,1)}, u32[]{:S(2)}, u32[]{:S(2)}) async-start(bf16[4,2,256,512]{3,2,1,0:T(8,128)(2,1)} %get-tuple-element.168), calls=%async_computation.3 | async-start | bytes 4194304 | tf_op jit(solution)/shard_map/all_to_all | solution.py:845
  482.9 65.1 %reduce-scatter.2.cloned.1.call-start = ((), (), s32[]{:S(2)}) async-start(), calls=%async_computation.11 | async-start | bytes 3833856 | tf_op jit(solution)/shard_map/reduce_scatter | solution.py:621
  483.8 77.7 %collective-permute-start.15 = (bf16[512,1024]{1,0:T(8,128)(2,1)}, bf16[512,1024]{1,0:T(8,128)(2,1)}, u32[]{:S(2)}, u32[]{:S(2)}) collective-permute-start(bf16[512,1024]{1,0:T(8,128)(2,1)} %get-tuple-element.116), channel_id=1, source_target_pairs={{0,1},{1,0},{2,3},{3,2},{4,5},{5,4},{6,7},{7,6},{8,9},{9,8},{10,11... | collective-permute-start | bytes 3145736 | tf_op jit(solution)/shard_map/ppermute | solution.py:581
  487.7 53.0 %collective-permute-start.35 = (bf16[512,1024]{1,0:T(8,128)(2,1)}, bf16[512,1024]{1,0:T(8,128)(2,1)}, u32[]{:S(2)}, u32[]{:S(2)}) collective-permute-start(bf16[512,1024]{1,0:T(8,128)(2,1)} %fusion.2), channel_id=1, source_target_pairs={{0,4},{2,6},{4,0},{6,2},{1,5},{3,7},{5,1},{7,3},{8,12},{10,14},{12... | collective-permute-start | bytes 3145736 | tf_op jit(solution)/shard_map/ppermute | solution.py:618
  491.6 50.5 %collective-permute-start.36 = (bf16[512,1024]{1,0:T(8,128)(2,1)}, bf16[512,1024]{1,0:T(8,128)(2,1)}, u32[]{:S(2)}, u32[]{:S(2)}) collective-permute-start(bf16[512,1024]{1,0:T(8,128)(2,1)} %fusion.1), channel_id=1, source_target_pairs={{0,2},{2,0},{4,6},{6,4},{1,3},{3,1},{5,7},{7,5},{8,10},{10,8},{12,... | collective-permute-start | bytes 3145736 | tf_op jit(solution)/shard_map/ppermute | solution.py:618
  495.2 57.8 %collective-permute-start.37 = (bf16[512,512]{1,0:T(8,128)(2,1)}, bf16[512,512]{1,0:T(8,128)(2,1)}, u32[]{:S(2)}, u32[]{:S(2)}) collective-permute-start(bf16[512,512]{1,0:T(8,128)(2,1)} %fusion.28), channel_id=1, source_target_pairs={{0,4},{2,6},{4,0},{6,2},{1,5},{3,7},{5,1},{7,3},{8,12},{10,14},{12... | collective-permute-start | bytes 1572872 | tf_op jit(solution)/shard_map/ppermute | solution.py:618
  (59 other events, 840.6 us)
Sparse Core Ops, SparseCore 0:
  9.9 55.3 all-gather.5
  84.8 22.5 all-gather.7
  109.3 29.0 all-gather.9
  140.1 87.5 all-gather.11
  275.2 35.4 all-gather.13
  486.9 58.7 reduce-scatter.1

commit v6 on v5

--- a/solution.py
+++ b/solution.py
@@ -859,7 +859,7 @@
         grad_tokens = (grad_mid + grad_state_norm).astype(jnp.bfloat16).reshape(tokens.shape)
         if near:
             grad_expert_in = finished(parts_in, near, after(far_in, grad_tokens))
-            grad_expert_out = finished(parts_out, near_out, after(far_out, mix_last))
+            grad_expert_out = finished(parts_out, near_out, after(far_out, grad_tokens))
         else:
             grad_expert_in, grad_expert_out = [
                 lax.psum_scatter(

time: 585 us -> 596 us (1.019)
  waiting for transfers between devices: 247 us -> 253 us
    ppermute x15, waiting for transfers between devices: 134 us -> 141 us  [onward(): return lax.ppermute(value, 'heads', ring)]
where the time goes in v6:
time: 596 us; the launch traced here: 587 us
  waiting for transfers between devices  253 us (42%)
  Pallas kernels  180 us (30%)
  other arithmetic  61.2 us (10%)
  starting transfers between devices  40.7 us (7%)
  local copies, waits for them, and re-layouts  18.6 us (3%)
  matrix products  18.3 us (3%)
  between operations  15.3 us (3%)
    ppermute x15, waiting for transfers between devices, onward(): return lax.ppermute(value, 'heads', ring)  141 us
    pallas_call x4, Pallas kernels, experts(): pl.pallas_call(functools.partial(expert_kernel, sources, n_local, len(kep...  93.5 us
    all_to_all x1, waiting for transfers between devices, local(): lax.all_to_all(jnp.broadcast_to(after(small, rings[1])[None], (n_heads,)...  41 us
    pallas_call x2, Pallas kernels, expert_grads(): pl.pallas_call(expert_grads_kernel, grid_spec=pltpu.PrefetchScalarGridSpe...  33.1 us
    all_to_all x1, waiting for transfers between devices, local(): lax.all_to_all(after(grad_before, mix_received), 'heads', split_axis=0, c...  28.7 us
    pallas_call x1, Pallas kernels, attention_backward(): pl.pallas_call(attention_backward_kernel, grid=(groups_local, slots), in_...  27.1 us
    all_to_all x1, waiting for transfers between devices, local(): lax.all_to_all(context_heads, 'heads', split_axis=0, concat_axis=0, tiled...  20.6 us
    pallas_call x1, Pallas kernels, attention_forward(): pl.pallas_call(functools.partial(attention_forward_kernel, pieces), grid_...  20.5 us
  transfers between devices with their start and end apart: 50, of which 22 were waited for; matrix products, arithmetic and copies ran while one was open for 15% of the time, Pallas kernels for 31%

profile of v6, /device:TPU:0, one launch (start us, length us, event | category | flops | bytes accessed | tf_op | source)
XLA Modules:
  0.0 587.4 jit_solution(12795735987924080447)
XLA Ops:
  13.5 22.9 %collective-permute-done.refs_1_ = bf16[2,256,1024]{2,1,0:T(8,128)(2,1)S(1)} collective-permute-done((bf16[2,256,1024]{2,1,0:T(8,128)(2,1)}, bf16[2,256,1024]{2,1,0:T(8,128)(2,1)S(1)}, u32[]{:S(2)}, u32[]{:S(2)}) %collective-permute-start) | collective-permute-done | bytes 1048608 | tf_op jit(solution)/shard_map/ppermute | solution.py:578
  42.9 41.0 %all-to-all-done = bf16[4,32,3200]{2,1,0:T(8,128)(2,1)S(1)} async-done(((bf16[4,32,3200]{2,1,0:T(8,128)(2,1)}), bf16[4,32,3200]{2,1,0:T(8,128)(2,1)S(1)}, u32[]{:S(2)}, u32[]{:S(2)}) %all-to-all-start) | async-done | bytes 819232 | tf_op jit(solution)/shard_map/all_to_all | solution.py:657
  85.6 26.1 %collective-permute-done.2.refs_3_ = bf16[2,256,1024]{2,1,0:T(8,128)(2,1)S(1)} collective-permute-done((bf16[2,256,1024]{2,1,0:T(8,128)(2,1)}, bf16[2,256,1024]{2,1,0:T(8,128)(2,1)S(1)}, u32[]{:S(2)}, u32[]{:S(2)}) %collective-permute-start.2) | collective-permute-done | bytes 1048608 | tf_op jit(solution)/shard_map/ppermute | solution.py:578
  114.3 20.5 %attention_forward.1 = (bf16[2,1024,512]{2,1,0:T(8,128)(2,1)}, bf16[4,2,256,256]{3,2,1,0:T(8,128)(2,1)}, f32[2,2,8,1024]{3,2,1,0:T(8,128)}, bf16[4,2,256,1024]{3,2,1,0:T(8,128)(2,1)}) custom-call(s32[4]{0:T(128)} %and_select_fusion.place_ref, bf16[2,256,1024]{2,1,0:T(8,128)(2,1)} %refs_0_.1, bf16[2,256,1024]{2,1,0:T(8,128)(2,1)} %copy-done.22, ...), custom_call_target="tpu_custom_call" | custom-call | flops 1024 | bytes 1024 | tf_op jit(solution)/shard_map/attention_forward/pallas_call | solution.py:165
  143.2 20.6 %all-to-all-done.1 = bf16[4,2,256,256]{3,2,1,0:T(8,128)(2,1)S(1)} async-done(((bf16[4,2,256,256]{3,2,1,0:T(8,128)(2,1)}), bf16[4,2,256,256]{3,2,1,0:T(8,128)(2,1)S(1)}, u32[]{:S(2)}, u32[]{:S(2)}) %all-to-all-start.1) | async-done | bytes 1048608 | tf_op jit(solution)/shard_map/all_to_all | solution.py:718
  169.4 20.6 %collective-permute-done.4.refs_2_ = bf16[512,1024]{1,0:T(8,128)(2,1)} collective-permute-done((bf16[512,1024]{1,0:T(8,128)(2,1)}, bf16[512,1024]{1,0:T(8,128)(2,1)}, u32[]{:S(2)}, u32[]{:S(2)}) %collective-permute-start.4) | collective-permute-done | bytes 1048608 | tf_op jit(solution)/shard_map/ppermute | solution.py:578
  198.4 16.9 %collective-permute-done.5.refs_2_ = bf16[512,1024]{1,0:T(8,128)(2,1)} collective-permute-done((bf16[512,1024]{1,0:T(8,128)(2,1)}, bf16[512,1024]{1,0:T(8,128)(2,1)}, u32[]{:S(2)}, u32[]{:S(2)}) %collective-permute-start.5) | collective-permute-done | bytes 1048608 | tf_op jit(solution)/shard_map/ppermute | solution.py:578
  215.3 27.2 %collective-permute-done.8.refs_0_ = bf16[512,1152]{1,0:T(8,128)(2,1)} collective-permute-done((bf16[512,1152]{1,0:T(8,128)(2,1)}, bf16[512,1152]{1,0:T(8,128)(2,1)}, u32[]{:S(2)}, u32[]{:S(2)}) %collective-permute-start.8) | collective-permute-done | bytes 1179680 | tf_op jit(solution)/shard_map/ppermute | solution.py:578
  247.2 23.5 %experts.4 = (bf16[4,4,320,1024]{3,2,1,0:T(8,128)(2,1)}, bf16[4,4,320,1024]{3,2,1,0:T(8,128)(2,1)}, bf16[4,4,320,512]{3,2,1,0:T(8,128)(2,1)}, bf16[4,4,320,1024]...) custom-call(s32[4]{0:T(128)} %multiply_add_fusion.1.ids_ref, ...), custom_call_target="tpu_custom_call" | custom-call | flops 8724152320 | bytes 20971520 | tf_op jit(solution)/shard_map/experts/pallas_call | solution.py:397
  280.3 23.4 %experts.5 = (bf16[4,4,320,1024]{3,2,1,0:T(8,128)(2,1)}, bf16[4,4,320,1024]{3,2,1,0:T(8,128)(2,1)}, bf16[4,4,320,512]{3,2,1,0:T(8,128)(2,1)}, bf16[4,4,320,1024]...) custom-call(s32[4]{0:T(128)} %multiply_add_fusion.1.ids_ref, ...), custom_call_target="tpu_custom_call", output_to_operand_aliasing={{0}: (7, {}), {1}: (8, {}), {2}: (9, {}), {3}: (10, {})} | custom-call | flops 8724152320 | bytes 20971520 | tf_op jit(solution)/shard_map/experts/pallas_call | solution.py:397
  307.6 23.4 %experts.6 = (bf16[4,4,320,1024]{3,2,1,0:T(8,128)(2,1)}, bf16[4,4,320,1024]{3,2,1,0:T(8,128)(2,1)}, bf16[4,4,320,512]{3,2,1,0:T(8,128)(2,1)}, bf16[4,4,320,1024]...) custom-call(s32[4]{0:T(128)} %multiply_add_fusion.1.ids_ref, ...), custom_call_target="tpu_custom_call", output_to_operand_aliasing={{0}: (7, {}), {1}: (8, {}), {2}: (9, {}), {3}: (10, {})} | custom-call | flops 8724152320 | bytes 20971520 | tf_op jit(solution)/shard_map/experts/pallas_call | solution.py:397
  334.7 23.2 %experts.7 = (bf16[4,4,320,1024]{3,2,1,0:T(8,128)(2,1)}, bf16[4,4,320,1024]{3,2,1,0:T(8,128)(2,1)}, bf16[4,4,320,512]{3,2,1,0:T(8,128)(2,1)}, bf16[4,4,320,1024]...) custom-call(s32[4]{0:T(128)} %multiply_add_fusion.1.ids_ref, ...), custom_call_target="tpu_custom_call", output_to_operand_aliasing={{0}: (7, {}), {1}: (8, {}), {2}: (9, {}), {3}: (10, {})} | custom-call | flops 8724152320 | bytes 20971520 | tf_op jit(solution)/shard_map/experts/pallas_call | solution.py:397
  358.5 5.2 collective-permute-done.25
  369.9 20.4 %expert_grads.2 = (f32[1024,1024]{1,0:T(8,128)}, bf16[2,512,1024]{2,1,0:T(8,128)(2,1)}, bf16[2,512,1024]{2,1,0:T(8,128)(2,1)}, f32[512,1024]{1,0:T(8,128)}, f32[512,1024]{1,0:T(8,128)}) custom-call(s32[4]{0:T(128)} %iota_xor_fusion.order_ref, bf16[4,1280,1024]{2,1,0:T(8,128)(2,1)} %bitcast.119, bf16[4,1280,1024]{2,1,0:T(8,128)(2,1)} %bitcast.121), custom_call_target="tpu_custom_call" | custom-call | flops 1024 | bytes 1024 | tf_op jit(solution)/shard_map/expert_grads/pallas_call | solution.py:513
  403.4 12.6 %expert_grads.3 = (f32[1024,512]{1,0:T(8,128)}, bf16[2,512,512]{2,1,0:T(8,128)(2,1)}, bf16[2,512,512]{2,1,0:T(8,128)(2,1)}, f32[512,512]{1,0:T(8,128)}, f32[512,512]{1,0:T(8,128)}) custom-call(s32[4]{0:T(128)} %iota_xor_fusion.order_ref, bf16[4,1280,1024]{2,1,0:T(8,128)(2,1)} %bitcast.120, bf16[4,1280,512]{2,1,0:T(8,128)(2,1)} %bitcast.122), custom_call_target="tpu_custom_call" | custom-call | flops 1024 | bytes 1024 | tf_op jit(solution)/shard_map/expert_grads/pallas_call | solution.py:513
  428.1 6.1 %cut_rows.1.filled_ref = bf16[8,4,32,1664]{3,2,1,0:T(8,128)(2,1)} custom-call(bf16[4,512,256]{2,1,0:T(8,128)(2,1)} %bitcast.136, bf16[512,1024]{1,0:T(8,128)(2,1)} %copy-done.30, bf16[512,1024]{1,0:T(8,128)(2,1)} %copy-done.1, f32[512,128]{1,0:T(8,128)} %concatenate.24.logits_ref, f32[1024,1]{1,0:T(8,128)} %copy.59.gain_ref), custom_call_target="tpu_custom_call" | custom-call | flops 3489660928 | bytes 8912896 | tf_op jit(solution)/shard_map/cut_rows/pallas_call | solution.py:454
  434.2 4.5 collective-permute-done.28
  444.9 5.3 all-to-all-done.2.grad_ref
  450.4 27.1 %attention_backward.1 = (bf16[4,2,256,512]{3,2,1,0:T(8,128)(2,1)}, bf16[8,4,32,1664]{3,2,1,0:T(8,128)(2,1)}) custom-call(bf16[2,1024,512]{2,1,0:T(8,128)(2,1)} %get-tuple-element.159.packed_ref, f32[2,2,8,1024]{3,2,1,0:T(8,128)} %get-tuple-element.160.lse_ref, bf16[4,2,256,256]{3,2,1,0:T(8,128)(2,1)} %all-to-all-done.2.grad_ref, ...), custom_call_target="tpu_custom_call", output_to_operand_aliasing={{1}: (6, {})} | custom-call | flops 1024 | bytes 1024 | tf_op jit(solution)/shard_map/attention_backward/pallas_call | solution.py:282
  477.5 5.0 all-to-all-start.3
  501.1 28.7 %all-to-all-done.3 = bf16[4,2,256,512]{3,2,1,0:T(8,128)(2,1)} async-done(((bf16[4,2,256,512]{3,2,1,0:T(8,128)(2,1)}), bf16[4,2,256,512]{3,2,1,0:T(8,128)(2,1)}, u32[]{:S(2)}, u32[]{:S(2)}) %all-to-all-start.3) | async-done | bytes 2097184 | tf_op jit(solution)/shard_map/all_to_all | solution.py:845
  543.6 5.4 fusion.3
  549.1 5.0 all-to-all-start.4
  559.5 9.1 %collective-permute-done.34 = bf16[512,1024]{1,0:T(8,128)(2,1)} collective-permute-done((bf16[512,1024]{1,0:T(8,128)(2,1)}, bf16[512,1024]{1,0:T(8,128)(2,1)}, u32[]{:S(2)}, u32[]{:S(2)}) %collective-permute-start.34) | collective-permute-done | bytes 1048608 | tf_op jit(solution)/shard_map/ppermute | solution.py:578
  (245 shorter events, 148.3 us)
Async XLA Ops:
  7.2 77.5 %all-gather.6.cloned.1.call-start = ((), (), s32[]{:S(2)}) async-start(), calls=%async_computation.6 | async-start | bytes 5242880 | tf_op jit(solution)/shard_map/all_gather | solution.py:665
  37.4 46.5 %all-to-all-start = ((bf16[4,32,3200]{2,1,0:T(8,128)(2,1)}), bf16[4,32,3200]{2,1,0:T(8,128)(2,1)S(1)}, u32[]{:S(2)}, u32[]{:S(2)}) async-start(bf16[4,32,3200]{2,1,0:T(8,128)(2,1)} %broadcast_in_dim.24), calls=%async_computation | async-start | bytes 1638400 | tf_op jit(solution)/shard_map/all_to_all | solution.py:657
  40.9 70.8 %all-gather.8.cloned.1.call-start = ((), (), s32[]{:S(2)}) async-start(), calls=%async_computation.7 | async-start | bytes 1474560 | tf_op jit(solution)/shard_map/all_gather | solution.py:668
  41.0 43.7 %collective-permute-start.1 = (bf16[2,256,1024]{2,1,0:T(8,128)(2,1)S(1)}, bf16[2,256,1024]{2,1,0:T(8,128)(2,1)}, u32[]{:S(2)}, u32[]{:S(2)}) collective-permute-start(bf16[2,256,1024]{2,1,0:T(8,128)(2,1)S(1)} %collective-permute-done.refs_1_), channel_id=1, source_target_pairs={{0,8},{8,16},{16,24},{24,0},{1,9},{9,17},{17,25},{25,1},{2,10},{10... | collective-permute-start | bytes 3145736 | tf_op jit(solution)/shard_map/ppermute | solution.py:578
  84.7 57.2 %all-gather.10.cloned.1.call-start = ((), (), s32[]{:S(2)}) async-start(), calls=%async_computation.8 | async-start | bytes 2654208 | tf_op jit(solution)/shard_map/all_gather | solution.py:668
  85.5 161.7 %all-gather.12.cloned.1.call-start = ((), (), s32[]{:S(2)}) async-start(), calls=%async_computation.9 | async-start | bytes 10485760 | tf_op jit(solution)/shard_map/all_gather | solution.py:691
  140.5 255.7 %all-gather.14.cloned.1.call-start = ((), (), s32[]{:S(2)}) async-start(), calls=%async_computation.10 | async-start | bytes 4718592 | tf_op jit(solution)/shard_map/all_gather | solution.py:668
  243.5 30.2 %collective-permute-start.9 = (bf16[512,1152]{1,0:T(8,128)(2,1)}, bf16[512,1152]{1,0:T(8,128)(2,1)}, u32[]{:S(2)}, u32[]{:S(2)}) collective-permute-start(bf16[512,1152]{1,0:T(8,128)(2,1)} %collective-permute-done.8.refs_0_), channel_id=1, source_target_pairs={{0,8},{8,16},{16,24},{24,0},{1,9},{9,17},{17,25},{25,1},{2,10},{10... | collective-permute-start | bytes 3538952 | tf_op jit(solution)/shard_map/ppermute | solution.py:578
  275.2 31.3 %collective-permute-start.6 = (bf16[512,1152]{1,0:T(8,128)(2,1)}, bf16[512,1152]{1,0:T(8,128)(2,1)S(1)}, u32[]{:S(2)}, u32[]{:S(2)}) collective-permute-start(bf16[512,1152]{1,0:T(8,128)(2,1)} %concatenate.23.refs_0_), channel_id=1, source_target_pairs={{0,1},{1,0},{2,3},{3,2},{4,5},{5,4},{6,7},{7,6},{8,9},{9,8},{10,11... | collective-permute-start | bytes 3538952 | tf_op jit(solution)/shard_map/ppermute | solution.py:581
  275.7 30.8 %collective-permute-start.16 = (bf16[512,1152]{1,0:T(8,128)(2,1)}, bf16[512,1152]{1,0:T(8,128)(2,1)S(1)}, u32[]{:S(2)}, u32[]{:S(2)}) collective-permute-start(bf16[512,1152]{1,0:T(8,128)(2,1)} %collective-permute-done.9.refs_0_), channel_id=1, source_target_pairs={{0,8},{8,16},{16,24},{24,0},{1,9},{9,17},{17,25},{25,1},{2,10},{10... | collective-permute-start | bytes 3538952 | tf_op jit(solution)/shard_map/ppermute | solution.py:578
  279.9 51.1 %collective-permute-start.18 = (bf16[512,1152]{1,0:T(8,128)(2,1)S(1)}, bf16[512,1152]{1,0:T(8,128)(2,1)}, u32[]{:S(2)}, u32[]{:S(2)}) collective-permute-start(bf16[512,1152]{1,0:T(8,128)(2,1)S(1)} %add_convert_fusion.2), channel_id=1, source_target_pairs={{0,8},{8,16},{16,24},{24,0},{1,9},{9,17},{17,25},{25,1},{2,10},{10... | collective-permute-start | bytes 3538952 | tf_op jit(solution)/shard_map/ppermute | solution.py:578
  333.4 30.3 %collective-permute-start.25 = (bf16[512,1152]{1,0:T(8,128)(2,1)S(1)}, bf16[512,1152]{1,0:T(8,128)(2,1)S(1)}, u32[]{:S(2)}, u32[]{:S(2)}) collective-permute-start(bf16[512,1152]{1,0:T(8,128)(2,1)S(1)} %add_convert_fusion.1), channel_id=1, source_target_pairs={{0,8},{8,16},{16,24},{24,0},{1,9},{9,17},{17,25},{25,1},{2,10},{10... | collective-permute-start | bytes 3538952 | tf_op jit(solution)/shard_map/ppermute | solution.py:578
  366.4 29.8 %collective-permute-start.30 = (bf16[512,1152]{1,0:T(8,128)(2,1)}, bf16[512,1152]{1,0:T(8,128)(2,1)}, u32[]{:S(2)}, u32[]{:S(2)}) collective-permute-start(bf16[512,1152]{1,0:T(8,128)(2,1)} %get-tuple-element.141), channel_id=1, source_target_pairs={{0,1},{1,0},{2,3},{3,2},{4,5},{5,4},{6,7},{7,6},{8,9},{9,8},{10,11... | collective-permute-start | bytes 3538952 | tf_op jit(solution)/shard_map/ppermute | solution.py:581
  390.3 48.3 %collective-permute-start.28 = (bf16[2,512,1024]{2,1,0:T(8,128)(2,1)}, bf16[2,512,1024]{2,1,0:T(8,128)(2,1)}, u32[]{:S(2)}, u32[]{:S(2)}) collective-permute-start(bf16[2,512,1024]{2,1,0:T(8,128)(2,1)} %get-tuple-element.138), channel_id=1, source_target_pairs={{0,2},{2,0},{4,6},{6,4},{1,3},{3,1},{5,7},{7,5},{8,10},{10,8},{12,... | collective-permute-start | bytes 6291464 | tf_op jit(solution)/shard_map/ppermute | solution.py:618
  391.6 48.1 %collective-permute-start.29 = (bf16[2,512,1024]{2,1,0:T(8,128)(2,1)}, bf16[2,512,1024]{2,1,0:T(8,128)(2,1)}, u32[]{:S(2)}, u32[]{:S(2)}) collective-permute-start(bf16[2,512,1024]{2,1,0:T(8,128)(2,1)} %get-tuple-element.139), channel_id=1, source_target_pairs={{0,4},{2,6},{4,0},{6,2},{1,5},{3,7},{5,1},{7,3},{8,12},{10,14},{12... | collective-permute-start | bytes 6291464 | tf_op jit(solution)/shard_map/ppermute | solution.py:618
  439.7 37.8 %collective-permute-start.32 = (bf16[2,512,512]{2,1,0:T(8,128)(2,1)}, bf16[2,512,512]{2,1,0:T(8,128)(2,1)}, u32[]{:S(2)}, u32[]{:S(2)}) collective-permute-start(bf16[2,512,512]{2,1,0:T(8,128)(2,1)} %get-tuple-element.165), channel_id=1, source_target_pairs={{0,2},{2,0},{4,6},{6,4},{1,3},{3,1},{5,7},{7,5},{8,10},{10,8},{12,... | collective-permute-start | bytes 3145736 | tf_op jit(solution)/shard_map/ppermute | solution.py:618
  440.4 37.1 %collective-permute-start.33 = (bf16[2,512,512]{2,1,0:T(8,128)(2,1)}, bf16[2,512,512]{2,1,0:T(8,128)(2,1)}, u32[]{:S(2)}, u32[]{:S(2)}) collective-permute-start(bf16[2,512,512]{2,1,0:T(8,128)(2,1)} %get-tuple-element.166), channel_id=1, source_target_pairs={{0,4},{2,6},{4,0},{6,2},{1,5},{3,7},{5,1},{7,3},{8,12},{10,14},{12... | collective-permute-start | bytes 3145736 | tf_op jit(solution)/shard_map/ppermute | solution.py:618
  477.5 52.3 %all-to-all-start.3 = ((bf16[4,2,256,512]{3,2,1,0:T(8,128)(2,1)}), bf16[4,2,256,512]{3,2,1,0:T(8,128)(2,1)}, u32[]{:S(2)}, u32[]{:S(2)}) async-start(bf16[4,2,256,512]{3,2,1,0:T(8,128)(2,1)} %get-tuple-element.168), calls=%async_computation.3 | async-start | bytes 4194304 | tf_op jit(solution)/shard_map/all_to_all | solution.py:845
  482.6 66.5 %reduce-scatter.2.cloned.1.call-start = ((), (), s32[]{:S(2)}) async-start(), calls=%async_computation.11 | async-start | bytes 3833856 | tf_op jit(solution)/shard_map/reduce_scatter | solution.py:621
  483.4 76.0 %collective-permute-start.15 = (bf16[512,1024]{1,0:T(8,128)(2,1)}, bf16[512,1024]{1,0:T(8,128)(2,1)}, u32[]{:S(2)}, u32[]{:S(2)}) collective-permute-start(bf16[512,1024]{1,0:T(8,128)(2,1)} %get-tuple-element.116), channel_id=1, source_target_pairs={{0,1},{1,0},{2,3},{3,2},{4,5},{5,4},{6,7},{7,6},{8,9},{9,8},{10,11... | collective-permute-start | bytes 3145736 | tf_op jit(solution)/shard_map/ppermute | solution.py:581
  487.3 56.3 %collective-permute-start.35 = (bf16[512,1024]{1,0:T(8,128)(2,1)}, bf16[512,1024]{1,0:T(8,128)(2,1)}, u32[]{:S(2)}, u32[]{:S(2)}) collective-permute-start(bf16[512,1024]{1,0:T(8,128)(2,1)} %fusion.2), channel_id=1, source_target_pairs={{0,4},{2,6},{4,0},{6,2},{1,5},{3,7},{5,1},{7,3},{8,12},{10,14},{12... | collective-permute-start | bytes 3145736 | tf_op jit(solution)/shard_map/ppermute | solution.py:618
  491.5 52.1 %collective-permute-start.36 = (bf16[512,1024]{1,0:T(8,128)(2,1)}, bf16[512,1024]{1,0:T(8,128)(2,1)}, u32[]{:S(2)}, u32[]{:S(2)}) collective-permute-start(bf16[512,1024]{1,0:T(8,128)(2,1)} %fusion.1), channel_id=1, source_target_pairs={{0,2},{2,0},{4,6},{6,4},{1,3},{3,1},{5,7},{7,5},{8,10},{10,8},{12,... | collective-permute-start | bytes 3145736 | tf_op jit(solution)/shard_map/ppermute | solution.py:618
  494.7 45.3 %collective-permute-start.37 = (bf16[512,512]{1,0:T(8,128)(2,1)}, bf16[512,512]{1,0:T(8,128)(2,1)}, u32[]{:S(2)}, u32[]{:S(2)}) collective-permute-start(bf16[512,512]{1,0:T(8,128)(2,1)} %fusion.28), channel_id=1, source_target_pairs={{0,4},{2,6},{4,0},{6,2},{1,5},{3,7},{5,1},{7,3},{8,12},{10,14},{12... | collective-permute-start | bytes 1572872 | tf_op jit(solution)/shard_map/ppermute | solution.py:618
  497.6 42.8 %collective-permute-start.38 = (bf16[512,512]{1,0:T(8,128)(2,1)}, bf16[512,512]{1,0:T(8,128)(2,1)}, u32[]{:S(2)}, u32[]{:S(2)}) collective-permute-start(bf16[512,512]{1,0:T(8,128)(2,1)} %fusion.27), channel_id=1, source_target_pairs={{0,2},{2,0},{4,6},{6,4},{1,3},{3,1},{5,7},{7,5},{8,10},{10,8},{12,... | collective-permute-start | bytes 1572872 | tf_op jit(solution)/shard_map/ppermute | solution.py:618
  (62 other events, 892.4 us)
Sparse Core Ops, SparseCore 0:
  9.9 55.3 all-gather.5
  84.8 22.5 all-gather.7
  109.3 29.0 all-gather.9
  140.1 87.6 all-gather.11
  275.2 35.4 all-gather.13
  486.5 57.9 reduce-scatter.1
